TPU v7x, 32 devices: a whole 2x2x4 slice. The times are simulated.
32 devices in a mesh: ka: 16 (over z, y, x), ga: 2 (over core).
Axes of the slice: x: 2, y: 2, z: 4, core: 2. Of those that a mesh axis runs over, the one named last changes fastest.
Arguments:
- densities: bfloat16 [64, 6144, 128], P('ka'), may hold values from -0.67578125 to 0.67578125
- screened: bfloat16 [2, 6144, 6144], P(None, 'ka', 'ga'), may hold values from -0.0546875 to 0.0546875
- partner: int32 [64], replicated, may hold values from 0 to 63, as said below
- pair_order: int32 [64], replicated, may hold values from 0 to 63, each once
Outputs:
- direct: float32 [64, 64, 128], P('ka')
- mirror: float32 [64, 64, 128], P('ka')
Inputs may be any that keep to these rules, and one draw needn't show every extreme that they name: Number the k-points of a 4 x 4 x 4 grid as k = (a * 4 + b) * 4 + c. partner[k] is the k-point (a + 1, b, c + s) with wrap-around in each direction, for one s from 0 to 3 drawn with the seed.
All inputs are finite; a program needn't handle non-finite values.
Results may differ from a plain program's by a relative error of at most 0.0003.
Values may be sent and summed in bfloat16 or wider, within the bound.
No kernel may reach another device: no remote copies, remote signals or barrier semaphores. Data moves between devices by JAX's collectives and lax.ppermute only.
A program may use at most 192 MiB of HBM per device.

v0:
```python
import jax
import jax.numpy as jnp
from jax import lax
from jax.sharding import PartitionSpec as P


def passed_along(value, axis, steps):
    count = lax.axis_size(axis)
    pairs = [(source, (source + steps) % count) for source in range(count)]
    return lax.ppermute(value, axis, pairs)


def conjugate_side(blocks, pair_count):
    real_half = jnp.swapaxes(blocks[:, :, :pair_count], 1, 2)
    imag_half = jnp.swapaxes(blocks[:, :, pair_count:], 1, 2)
    return jnp.concatenate([real_half, -imag_half], axis=2)


def combine_terms(partial_value, order_table, pair_count):
    block_re = partial_value[:, 0, :, :pair_count] - partial_value[:, 1, :, pair_count:]
    block_im = partial_value[:, 0, :, pair_count:] + partial_value[:, 1, :, :pair_count]
    block_re = jnp.einsum("kpq,qj->kpj", block_re, order_table, precision=lax.Precision.HIGHEST)
    block_im = jnp.einsum("kpq,qj->kpj", block_im, order_table, precision=lax.Precision.HIGHEST)
    return jnp.concatenate([block_re, block_im], axis=2)


def finish_terms(left_sums, matched, pair_count):
    left_re = left_sums[:, 0, :pair_count] + left_sums[:, 1, pair_count:]
    left_im = left_sums[:, 1, :pair_count] - left_sums[:, 0, pair_count:]
    left_factor = jnp.stack([left_re, left_im], axis=1)
    return jnp.einsum(
        "kwpc,kcq->kwpq", left_factor, matched.astype(jnp.float32), precision=lax.Precision.HIGHEST
    )


def body(densities, screened, partner, pair_order):
    k_count = densities.shape[0]
    pair_count = densities.shape[2] // 2
    panel_width = screened.shape[2]
    k_owner = lax.axis_index("ka")
    column = lax.axis_index("ga")
    own_columns = lax.dynamic_slice_in_dim(densities, column * panel_width, panel_width, 1)
    arrived = passed_along(own_columns, "ka", -4)
    own_partner = lax.dynamic_slice_in_dim(partner, k_owner * k_count, k_count, 0)
    slot_index = own_partner % k_count
    offset = slot_index[0]
    matched = jnp.take(arrived, slot_index, axis=0)
    left_sums = jnp.einsum(
        "kgp,wgc->kwpc",
        densities,
        lax.all_gather(screened, "ka", axis=1, tiled=True),
        preferred_element_type=jnp.float32,
    )
    partial_value = finish_terms(left_sums, matched, pair_count)
    order_table = (jnp.arange(pair_count)[:, None] == pair_order[None, :]).astype(jnp.float32)
    sources = (jnp.arange(k_count) - offset) % k_count
    summed = lax.psum(partial_value, "ga")
    direct = combine_terms(summed, order_table, pair_count)
    received = passed_along(direct, "ka", 4)
    mirror = conjugate_side(jnp.take(received, sources, axis=0), pair_count)
    return (direct, mirror)


def solution(mesh):
    in_specs = (P("ka", None, None), P(None, "ka", "ga"), P(), P())
    out_specs = (P("ka", None, None), P("ka", None, None))
    return jax.shard_map(body, mesh=mesh, in_specs=in_specs, out_specs=out_specs, check_vma=False)
```

profile of v0, /device:TPU:0, one launch (start us, length us, event | category | flops | bytes accessed | tf_op | source)
XLA Modules:
  0.0 907.9 jit_solution(4272330263730085626)
XLA Ops:
  7.2 0.0 all-gather.2.cloned.1.call-start
  7.2 0.7 all-gather.2.cloned.1.call-update
  7.9 0.0 all-reduce.2.cloned.1.call-start
  8.0 0.0 copy-start.2
  8.0 2.1 constant_dynamic-slice_fusion
  10.1 5.1 collective-permute-start
  15.2 0.0 copy-done.2
  15.2 0.1 compare_and_fusion.1
  15.3 165.4 %collective-permute-done = bf16[4,3072,128]{2,1,0:T(8,128)(2,1)} collective-permute-done((bf16[4,3072,128]{2,1,0:T(8,128)(2,1)S(1)}, bf16[4,3072,128]{2,1,0:T(8,128)(2,1)}, u32[]{:S(2)}, u32[]{:S(2)}) %collective-permute-start) | collective-permute-done | bytes 3145760 | tf_op jit(solution)/shard_map/ppermute | solution.py:10
  180.7 3.0 gather_fusion
  183.7 631.0 %all-gather.2.cloned.1.call-done = bf16[2,6144,3072]{2,1,0:T(8,128)(2,1)} async-done(((bf16[2,384,3072]{2,1,0:T(8,128)(2,1)}), bf16[2,6144,3072]{2,1,0:T(8,128)(2,1)}) %all-gather.2.cloned.1.call-update) | async-done | bytes 75497488 | tf_op jit(solution)/shard_map/all_gather | solution.py:51
  814.8 48.0 %fusion.2 = f32[4,2,128,3072]{3,2,0,1:T(8,128)} fusion(bf16[2,6144,3072]{2,1,0:T(8,128)(2,1)} %all-gather.2.cloned.1.call-done, bf16[4,6144,128]{2,1,0:T(8,128)(2,1)} %param.4), kind=kOutput, calls=%fused_computation.4 | convolution fusion | flops 38654705664 | bytes 94371840 | tf_op jit(solution)/shard_map/kgp,wgc->kwpc/dot_general | solution.py:48
  862.7 5.8 slice_add_fusion
  868.5 0.0 copy-start.1
  868.5 4.1 fusion.6
  872.7 0.0 all-reduce.2.cloned.1.call-update
  872.7 16.6 %all-reduce.2.cloned.1.call-done = f32[4,2,64,128]{3,2,1,0:T(8,128)} async-done(((f32[4,2,64,128]{3,2,1,0:T(8,128)}), f32[4,2,64,128]{3,2,1,0:T(8,128)}) %all-reduce.2.cloned.1.call-update) | async-done | bytes 262160 | tf_op jit(solution)/shard_map/psum | solution.py:57
  889.3 0.0 copy-done.1
  889.3 1.2 fusion.18
  890.5 1.2 fusion.14
  891.8 0.1 pad_maximum_fusion.2
  891.9 0.0 copy-start
  891.9 1.8 collective-permute-start.1
  893.8 5.7 collective-permute-done.1
  899.5 0.6 gather_fusion.1
  900.1 0.1 broadcast_select_fusion
  900.1 0.1 slice_bitcast_fusion
  900.3 0.8 copy.8
  901.0 0.0 copy-done
  (6 shorter events, 0.1 us)
Async XLA Ops:
  7.2 807.6 %all-gather.2.cloned.1.call-start = ((), (), s32[]{:S(2)}) async-start(), calls=%async_computation | async-start | bytes 80216064 | tf_op jit(solution)/shard_map/all_gather | solution.py:51
  7.9 881.4 %all-reduce.2.cloned.1.call-start = ((), (), s32[]{:S(2)}) async-start(), calls=%async_computation.1 | async-start | bytes 524288 | tf_op jit(solution)/shard_map/psum | solution.py:57
  8.0 7.3 copy-start.2
  10.1 170.6 %collective-permute-start = (bf16[4,3072,128]{2,1,0:T(8,128)(2,1)S(1)}, bf16[4,3072,128]{2,1,0:T(8,128)(2,1)}, u32[]{:S(2)}, u32[]{:S(2)}) collective-permute-start(bf16[4,3072,128]{2,1,0:T(8,128)(2,1)S(1)} %constant_dynamic-slice_fusion), channel_id=1, source_target_pairs={{0,24},{2,26},{4,28},{6,30},{8,0},{10,2},{12,4},{14,6},{16,8},{18,... | collective-permute-start | bytes 9437192 | tf_op jit(solution)/shard_map/ppermute | solution.py:10
  868.5 20.8 %copy-start.1 = (s32[64]{0:T(128)S(1)}, s32[64]{0:T(128)}, u32[]{:S(2)}) copy-start(s32[64]{0:T(128)} %param.7) | copy-start | bytes 772
  891.9 9.2 %copy-start = (f32[4,64,128]{2,1,0:T(8,128)}, f32[4,64,128]{2,1,0:T(8,128)S(1)}, u32[]{:S(2)}) copy-start(f32[4,64,128]{2,1,0:T(8,128)S(1)} %pad_maximum_fusion.2) | copy-start | bytes 393220
  891.9 7.6 collective-permute-start.1
Sparse Core Ops, SparseCore 0:
  10.7 803.9 all-gather.1
  872.8 16.4 all-reduce.1
where the time goes:
time: 908 us
  waiting for transfers between devices  819 us (90%)
  matrix products  54.6 us (6%)
  between operations  14.2 us (2%)
    all_gather x1, waiting for transfers between devices, body(): lax.all_gather(screened, 'ka', axis=1, tiled=True)  631 us
    ppermute x2, waiting for transfers between devices, passed_along(): return lax.ppermute(value, axis, pairs)  171 us
    dot_general x1, matrix products, body(): jnp.einsum('kgp,wgc->kwpc', densities, lax.all_gather(screened, 'ka', axi...  48 us
  transfers between devices with their start and end apart: 4, of which 4 were waited for; matrix products, arithmetic and copies ran while one was open for 1% of the time, Pallas kernels for 0%

commit v1 on v0

--- a/solution.py
+++ b/solution.py
@@ -1,6 +1,10 @@
+import functools
+
 import jax
 import jax.numpy as jnp
 from jax import lax
+from jax.experimental import pallas as pl
+from jax.experimental.pallas import tpu as pltpu
 from jax.sharding import PartitionSpec as P
 
 
@@ -19,6 +23,10 @@
 def combine_terms(partial_value, order_table, pair_count):
     block_re = partial_value[:, 0, :, :pair_count] - partial_value[:, 1, :, pair_count:]
     block_im = partial_value[:, 0, :, pair_count:] + partial_value[:, 1, :, :pair_count]
+    return reorder(block_re, block_im, order_table)
+
+
+def reorder(block_re, block_im, order_table):
     block_re = jnp.einsum("kpq,qj->kpj", block_re, order_table, precision=lax.Precision.HIGHEST)
     block_im = jnp.einsum("kpq,qj->kpj", block_im, order_table, precision=lax.Precision.HIGHEST)
     return jnp.concatenate([block_re, block_im], axis=2)
@@ -33,7 +41,7 @@
     )
 
 
-def body(densities, screened, partner, pair_order):
+def general_body(densities, screened, partner, pair_order):
     k_count = densities.shape[0]
     pair_count = densities.shape[2] // 2
     panel_width = screened.shape[2]
@@ -61,7 +69,248 @@
     return (direct, mirror)
 
 
+AXES = ("ka", "ga")
+CHUNKS = 3
+
+
+def device(z, b, c):
+    return (z * 4 + b) * 2 + c
+
+
+def moved(value, rule):
+    pairs = []
+    for z in range(4):
+        for b in range(4):
+            for c in range(2):
+                target = rule(z, b, c)
+                if target is not None:
+                    pairs.append((device(z, b, c), device(*target)))
+    return lax.ppermute(value, AXES, pairs)
+
+
+def along_x(value):
+    return moved(value, lambda z, b, c: (z, b ^ 1, c))
+
+
+def along_y(value):
+    return moved(value, lambda z, b, c: (z, b ^ 2, c))
+
+
+def other_core(value):
+    return moved(value, lambda z, b, c: (z, b, 1 - c))
+
+
+def end_with_mid(value):
+    return moved(value, lambda z, b, c: (z ^ 1, b, c))
+
+
+def mid_to_end(value):
+    return moved(value, lambda z, b, c: (z ^ 1, b, c) if z in (1, 2) else None)
+
+
+def mid_with_mid(value):
+    return moved(value, lambda z, b, c: (3 - z, b, c) if z in (1, 2) else None)
+
+
+def in_plane(chunk):
+    x_side = along_x(chunk)
+    y_side = along_y(chunk)
+    diagonal_re = along_y(x_side[0])
+    diagonal_im = along_x(y_side[1])
+    return (chunk, x_side, y_side, diagonal_re, diagonal_im)
+
+
+def terms_kernel(flags, *refs, n_chunks, slots, near):
+    n_slots = len(slots)
+    w_refs = [refs[5 * i : 5 * i + 5] for i in range(n_chunks)]
+    rest = refs[5 * n_chunks :]
+    carried, swapped = rest[:n_slots], rest[n_slots : 2 * n_slots]
+    up_refs, down_refs = rest[2 * n_slots : 3 * n_slots], rest[3 * n_slots : 4 * n_slots]
+    rest = rest[4 * n_slots :]
+    acc_in, acc, w_buf, m_buf, c_buf, w_sems, m_sems, c_sems = rest
+    own_b, own_near, half, shift = flags[0], flags[1], flags[2], flags[3]
+    rows = w_refs[0][0].shape[1]
+    width = w_refs[0][0].shape[2]
+    depth = 4 * rows
+    copies = []
+    for i in range(n_chunks):
+        own, x_side, y_side, d_re, d_im = w_refs[i]
+        here = []
+        for turn, source in ((0, own), (1, x_side), (2, y_side)):
+            start = pl.multiple_of((own_b ^ turn) * rows, rows)
+            here.append(pltpu.make_async_copy(source, w_buf.at[i, :, pl.ds(start, rows), :], w_sems.at[i, turn]))
+        start = pl.multiple_of((own_b ^ 3) * rows, rows)
+        for part, source in ((0, d_re), (1, d_im)):
+            here.append(pltpu.make_async_copy(source, w_buf.at[i, part, pl.ds(start, rows), :], w_sems.at[i, 3 + part]))
+        copies.append(here)
+    chosen = own_near == (1 if near else 0)
+    for copy in copies[0]:
+        copy.start()
+    m_waits, c_waits = [], []
+    for s in range(n_slots):
+        first = pltpu.make_async_copy(carried[s], m_buf.at[s], m_sems.at[s])
+        second = pltpu.make_async_copy(swapped[s], m_buf.at[s], m_sems.at[s])
+        pl.when(chosen)(first.start)
+        pl.when(jnp.logical_not(chosen))(second.start)
+        m_waits.append(first)
+        first = pltpu.make_async_copy(up_refs[s], c_buf.at[s], c_sems.at[s])
+        second = pltpu.make_async_copy(down_refs[s], c_buf.at[s], c_sems.at[s])
+        pl.when(half == 0)(first.start)
+        pl.when(half != 0)(second.start)
+        c_waits.append(first)
+    for here in copies[1:]:
+        for copy in here:
+            copy.start()
+    acc[...] = acc_in[...]
+    for i in range(n_chunks):
+        for copy in copies[i]:
+            copy.wait()
+        for s in range(n_slots):
+            if i == 0:
+                m_waits[s].wait()
+            lhs = m_buf[s].reshape(-1, depth)
+            re_side = jnp.dot(lhs, w_buf[i, 0], preferred_element_type=jnp.float32)
+            im_side = jnp.dot(lhs, w_buf[i, 1], preferred_element_type=jnp.float32)
+            if i == 0:
+                c_waits[s].wait()
+            k_count, both = m_buf.shape[1], m_buf.shape[2]
+            half_count = both // 2
+            for k in range(k_count):
+                top = slice(k * both, k * both + half_count)
+                low = slice(k * both + half_count, (k + 1) * both)
+                left = jnp.concatenate([re_side[top] + im_side[low], im_side[top] - re_side[low]], axis=0)
+                high_part = left.astype(jnp.bfloat16)
+                low_part = (left - high_part.astype(jnp.float32)).astype(jnp.bfloat16)
+                matched = c_buf[s, (k + shift) % k_count, :, i * width : (i + 1) * width]
+                dims = (((1,), (1,)), ((), ()))
+                added = lax.dot_general(high_part, matched, dims, preferred_element_type=jnp.float32)
+                added += lax.dot_general(low_part, matched, dims, preferred_element_type=jnp.float32)
+                acc[slots[s], k] = acc[slots[s], k] + added
+
+
+def add_terms(acc, flags, w_chunks, first_chunk, slots, carried, swapped, matched, near):
+    n_chunks, n_slots = len(w_chunks), len(slots)
+    _, rows, width = w_chunks[0][0].shape
+    k_count, both, depth = carried[0].shape
+    span = n_chunks * width
+    if n_chunks == CHUNKS:
+        pieces = matched
+    else:
+        pieces = [m[:, :, first_chunk * width : first_chunk * width + span] for m in matched]
+    operands = [ref for blocks in w_chunks for ref in blocks]
+    operands += [carried[s] for s in slots] + [swapped[s] for s in slots]
+    operands += [pieces[(s + 1) % 4] for s in slots] + [pieces[(s - 1) % 4] for s in slots]
+    flops = n_chunks * n_slots * (2 * 2 * k_count * both * depth * width + 4 * k_count * both * both * width)
+    moved_bytes = n_chunks * 4 * depth * width + n_slots * 2 * k_count * both * (depth + span) + 2 * acc.size * 4
+    whole = pl.BlockSpec(memory_space=pltpu.VMEM)
+    return pl.pallas_call(
+        functools.partial(terms_kernel, n_chunks=n_chunks, slots=tuple(slots), near=near),
+        out_shape=jax.ShapeDtypeStruct(acc.shape, acc.dtype),
+        in_specs=[pl.BlockSpec(memory_space=pltpu.SMEM)] + [pl.BlockSpec(memory_space=pl.ANY)] * len(operands) + [whole],
+        out_specs=whole,
+        scratch_shapes=[
+            pltpu.VMEM((n_chunks, 2, depth, width), jnp.bfloat16),
+            pltpu.VMEM((n_slots, k_count, both, depth), jnp.bfloat16),
+            pltpu.VMEM((n_slots, k_count, both, span), jnp.bfloat16),
+            pltpu.SemaphoreType.DMA((n_chunks, 5)),
+            pltpu.SemaphoreType.DMA((n_slots,)),
+            pltpu.SemaphoreType.DMA((n_slots,)),
+        ],
+        compiler_params=pltpu.CompilerParams(vmem_limit_bytes=56 * 1024 * 1024),
+        cost_estimate=pl.CostEstimate(flops=flops, bytes_accessed=moved_bytes, transcendentals=0),
+        name="terms",
+    )(flags, *operands, acc)
+
+
+def body(densities, screened, partner, pair_order):
+    k_count, n_rows, both = densities.shape
+    pair_count = both // 2
+    quarter = n_rows // 4
+    width = quarter // CHUNKS
+    k_owner = lax.axis_index("ka")
+    c = lax.axis_index("ga")
+    z, b = k_owner // 4, k_owner % 4
+    half, odd = z // 2, z % 2
+    at_end = (z == 0) | (z == 3)
+    own_near = c == odd
+    offset = partner[0] % k_count
+    flags = jnp.stack([b, own_near.astype(jnp.int32), half, offset]).astype(jnp.int32)
+
+    kept_half = lax.dynamic_slice_in_dim(screened, c * quarter, quarter, 2)
+    given_half = lax.dynamic_slice_in_dim(screened, (1 - c) * quarter, quarter, 2)
+
+    def cut(value, n):
+        return value[:, :, n * width : (n + 1) * width]
+
+    near_chunks, far_chunks = [], []
+    for n in range(CHUNKS):
+        kept, given = cut(kept_half, n), cut(given_half, n)
+        near_chunks.append(in_plane(jnp.where(own_near, kept, other_core(given))))
+    for n in range(CHUNKS):
+        kept, given = cut(kept_half, n), cut(given_half, n)
+        straight = moved(kept, lambda z, b, c: (z ^ 1, b, c) if c != z % 2 else None)
+        crossed = moved(given, lambda z, b, c: (z ^ 1, b, 1 - c) if c != z % 2 else None)
+        far_chunks.append(in_plane(jnp.where(own_near, straight, crossed)))
+
+    def own_part(number):
+        part = lax.dynamic_slice_in_dim(densities, number * quarter, quarter, 1)
+        return jnp.swapaxes(part, 1, 2)
+
+    own_first = own_part(2 * (1 - odd) + c)
+    own_second = own_part(2 * odd + c)
+    pair_a = end_with_mid(own_first)
+    mid_a = mid_with_mid(own_second)
+    pair_b = end_with_mid(jnp.where(at_end, own_second, mid_a))
+    mid_b = mid_with_mid(pair_a)
+    mid_c = mid_with_mid(pair_b)
+    pair_c = mid_to_end(mid_b)
+    mid_d = mid_with_mid(own_first)
+    carried = [
+        jnp.where(at_end, own_second, own_first),
+        jnp.where(at_end, pair_a, mid_a),
+        jnp.where(at_end, pair_b, mid_b),
+        jnp.where(at_end, pair_c, pair_b),
+    ]
+    matched = [
+        own_second,
+        jnp.where(at_end, pair_a, mid_d),
+        jnp.where(at_end, pair_b, mid_c),
+        jnp.where(at_end, pair_c, pair_a),
+    ]
+    swapped = [other_core(part) for part in carried]
+
+    acc = jnp.zeros((4, k_count, both, both), jnp.float32)
+
+    def add(acc, chunks, first, count, slots, near):
+        return add_terms(acc, flags, chunks[first : first + count], first, slots, carried, swapped, matched, near)
+
+    for n in range(CHUNKS):
+        acc = add(acc, near_chunks, n, 1, (0, 1), True)
+    acc = add(acc, near_chunks, 0, CHUNKS, (2,), True)
+    for n in range(CHUNKS):
+        acc = add(acc, far_chunks, n, 1, (0, 1, 2), False)
+    acc = add(acc, near_chunks, 0, CHUNKS, (3,), True)
+    acc = add(acc, far_chunks, 0, CHUNKS, (3,), False)
+
+    block_re = acc[:, :, :pair_count, :pair_count] - acc[:, :, pair_count:, pair_count:]
+    block_im = acc[:, :, :pair_count, pair_count:] + acc[:, :, pair_count:, :pair_count]
+    blocks = jnp.concatenate([block_re, block_im], axis=3)
+    blocks = blocks + other_core(blocks)
+    total = blocks[0]
+    for shift in (1, 2, 3):
+        sent = jnp.where(half == 0, blocks[shift], blocks[4 - shift])
+        total = total + moved(sent, lambda z, b, c: ((z + shift) % 4, b, c))
+    order_table = (jnp.arange(pair_count)[:, None] == pair_order[None, :]).astype(jnp.float32)
+    direct = reorder(total[:, :, :pair_count], total[:, :, pair_count:], order_table)
+    received = moved(direct, lambda z, b, c: ((z + 1) % 4, b, c))
+    sources = (jnp.arange(k_count) - offset) % k_count
+    mirror = conjugate_side(jnp.take(received, sources, axis=0), pair_count)
+    return (direct, mirror)
+
+
 def solution(mesh):
     in_specs = (P("ka", None, None), P(None, "ka", "ga"), P(), P())
     out_specs = (P("ka", None, None), P("ka", None, None))
-    return jax.shard_map(body, mesh=mesh, in_specs=in_specs, out_specs=out_specs, check_vma=False)
+    planes = mesh.shape["ka"] == 16 and mesh.shape["ga"] == 2
+    chosen = body if planes else general_body
+    return jax.shard_map(chosen, mesh=mesh, in_specs=in_specs, out_specs=out_specs, check_vma=False)

time: 908 us -> 429 us (0.47)
  waiting for transfers between devices: 819 us -> 175 us
  Pallas kernels: 0 us -> 106 us
  starting transfers between devices: 6.97 us -> 98.9 us
  matrix products: 54.6 us -> 0.46 us
  local copies, waits for them, and re-layouts: 6.52 us -> 26.5 us
  between operations: 14.2 us -> 2.13 us
    all_gather x1 -> x0, waiting for transfers between devices: 631 us -> none  [body(): lax.all_gather(screened, 'ka', axis=1, tiled=True)]
    pallas_call x0 -> x9, Pallas kernels: none -> 106 us  [add_terms(): pl.pallas_call(functools.partial(terms_kernel, n_chunks=n_chunks, slots=t...]
    ppermute x2 -> x49, starting transfers between devices: 6.9 us -> 98.9 us  [moved(): return lax.ppermute(value, AXES, pairs)]
    dot_general x4 -> x2, matrix products: 54.6 us -> 0.46 us  [the longest x1 0.26 us: reorder(): jnp.einsum('kpq,qj->kpj', block_im, order_table, precision=lax.Precision....]
    psum x1 -> x0, waiting for transfers between devices: 16.6 us -> none  [body(): summed = lax.psum(partial_value, 'ga')]
    select_n x1 -> x8, other arithmetic: 0.01 us -> 11.4 us  [the longest x2 5.53 us: body(): near_chunks.append(in_plane(jnp.where(own_near, kept, other_core(given))))]
    ppermute x2 -> x49, waiting for transfers between devices: 171 us -> 175 us  [moved(): return lax.ppermute(value, AXES, pairs)]
  transfers between devices with their start and end apart: 4 -> 49, of which waited for: 4 -> 17; matrix products, arithmetic and copies ran while one was open for 1% -> 7% of each run, Pallas kernels for 0% -> 19%
where the time goes in v1:
time: 429 us; the launch traced here: 424 us
  waiting for transfers between devices  175 us (41%)
  Pallas kernels  106 us (25%)
  starting transfers between devices  98.9 us (23%)
  local copies, waits for them, and re-layouts  26.5 us (6%)
  other arithmetic  14.7 us (3%)
    ppermute x49, waiting for transfers between devices, moved(): return lax.ppermute(value, AXES, pairs)  175 us
    pallas_call x9, Pallas kernels, add_terms(): pl.pallas_call(functools.partial(terms_kernel, n_chunks=n_chunks, slots=t...  106 us
    ppermute x49, starting transfers between devices, moved(): return lax.ppermute(value, AXES, pairs)  98.9 us
    unnamed x95, local copies, waits for them, and re-layouts  8.59 us
  transfers between devices with their start and end apart: 49, of which 17 were waited for; matrix products, arithmetic and copies ran while one was open for 7% of the time, Pallas kernels for 19%

profile of v1, /device:TPU:0, one launch (start us, length us, event | category | flops | bytes accessed | tf_op | source)
XLA Modules:
  0.0 424.2 jit_solution(4546137407427669468)
XLA Ops:
  0.7 3.4 constant_dynamic-slice_fusion.4
  4.8 3.1 collective-permute-start.18
  7.8 34.5 %collective-permute-done.18 = bf16[4,128,1536]{2,1,0:T(8,128)(2,1)} collective-permute-done((bf16[4,128,1536]{2,1,0:T(8,128)(2,1)S(1)}, bf16[4,128,1536]{2,1,0:T(8,128)(2,1)}, u32[]{:S(2)}, u32[]{:S(2)}) %collective-permute-start.18) | collective-permute-done | bytes 1572896 | tf_op jit(solution)/shard_map/ppermute | solution.py:88
  44.1 2.1 constant_dynamic-slice_fusion.6
  48.7 3.5 broadcast_select_fusion.8
  52.3 3.0 collective-permute-start.25
  63.2 2.3 collective-permute-start.30
  65.5 4.8 %collective-permute-done.12 = bf16[2,384,512]{2,1,0:T(8,128)(2,1)} collective-permute-done((bf16[2,384,512]{2,1,0:T(8,128)(2,1)}, bf16[2,384,512]{2,1,0:T(8,128)(2,1)}, u32[]{:S(2)}, u32[]{:S(2)}) %collective-permute-start.12) | collective-permute-done | bytes 786464 | tf_op jit(solution)/shard_map/ppermute | solution.py:88
  80.1 9.0 %collective-permute-done.36.refs_1_.refs_11_ = bf16[2,384,512]{2,1,0:T(8,128)(2,1)} collective-permute-done((bf16[2,384,512]{2,1,0:T(8,128)(2,1)}, bf16[2,384,512]{2,1,0:T(8,128)(2,1)}, u32[]{:S(2)}, u32[]{:S(2)}) %collective-permute-start.36) | collective-permute-done | bytes 786464 | tf_op jit(solution)/shard_map/ppermute | solution.py:88
  90.4 25.3 %collective-permute-done.20 = bf16[4,128,1536]{2,1,0:T(8,128)(2,1)} collective-permute-done((bf16[4,128,1536]{2,1,0:T(8,128)(2,1)}, bf16[4,128,1536]{2,1,0:T(8,128)(2,1)}, u32[]{:S(2)}, u32[]{:S(2)}) %collective-permute-start.20) | collective-permute-done | bytes 1572896 | tf_op jit(solution)/shard_map/ppermute | solution.py:88
  117.0 2.6 broadcast_select_fusion
  119.7 36.6 %collective-permute-start.22 = (bf16[4,128,1536]{2,1,0:T(8,128)(2,1)S(1)}, bf16[4,128,1536]{2,1,0:T(8,128)(2,1)S(1)}, u32[]{:S(2)}, u32[]{:S(2)}) collective-permute-start(bf16[4,128,1536]{2,1,0:T(8,128)(2,1)S(1)} %get-tuple-element.31), channel_id=1, source_target_pairs={{0,8},{1,9},{2,10},{3,11},{4,12},{5,13},{6,14},{7,15},{8,0},{9,1},... | collective-permute-start | bytes 4718600 | tf_op jit(solution)/shard_map/ppermute | solution.py:88
  161.3 18.0 %collective-permute-done = bf16[2,384,512]{2,1,0:T(8,128)(2,1)S(1)} collective-permute-done((bf16[2,384,512]{2,1,0:T(8,128)(2,1)S(1)}, bf16[2,384,512]{2,1,0:T(8,128)(2,1)S(1)}, u32[]{:S(2)}, u32[]{:S(2)}) %collective-permute-start) | collective-permute-done | bytes 786464 | tf_op jit(solution)/shard_map/ppermute | solution.py:88
  180.9 13.6 %collective-permute-done.6 = bf16[2,384,512]{2,1,0:T(8,128)(2,1)S(1)} collective-permute-done((bf16[2,384,512]{2,1,0:T(8,128)(2,1)S(1)}, bf16[2,384,512]{2,1,0:T(8,128)(2,1)S(1)}, u32[]{:S(2)}, u32[]{:S(2)}) %collective-permute-start.6) | collective-permute-done | bytes 786464 | tf_op jit(solution)/shard_map/ppermute | solution.py:88
  201.4 13.6 %collective-permute-done.32.refs_2_.refs_7_ = bf16[2,384,512]{2,1,0:T(8,128)(2,1)S(1)} collective-permute-done((bf16[2,384,512]{2,1,0:T(8,128)(2,1)S(1)}, bf16[2,384,512]{2,1,0:T(8,128)(2,1)S(1)}, u32[]{:S(2)}, u32[]{:S(2)}) %collective-permute-start.32) | collective-permute-done | bytes 786464 | tf_op jit(solution)/shard_map/ppermute | solution.py:88
  220.6 11.2 %collective-permute-done.15.refs_2_.refs_12_ = bf16[2,384,512]{2,1,0:T(8,128)(2,1)S(1)} collective-permute-done((bf16[2,384,512]{2,1,0:T(8,128)(2,1)S(1)}, bf16[2,384,512]{2,1,0:T(8,128)(2,1)S(1)}, u32[]{:S(2)}, u32[]{:S(2)}) %collective-permute-start.15) | collective-permute-done | bytes 786464 | tf_op jit(solution)/shard_map/ppermute | solution.py:88
  235.8 12.9 %collective-permute-done.3.refs_2_ = bf16[2,384,512]{2,1,0:T(8,128)(2,1)S(1)} collective-permute-done((bf16[2,384,512]{2,1,0:T(8,128)(2,1)S(1)}, bf16[2,384,512]{2,1,0:T(8,128)(2,1)S(1)}, u32[]{:S(2)}, u32[]{:S(2)}) %collective-permute-start.3) | collective-permute-done | bytes 786464 | tf_op jit(solution)/shard_map/ppermute | solution.py:88
  251.1 14.5 %collective-permute-done.9.refs_2_.refs_7_ = bf16[2,384,512]{2,1,0:T(8,128)(2,1)S(1)} collective-permute-done((bf16[2,384,512]{2,1,0:T(8,128)(2,1)S(1)}, bf16[2,384,512]{2,1,0:T(8,128)(2,1)S(1)}, u32[]{:S(2)}, u32[]{:S(2)}) %collective-permute-start.9) | collective-permute-done | bytes 786464 | tf_op jit(solution)/shard_map/ppermute | solution.py:88
  278.5 9.9 %terms.9.refs_13_ = f32[4,4,128,128]{3,2,1,0:T(8,128)} custom-call(s32[4]{0:T(128)} %pad_add_fusion.flags, bf16[2,384,512]{2,1,0:T(8,128)(2,1)} %copy-done.12, bf16[2,384,512]{2,1,0:T(8,128)(2,1)} %copy-done.14, bf16[2,384,512]{2,1,0:T(8,128)(2,1)} %copy-done.15, bf16[384,512]{1,0:T(8,128)(2,1)} %copy-done.28, bf16[384,512]{1,0:T(8,128)(2,1)} %copy-done.29, ...), custom_call_target="tpu_custom_call" | custom-call | flops 3489660928 | bytes 9437184 | tf_op jit(solution)/shard_map/terms/pallas_call | solution.py:206
  291.5 9.9 %terms.10.refs_13_ = f32[4,4,128,128]{3,2,1,0:T(8,128)} custom-call(s32[4]{0:T(128)} %pad_add_fusion.flags, bf16[2,384,512]{2,1,0:T(8,128)(2,1)} %copy-done.11, bf16[2,384,512]{2,1,0:T(8,128)(2,1)} %copy-done.16, bf16[2,384,512]{2,1,0:T(8,128)(2,1)} %copy-done.17, bf16[384,512]{1,0:T(8,128)(2,1)} %collective-permute-done.33.refs_3_.refs_8_, ...), custom_call_target="tpu_custom_call" | custom-call | flops 3489660928 | bytes 9437184 | tf_op jit(solution)/shard_map/terms/pallas_call | solution.py:206
  302.5 9.8 %terms.11.refs_19_ = f32[4,4,128,128]{3,2,1,0:T(8,128)} custom-call(s32[4]{0:T(128)} %pad_add_fusion.flags, bf16[2,384,512]{2,1,0:T(8,128)(2,1)} %get-tuple-element.4.refs_0_.refs_10_, bf16[2,384,512]{2,1,0:T(8,128)(2,1)} %collective-permute-done.36.refs_1_.refs_11_, bf16[2,384,512]{2,1,0:T(8,128)(2,1)} %copy-done.13, ...), custom_call_target="tpu_custom_call" | custom-call | flops 3489660928 | bytes 9437184 | tf_op jit(solution)/shard_map/terms/pallas_call | solution.py:206
  312.4 13.3 %terms.12.refs_17_ = f32[4,4,128,128]{3,2,1,0:T(8,128)} custom-call(s32[4]{0:T(128)} %pad_add_fusion.flags, bf16[2,384,512]{2,1,0:T(8,128)(2,1)} %copy-done.12, bf16[2,384,512]{2,1,0:T(8,128)(2,1)} %copy-done.14, bf16[2,384,512]{2,1,0:T(8,128)(2,1)} %copy-done.15, bf16[384,512]{1,0:T(8,128)(2,1)} %copy-done.28, bf16[384,512]{1,0:T(8,128)(2,1)} %copy-done.29, ...), custom_call_target="tpu_custom_call" | custom-call | flops 5234491392 | bytes 14680064 | tf_op jit(solution)/shard_map/terms/pallas_call | solution.py:206
  328.8 12.2 %terms.13.refs_17_ = f32[4,4,128,128]{3,2,1,0:T(8,128)} custom-call(s32[4]{0:T(128)} %pad_add_fusion.flags, bf16[2,384,512]{2,1,0:T(8,128)(2,1)} %copy-done.21, bf16[2,384,512]{2,1,0:T(8,128)(2,1)} %copy-done.32, bf16[2,384,512]{2,1,0:T(8,128)(2,1)} %copy-done.33, bf16[384,512]{1,0:T(8,128)(2,1)} %copy-done.42, bf16[384,512]{1,0:T(8,128)(2,1)} %copy-done.43, ...), custom_call_target="tpu_custom_call" | custom-call | flops 5234491392 | bytes 11534336 | tf_op jit(solution)/shard_map/terms/pallas_call | solution.py:206
  342.6 12.3 %terms.14.refs_17_ = f32[4,4,128,128]{3,2,1,0:T(8,128)} custom-call(s32[4]{0:T(128)} %pad_add_fusion.flags, bf16[2,384,512]{2,1,0:T(8,128)(2,1)} %copy-done.22, bf16[2,384,512]{2,1,0:T(8,128)(2,1)} %copy-done.34, bf16[2,384,512]{2,1,0:T(8,128)(2,1)} %copy-done.35, bf16[384,512]{1,0:T(8,128)(2,1)} %copy-done.44, bf16[384,512]{1,0:T(8,128)(2,1)} %copy-done.45, ...), custom_call_target="tpu_custom_call" | custom-call | flops 5234491392 | bytes 11534336 | tf_op jit(solution)/shard_map/terms/pallas_call | solution.py:206
  356.4 12.5 %terms.15.refs_19_ = f32[4,4,128,128]{3,2,1,0:T(8,128)} custom-call(s32[4]{0:T(128)} %pad_add_fusion.flags, bf16[2,384,512]{2,1,0:T(8,128)(2,1)} %copy-done.20, bf16[2,384,512]{2,1,0:T(8,128)(2,1)} %copy-done.30, bf16[2,384,512]{2,1,0:T(8,128)(2,1)} %copy-done.31, bf16[384,512]{1,0:T(8,128)(2,1)} %copy-done.40, bf16[384,512]{1,0:T(8,128)(2,1)} %copy-done.41, ...), custom_call_target="tpu_custom_call" | custom-call | flops 5234491392 | bytes 11534336 | tf_op jit(solution)/shard_map/terms/pallas_call | solution.py:206
  370.2 13.1 %terms.16.refs_19_ = f32[4,4,128,128]{3,2,1,0:T(8,128)} custom-call(s32[4]{0:T(128)} %pad_add_fusion.flags, bf16[2,384,512]{2,1,0:T(8,128)(2,1)} %copy-done.12, bf16[2,384,512]{2,1,0:T(8,128)(2,1)} %copy-done.14, bf16[2,384,512]{2,1,0:T(8,128)(2,1)} %copy-done.15, bf16[384,512]{1,0:T(8,128)(2,1)} %copy-done.28, bf16[384,512]{1,0:T(8,128)(2,1)} %copy-done.29, ...), custom_call_target="tpu_custom_call" | custom-call | flops 5234491392 | bytes 14680064 | tf_op jit(solution)/shard_map/terms/pallas_call | solution.py:206
  383.2 13.2 %terms.17 = f32[4,4,128,128]{3,2,1,0:T(8,128)} custom-call(s32[4]{0:T(128)} %pad_add_fusion.flags, bf16[2,384,512]{2,1,0:T(8,128)(2,1)} %copy-done.21, bf16[2,384,512]{2,1,0:T(8,128)(2,1)} %copy-done.32, bf16[2,384,512]{2,1,0:T(8,128)(2,1)} %copy-done.33, bf16[384,512]{1,0:T(8,128)(2,1)} %copy-done.42, bf16[384,512]{1,0:T(8,128)(2,1)} %copy-done.43, ...), custom_call_target="tpu_custom_call" | custom-call | flops 5234491392 | bytes 14680064 | tf_op jit(solution)/shard_map/terms/pallas_call | solution.py:206
  401.9 3.7 collective-permute-start.47
  405.7 4.4 %collective-permute-done.45 = f32[4,64,128]{2,1,0:T(8,128)S(1)} collective-permute-done((f32[4,64,128]{2,1,0:T(8,128)S(1)}, f32[4,64,128]{2,1,0:T(8,128)S(1)}, u32[]{:S(2)}, u32[]{:S(2)}) %collective-permute-start.45) | collective-permute-done | bytes 131104 | tf_op jit(solution)/shard_map/ppermute | solution.py:88
  410.1 4.7 %collective-permute-done.46 = f32[4,64,128]{2,1,0:T(8,128)S(1)} collective-permute-done((f32[4,64,128]{2,1,0:T(8,128)S(1)}, f32[4,64,128]{2,1,0:T(8,128)S(1)}, u32[]{:S(2)}, u32[]{:S(2)}) %collective-permute-start.46) | collective-permute-done | bytes 131104 | tf_op jit(solution)/shard_map/ppermute | solution.py:88
  415.4 2.9 collective-permute-start.48
  418.3 3.9 collective-permute-done.48
  (211 shorter events, 82.4 us)
Async XLA Ops:
  4.8 37.6 %collective-permute-start.18 = (bf16[4,128,1536]{2,1,0:T(8,128)(2,1)S(1)}, bf16[4,128,1536]{2,1,0:T(8,128)(2,1)}, u32[]{:S(2)}, u32[]{:S(2)}) collective-permute-start(bf16[4,128,1536]{2,1,0:T(8,128)(2,1)S(1)} %bitcast.63), channel_id=1, source_target_pairs={{0,8},{1,9},{2,10},{3,11},{4,12},{5,13},{6,14},{7,15},{8,0},{9,1},... | collective-permute-start | bytes 4718600 | tf_op jit(solution)/shard_map/ppermute | solution.py:88
  42.3 19.6 %collective-permute-start.19 = (bf16[4,128,1536]{2,1,0:T(8,128)(2,1)}, bf16[4,128,1536]{2,1,0:T(8,128)(2,1)}, u32[]{:S(2)}, u32[]{:S(2)}) collective-permute-start(bf16[4,128,1536]{2,1,0:T(8,128)(2,1)} %collective-permute-done.18), channel_id=1, source_target_pairs={{8,16},{9,17},{10,18},{11,19},{12,20},{13,21},{14,22},{15,23},{16,... | collective-permute-start | bytes 4718600 | tf_op jit(solution)/shard_map/ppermute | solution.py:88
  58.3 20.4 %collective-permute-start.21 = (bf16[4,128,1536]{2,1,0:T(8,128)(2,1)S(1)}, bf16[4,128,1536]{2,1,0:T(8,128)(2,1)}, u32[]{:S(2)}, u32[]{:S(2)}) collective-permute-start(bf16[4,128,1536]{2,1,0:T(8,128)(2,1)S(1)} %bitcast.59), channel_id=1, source_target_pairs={{8,16},{9,17},{10,18},{11,19},{12,20},{13,21},{14,22},{15,23},{16,... | collective-permute-start | bytes 4718600 | tf_op jit(solution)/shard_map/ppermute | solution.py:88
  61.9 53.8 %collective-permute-start.20 = (bf16[4,128,1536]{2,1,0:T(8,128)(2,1)}, bf16[4,128,1536]{2,1,0:T(8,128)(2,1)}, u32[]{:S(2)}, u32[]{:S(2)}) collective-permute-start(bf16[4,128,1536]{2,1,0:T(8,128)(2,1)} %collective-permute-done.19), channel_id=1, source_target_pairs={{8,0},{9,1},{10,2},{11,3},{12,4},{13,5},{14,6},{15,7},{16,24},{17,... | collective-permute-start | bytes 4718600 | tf_op jit(solution)/shard_map/ppermute | solution.py:88
  75.1 44.7 %collective-permute-start.37 = (bf16[2,384,512]{2,1,0:T(8,128)(2,1)S(1)}, bf16[2,384,512]{2,1,0:T(8,128)(2,1)S(1)}, u32[]{:S(2)}, u32[]{:S(2)}) collective-permute-start(bf16[2,384,512]{2,1,0:T(8,128)(2,1)S(1)} %copy-done.10), channel_id=1, source_target_pairs={{0,4},{1,5},{2,6},{3,7},{4,0},{5,1},{6,2},{7,3},{8,12},{9,13},{10,... | collective-permute-start | bytes 2359304 | tf_op jit(solution)/shard_map/ppermute | solution.py:88
  78.7 78.8 %collective-permute-start.1 = (bf16[2,384,512]{2,1,0:T(8,128)(2,1)}, bf16[2,384,512]{2,1,0:T(8,128)(2,1)S(1)}, u32[]{:S(2)}, u32[]{:S(2)}) collective-permute-start(bf16[2,384,512]{2,1,0:T(8,128)(2,1)} %get-tuple-element.13), channel_id=1, source_target_pairs={{1,8},{3,10},{5,12},{7,14},{8,1},{10,3},{12,5},{14,7},{17,24},{19,... | collective-permute-start | bytes 2359304 | tf_op jit(solution)/shard_map/ppermute | solution.py:88
  79.4 80.4 %collective-permute-start.7 = (bf16[2,384,512]{2,1,0:T(8,128)(2,1)S(1)}, bf16[2,384,512]{2,1,0:T(8,128)(2,1)S(1)}, u32[]{:S(2)}, u32[]{:S(2)}) collective-permute-start(bf16[2,384,512]{2,1,0:T(8,128)(2,1)S(1)} %copy-done.23), channel_id=1, source_target_pairs={{1,8},{3,10},{5,12},{7,14},{8,1},{10,3},{12,5},{14,7},{17,24},{19,... | collective-permute-start | bytes 2359304 | tf_op jit(solution)/shard_map/ppermute | solution.py:88
  89.1 90.2 %collective-permute-start = (bf16[2,384,512]{2,1,0:T(8,128)(2,1)S(1)}, bf16[2,384,512]{2,1,0:T(8,128)(2,1)S(1)}, u32[]{:S(2)}, u32[]{:S(2)}) collective-permute-start(bf16[2,384,512]{2,1,0:T(8,128)(2,1)S(1)} %get-tuple-element.15), channel_id=1, source_target_pairs={{1,9},{3,11},{5,13},{7,15},{8,0},{10,2},{12,4},{14,6},{17,25},{19,... | collective-permute-start | bytes 2359304 | tf_op jit(solution)/shard_map/ppermute | solution.py:88
  115.7 78.8 %collective-permute-start.6 = (bf16[2,384,512]{2,1,0:T(8,128)(2,1)S(1)}, bf16[2,384,512]{2,1,0:T(8,128)(2,1)S(1)}, u32[]{:S(2)}, u32[]{:S(2)}) collective-permute-start(bf16[2,384,512]{2,1,0:T(8,128)(2,1)S(1)} %get-tuple-element.7), channel_id=1, source_target_pairs={{1,9},{3,11},{5,13},{7,15},{8,0},{10,2},{12,4},{14,6},{17,25},{19,... | collective-permute-start | bytes 2359304 | tf_op jit(solution)/shard_map/ppermute | solution.py:88
  119.7 96.8 %collective-permute-start.22 = (bf16[4,128,1536]{2,1,0:T(8,128)(2,1)S(1)}, bf16[4,128,1536]{2,1,0:T(8,128)(2,1)S(1)}, u32[]{:S(2)}, u32[]{:S(2)}) collective-permute-start(bf16[4,128,1536]{2,1,0:T(8,128)(2,1)S(1)} %get-tuple-element.31), channel_id=1, source_target_pairs={{0,8},{1,9},{2,10},{3,11},{4,12},{5,13},{6,14},{7,15},{8,0},{9,1},... | collective-permute-start | bytes 4718600 | tf_op jit(solution)/shard_map/ppermute | solution.py:88
  157.4 38.7 %collective-permute-start.26 = (bf16[2,384,512]{2,1,0:T(8,128)(2,1)S(1)}, bf16[2,384,512]{2,1,0:T(8,128)(2,1)S(1)}, u32[]{:S(2)}, u32[]{:S(2)}) collective-permute-start(bf16[2,384,512]{2,1,0:T(8,128)(2,1)S(1)} %get-tuple-element.14.refs_0_), channel_id=1, source_target_pairs={{0,2},{1,3},{2,0},{3,1},{4,6},{5,7},{6,4},{7,5},{8,10},{9,11},{10,... | collective-permute-start | bytes 2359304 | tf_op jit(solution)/shard_map/ppermute | solution.py:88
  159.8 37.9 %collective-permute-start.27 = (bf16[2,384,512]{2,1,0:T(8,128)(2,1)S(1)}, bf16[2,384,512]{2,1,0:T(8,128)(2,1)S(1)}, u32[]{:S(2)}, u32[]{:S(2)}) collective-permute-start(bf16[2,384,512]{2,1,0:T(8,128)(2,1)S(1)} %get-tuple-element.14.refs_0_), channel_id=1, source_target_pairs={{0,4},{1,5},{2,6},{3,7},{4,0},{5,1},{6,2},{7,3},{8,12},{9,13},{10,... | collective-permute-start | bytes 2359304 | tf_op jit(solution)/shard_map/ppermute | solution.py:88
  179.3 19.8 %collective-permute-start.31 = (bf16[2,384,512]{2,1,0:T(8,128)(2,1)S(1)}, bf16[2,384,512]{2,1,0:T(8,128)(2,1)S(1)}, u32[]{:S(2)}, u32[]{:S(2)}) collective-permute-start(bf16[2,384,512]{2,1,0:T(8,128)(2,1)S(1)} %get-tuple-element.6.refs_0_.refs_5_), channel_id=1, source_target_pairs={{0,2},{1,3},{2,0},{3,1},{4,6},{5,7},{6,4},{7,5},{8,10},{9,11},{10,... | collective-permute-start | bytes 2359304 | tf_op jit(solution)/shard_map/ppermute | solution.py:88
  194.5 20.5 %collective-permute-start.32 = (bf16[2,384,512]{2,1,0:T(8,128)(2,1)S(1)}, bf16[2,384,512]{2,1,0:T(8,128)(2,1)S(1)}, u32[]{:S(2)}, u32[]{:S(2)}) collective-permute-start(bf16[2,384,512]{2,1,0:T(8,128)(2,1)S(1)} %get-tuple-element.6.refs_0_.refs_5_), channel_id=1, source_target_pairs={{0,4},{1,5},{2,6},{3,7},{4,0},{5,1},{6,2},{7,3},{8,12},{9,13},{10,... | collective-permute-start | bytes 2359304 | tf_op jit(solution)/shard_map/ppermute | solution.py:88
  196.2 22.1 %collective-permute-start.14 = (bf16[2,384,512]{2,1,0:T(8,128)(2,1)S(1)}, bf16[2,384,512]{2,1,0:T(8,128)(2,1)S(1)}, u32[]{:S(2)}, u32[]{:S(2)}) collective-permute-start(bf16[2,384,512]{2,1,0:T(8,128)(2,1)S(1)} %broadcast_select_fusion.11.refs_0_.refs_10_), channel_id=1, source_target_pairs={{0,2},{1,3},{2,0},{3,1},{4,6},{5,7},{6,4},{7,5},{8,10},{9,11},{10,... | collective-permute-start | bytes 2359304 | tf_op jit(solution)/shard_map/ppermute | solution.py:88
  197.8 34.1 %collective-permute-start.15 = (bf16[2,384,512]{2,1,0:T(8,128)(2,1)S(1)}, bf16[2,384,512]{2,1,0:T(8,128)(2,1)S(1)}, u32[]{:S(2)}, u32[]{:S(2)}) collective-permute-start(bf16[2,384,512]{2,1,0:T(8,128)(2,1)S(1)} %broadcast_select_fusion.11.refs_0_.refs_10_), channel_id=1, source_target_pairs={{0,4},{1,5},{2,6},{3,7},{4,0},{5,1},{6,2},{7,3},{8,12},{9,13},{10,... | collective-permute-start | bytes 2359304 | tf_op jit(solution)/shard_map/ppermute | solution.py:88
  199.2 35.0 %collective-permute-start.2 = (bf16[2,384,512]{2,1,0:T(8,128)(2,1)S(1)}, bf16[2,384,512]{2,1,0:T(8,128)(2,1)S(1)}, u32[]{:S(2)}, u32[]{:S(2)}) collective-permute-start(bf16[2,384,512]{2,1,0:T(8,128)(2,1)S(1)} %broadcast_select_fusion.13.refs_0_), channel_id=1, source_target_pairs={{0,2},{1,3},{2,0},{3,1},{4,6},{5,7},{6,4},{7,5},{8,10},{9,11},{10,... | collective-permute-start | bytes 2359304 | tf_op jit(solution)/shard_map/ppermute | solution.py:88
  215.0 33.7 %collective-permute-start.3 = (bf16[2,384,512]{2,1,0:T(8,128)(2,1)S(1)}, bf16[2,384,512]{2,1,0:T(8,128)(2,1)S(1)}, u32[]{:S(2)}, u32[]{:S(2)}) collective-permute-start(bf16[2,384,512]{2,1,0:T(8,128)(2,1)S(1)} %broadcast_select_fusion.13.refs_0_), channel_id=1, source_target_pairs={{0,4},{1,5},{2,6},{3,7},{4,0},{5,1},{6,2},{7,3},{8,12},{9,13},{10,... | collective-permute-start | bytes 2359304 | tf_op jit(solution)/shard_map/ppermute | solution.py:88
  216.5 49.9 %collective-permute-start.24 = (bf16[4,128,1536]{2,1,0:T(8,128)(2,1)S(1)}, bf16[4,128,1536]{2,1,0:T(8,128)(2,1)S(1)}, u32[]{:S(2)}, u32[]{:S(2)}) collective-permute-start(bf16[4,128,1536]{2,1,0:T(8,128)(2,1)S(1)} %collective-permute-done.22), channel_id=1, source_target_pairs={{8,16},{9,17},{10,18},{11,19},{12,20},{13,21},{14,22},{15,23},{16,... | collective-permute-start | bytes 4718600 | tf_op jit(solution)/shard_map/ppermute | solution.py:88
  218.3 32.7 %collective-permute-start.8 = (bf16[2,384,512]{2,1,0:T(8,128)(2,1)S(1)}, bf16[2,384,512]{2,1,0:T(8,128)(2,1)S(1)}, u32[]{:S(2)}, u32[]{:S(2)}) collective-permute-start(bf16[2,384,512]{2,1,0:T(8,128)(2,1)S(1)} %broadcast_select_fusion.12.refs_0_.refs_5_), channel_id=1, source_target_pairs={{0,2},{1,3},{2,0},{3,1},{4,6},{5,7},{6,4},{7,5},{8,10},{9,11},{10,... | collective-permute-start | bytes 2359304 | tf_op jit(solution)/shard_map/ppermute | solution.py:88
  231.9 33.7 %collective-permute-start.9 = (bf16[2,384,512]{2,1,0:T(8,128)(2,1)S(1)}, bf16[2,384,512]{2,1,0:T(8,128)(2,1)S(1)}, u32[]{:S(2)}, u32[]{:S(2)}) collective-permute-start(bf16[2,384,512]{2,1,0:T(8,128)(2,1)S(1)} %broadcast_select_fusion.12.refs_0_.refs_5_), channel_id=1, source_target_pairs={{0,4},{1,5},{2,6},{3,7},{4,0},{5,1},{6,2},{7,3},{8,12},{9,13},{10,... | collective-permute-start | bytes 2359304 | tf_op jit(solution)/shard_map/ppermute | solution.py:88
  234.2 37.9 %collective-permute-start.28 = (bf16[384,512]{1,0:T(8,128)(2,1)S(1)}, bf16[384,512]{1,0:T(8,128)(2,1)S(1)}, u32[]{:S(2)}, u32[]{:S(2)}) collective-permute-start(bf16[384,512]{1,0:T(8,128)(2,1)S(1)} %slice_bitcast_fusion.5), channel_id=1, source_target_pairs={{0,4},{1,5},{2,6},{3,7},{4,0},{5,1},{6,2},{7,3},{8,12},{9,13},{10,... | collective-permute-start | bytes 1179656 | tf_op jit(solution)/shard_map/ppermute | solution.py:88
  248.7 24.8 %collective-permute-start.29 = (bf16[384,512]{1,0:T(8,128)(2,1)S(1)}, bf16[384,512]{1,0:T(8,128)(2,1)S(1)}, u32[]{:S(2)}, u32[]{:S(2)}) collective-permute-start(bf16[384,512]{1,0:T(8,128)(2,1)S(1)} %slice_bitcast_fusion.4), channel_id=1, source_target_pairs={{0,2},{1,3},{2,0},{3,1},{4,6},{5,7},{6,4},{7,5},{8,10},{9,11},{10,... | collective-permute-start | bytes 1179656 | tf_op jit(solution)/shard_map/ppermute | solution.py:88
  251.0 25.2 %collective-permute-start.40 = (bf16[4,128,1536]{2,1,0:T(8,128)(2,1)S(1)}, bf16[4,128,1536]{2,1,0:T(8,128)(2,1)S(1)}, u32[]{:S(2)}, u32[]{:S(2)}) collective-permute-start(bf16[4,128,1536]{2,1,0:T(8,128)(2,1)S(1)} %get-tuple-element.32.refs_5_), channel_id=1, source_target_pairs={{0,1},{1,0},{2,3},{3,2},{4,5},{5,4},{6,7},{7,6},{8,9},{9,8},{10,11... | collective-permute-start | bytes 4718600 | tf_op jit(solution)/shard_map/ppermute | solution.py:88
  268.3 44.0 %collective-permute-start.42 = (bf16[4,128,1536]{2,1,0:T(8,128)(2,1)S(1)}, bf16[4,128,1536]{2,1,0:T(8,128)(2,1)}, u32[]{:S(2)}, u32[]{:S(2)}) collective-permute-start(bf16[4,128,1536]{2,1,0:T(8,128)(2,1)S(1)} %get-tuple-element.33.refs_15_.refs_7_), channel_id=1, source_target_pairs={{0,1},{1,0},{2,3},{3,2},{4,5},{5,4},{6,7},{7,6},{8,9},{9,8},{10,11... | collective-permute-start | bytes 4718600 | tf_op jit(solution)/shard_map/ppermute | solution.py:88
  276.3 25.1 %collective-permute-start.38 = (bf16[384,512]{1,0:T(8,128)(2,1)S(1)}, bf16[384,512]{1,0:T(8,128)(2,1)}, u32[]{:S(2)}, u32[]{:S(2)}) collective-permute-start(bf16[384,512]{1,0:T(8,128)(2,1)S(1)} %slice_bitcast_fusion.1), channel_id=1, source_target_pairs={{0,4},{1,5},{2,6},{3,7},{4,0},{5,1},{6,2},{7,3},{8,12},{9,13},{10,... | collective-permute-start | bytes 1179656 | tf_op jit(solution)/shard_map/ppermute | solution.py:88
  276.8 25.1 %collective-permute-start.39 = (bf16[384,512]{1,0:T(8,128)(2,1)}, bf16[384,512]{1,0:T(8,128)(2,1)}, u32[]{:S(2)}, u32[]{:S(2)}) collective-permute-start(bf16[384,512]{1,0:T(8,128)(2,1)} %slice_bitcast_fusion), channel_id=1, source_target_pairs={{0,2},{1,3},{2,0},{3,1},{4,6},{5,7},{6,4},{7,5},{8,10},{9,11},{10,... | collective-permute-start | bytes 1179656 | tf_op jit(solution)/shard_map/ppermute | solution.py:88
  288.4 66.5 %collective-permute-start.16 = (bf16[384,512]{1,0:T(8,128)(2,1)S(1)}, bf16[384,512]{1,0:T(8,128)(2,1)S(1)}, u32[]{:S(2)}, u32[]{:S(2)}) collective-permute-start(bf16[384,512]{1,0:T(8,128)(2,1)S(1)} %copy-done.24), channel_id=1, source_target_pairs={{0,4},{1,5},{2,6},{3,7},{4,0},{5,1},{6,2},{7,3},{8,12},{9,13},{10,... | collective-permute-start | bytes 1179656 | tf_op jit(solution)/shard_map/ppermute | solution.py:88
  290.0 64.9 %collective-permute-start.17 = (bf16[384,512]{1,0:T(8,128)(2,1)S(1)}, bf16[384,512]{1,0:T(8,128)(2,1)S(1)}, u32[]{:S(2)}, u32[]{:S(2)}) collective-permute-start(bf16[384,512]{1,0:T(8,128)(2,1)S(1)} %copy-done.25), channel_id=1, source_target_pairs={{0,2},{1,3},{2,0},{3,1},{4,6},{5,7},{6,4},{7,5},{8,10},{9,11},{10,... | collective-permute-start | bytes 1179656 | tf_op jit(solution)/shard_map/ppermute | solution.py:88
  301.4 24.3 %collective-permute-start.4 = (bf16[384,512]{1,0:T(8,128)(2,1)S(1)}, bf16[384,512]{1,0:T(8,128)(2,1)S(1)}, u32[]{:S(2)}, u32[]{:S(2)}) collective-permute-start(bf16[384,512]{1,0:T(8,128)(2,1)S(1)} %copy-done.26), channel_id=1, source_target_pairs={{0,4},{1,5},{2,6},{3,7},{4,0},{5,1},{6,2},{7,3},{8,12},{9,13},{10,... | collective-permute-start | bytes 1179656 | tf_op jit(solution)/shard_map/ppermute | solution.py:88
  302.0 25.3 %collective-permute-start.5 = (bf16[384,512]{1,0:T(8,128)(2,1)S(1)}, bf16[384,512]{1,0:T(8,128)(2,1)S(1)}, u32[]{:S(2)}, u32[]{:S(2)}) collective-permute-start(bf16[384,512]{1,0:T(8,128)(2,1)S(1)} %copy-done.27), channel_id=1, source_target_pairs={{0,2},{1,3},{2,0},{3,1},{4,6},{5,7},{6,4},{7,5},{8,10},{9,11},{10,... | collective-permute-start | bytes 1179656 | tf_op jit(solution)/shard_map/ppermute | solution.py:88
  312.3 56.6 %collective-permute-start.23 = (bf16[4,128,1536]{2,1,0:T(8,128)(2,1)S(1)}, bf16[4,128,1536]{2,1,0:T(8,128)(2,1)S(1)}, u32[]{:S(2)}, u32[]{:S(2)}) collective-permute-start(bf16[4,128,1536]{2,1,0:T(8,128)(2,1)S(1)} %get-tuple-element.35.refs_15_), channel_id=1, source_target_pairs={{0,1},{1,0},{2,3},{3,2},{4,5},{5,4},{6,7},{7,6},{8,9},{9,8},{10,11... | collective-permute-start | bytes 4718600 | tf_op jit(solution)/shard_map/ppermute | solution.py:88
  (63 other events, 1796.2 us)

commit v2 on v0

--- a/solution.py
+++ b/solution.py
@@ -1,6 +1,10 @@
+import functools
+
 import jax
 import jax.numpy as jnp
 from jax import lax
+from jax.experimental import pallas as pl
+from jax.experimental.pallas import tpu as pltpu
 from jax.sharding import PartitionSpec as P
 
 
@@ -19,6 +23,10 @@
 def combine_terms(partial_value, order_table, pair_count):
     block_re = partial_value[:, 0, :, :pair_count] - partial_value[:, 1, :, pair_count:]
     block_im = partial_value[:, 0, :, pair_count:] + partial_value[:, 1, :, :pair_count]
+    return reorder(block_re, block_im, order_table)
+
+
+def reorder(block_re, block_im, order_table):
     block_re = jnp.einsum("kpq,qj->kpj", block_re, order_table, precision=lax.Precision.HIGHEST)
     block_im = jnp.einsum("kpq,qj->kpj", block_im, order_table, precision=lax.Precision.HIGHEST)
     return jnp.concatenate([block_re, block_im], axis=2)
@@ -33,7 +41,7 @@
     )
 
 
-def body(densities, screened, partner, pair_order):
+def general_body(densities, screened, partner, pair_order):
     k_count = densities.shape[0]
     pair_count = densities.shape[2] // 2
     panel_width = screened.shape[2]
@@ -61,7 +69,592 @@
     return (direct, mirror)
 
 
+AXES = ("ka", "ga")
+STEP = 256
+WIDE_STEP = 512
+
+
+def device(z, b, c):
+    return (z * 4 + b) * 2 + c
+
+
+def moved(value, rule):
+    pairs = []
+    for z in range(4):
+        for b in range(4):
+            for c in range(2):
+                target = rule(z, b, c)
+                if target is not None:
+                    pairs.append((device(z, b, c), device(*target)))
+    return lax.ppermute(value, AXES, pairs)
+
+
+def along_x(value):
+    return moved(value, lambda z, b, c: (z, b ^ 1, c))
+
+
+def along_y(value):
+    return moved(value, lambda z, b, c: (z, b ^ 2, c))
+
+
+def other_core(value):
+    return moved(value, lambda z, b, c: (z, b, 1 - c))
+
+
+def end_with_mid(value):
+    return moved(value, lambda z, b, c: (z ^ 1, b, c))
+
+
+def mid_to_end(value):
+    return moved(value, lambda z, b, c: (z ^ 1, b, c) if z in (1, 2) else None)
+
+
+def mid_with_mid(value):
+    return moved(value, lambda z, b, c: (3 - z, b, c) if z in (1, 2) else None)
+
+
+ANYWHERE = pl.BlockSpec(memory_space=pltpu.HBM)
+IN_SMEM = pl.BlockSpec(memory_space=pltpu.SMEM)
+IN_VMEM = pl.BlockSpec(memory_space=pltpu.VMEM)
+PARAMS = pltpu.CompilerParams(vmem_limit_bytes=60 * 1024 * 1024)
+COST = pl.CostEstimate(flops=1000, bytes_accessed=1000, transcendentals=0)
+FLAGS = jax.ShapeDtypeStruct((8,), jnp.int32)
+
+
+def keep_flags(flags, out):
+    for i in range(flags.shape[0]):
+        out[i] = flags[i]
+
+
+def always(flags):
+    return None
+
+
+def at_end(flags):
+    return flags[4] == 1
+
+
+def at_mid(flags):
+    return flags[4] == 0
+
+
+def own_near(flags):
+    return flags[1] == 1
+
+
+def own_far(flags):
+    return flags[1] == 0
+
+
+def whole(ref):
+    return ref
+
+
+def real(first, width):
+    return lambda ref: ref.at[0, :, first : first + width]
+
+
+def imaginary(first, width):
+    return lambda ref: ref.at[1, :, first : first + width]
+
+
+def columns_of(first, width):
+    return lambda ref: ref.at[:, first : first + width]
+
+
+def moves_kernel(flags, *refs, plan, n_sources, n_outs, n_passing):
+    sources, outs = refs[:n_sources], refs[n_sources : n_sources + n_outs]
+    flags_out, *stages = refs[n_sources + n_outs + n_passing : -2]
+    in_sems, out_sems = refs[-2:]
+
+    def run(chosen, act):
+        if chosen is None:
+            act()
+        else:
+            pl.when(chosen)(act)
+
+    copies = []
+    for i, (when, number, view, out_number, target) in enumerate(plan):
+        stage = target(stages[out_number])
+        load = pltpu.make_async_copy(view(sources[number]), stage, in_sems.at[i])
+        store = pltpu.make_async_copy(stage, target(outs[out_number]), out_sems.at[i])
+        copies.append((when(flags), load, store))
+        run(when(flags), load.start)
+    keep_flags(flags, flags_out)
+    for chosen, load, store in copies:
+        def forward():
+            load.wait()
+            store.start()
+
+        run(chosen, forward)
+    for chosen, _, store in copies:
+        run(chosen, store.wait)
+
+
+def moves(flags, waits, *outputs, passing=()):
+    sources, plan = [], []
+    for number, (_, pieces) in enumerate(outputs):
+        for when, source, view, target in pieces:
+            plan.append((when, len(sources), view, number, target))
+            sources.append(source)
+    operands = sources + list(waits)
+    shapes = [jax.ShapeDtypeStruct(shape, jnp.bfloat16) for shape, _ in outputs]
+    aliases = {1 + len(operands) + i: len(outputs) + i for i in range(len(passing))}
+    operands += list(passing)
+    shapes += [jax.ShapeDtypeStruct(value.shape, value.dtype) for value in passing]
+    results = pl.pallas_call(
+        functools.partial(
+            moves_kernel, plan=tuple(plan), n_sources=len(operands), n_outs=len(outputs), n_passing=len(passing)
+        ),
+        out_shape=tuple(shapes) + (FLAGS,),
+        in_specs=[IN_SMEM] + [ANYWHERE] * len(operands),
+        out_specs=(ANYWHERE,) * len(shapes) + (IN_SMEM,),
+        input_output_aliases=aliases,
+        scratch_shapes=[pltpu.VMEM(shape, jnp.bfloat16) for shape, _ in outputs]
+        + [pltpu.SemaphoreType.DMA((max(len(plan), 1),))] * 2,
+        compiler_params=PARAMS,
+        cost_estimate=COST,
+        name="moves",
+    )(flags, *operands)
+    return results[-1], *results[:-1]
+
+
+def w_copies(blocks, places, own_b, w_buf, source_at, target_at, step, sems):
+    width, real_at, imaginary_at = places
+    own, x_side, y_side, d_re, d_im = blocks
+    rows = own.shape[0]
+    copies = []
+
+    def add(source, first, part, turn):
+        start = pl.multiple_of((own_b ^ turn) * rows, rows)
+        target = w_buf.at[part, pl.ds(start, rows), target_at : target_at + step]
+        source = source.at[:, first + source_at : first + source_at + step]
+        copies.append(pltpu.make_async_copy(source, target, sems.at[len(copies)]))
+
+    for turn, source in ((0, own), (1, x_side), (2, y_side)):
+        add(source, 0, 0, turn)
+        add(source, width, 1, turn)
+    add(d_re, real_at, 0, 3)
+    add(d_im, imaginary_at, 1, 3)
+    return copies
+
+
+def either(chosen, first, second, target, sem):
+    a = pltpu.make_async_copy(first, target, sem)
+    b = pltpu.make_async_copy(second, target, sem)
+    pl.when(chosen)(a.start)
+    pl.when(jnp.logical_not(chosen))(b.start)
+    return a
+
+
+def matched_copies(flags, matched, c_buf, first, width, sems):
+    n_slots = c_buf.shape[0]
+    slot_0, slot_2, near_one, far_one = [matched[2 * i : 2 * i + 2] for i in range(4)]
+    quarter = slot_0[0].shape[2]
+    for s in range(n_slots):
+        for half, s_matched in ((0, (s + 1) % n_slots), (1, (s - 1) % n_slots)):
+            for end, ordered in ((1, (slot_0, near_one, slot_2, far_one)), (0, (slot_0, far_one, slot_2, near_one))):
+                for number in range(2):
+                    low, high = max(first, number * quarter), min(first + width, (number + 1) * quarter)
+                    if low >= high:
+                        continue
+                    for core in range(2):
+                        source = ordered[s_matched][0 if core == number else 1]
+                        copy = pltpu.make_async_copy(
+                            source.at[:, :, low - number * quarter : high - number * quarter],
+                            c_buf.at[s, :, :, low - first : high - first],
+                            sems.at[s],
+                        )
+                        pl.when((flags[2] == half) & (flags[4] == end) & (flags[5] == core))(copy.start)
+
+
+def matched_wait(c_buf, s, sems):
+    pltpu.make_async_copy(c_buf.at[s], c_buf.at[s], sems.at[s]).wait()
+
+
+def left_tile(lhs, w_re, w_im, k_count, both):
+    re_side = jnp.dot(lhs, w_re, preferred_element_type=jnp.float32).reshape(k_count, both, -1)
+    im_side = jnp.dot(lhs, w_im, preferred_element_type=jnp.float32).reshape(k_count, both, -1)
+    pairs = both // 2
+    left_re = re_side[:, :pairs] + im_side[:, pairs:]
+    left_im = im_side[:, :pairs] - re_side[:, pairs:]
+    return jnp.concatenate([left_re, left_im], axis=1)
+
+
+def times_matched(left, matched):
+    high_part = left.astype(jnp.bfloat16)
+    low_part = (left - high_part.astype(jnp.float32)).astype(jnp.bfloat16)
+    rows = left.shape[0]
+    both_parts = jnp.concatenate([high_part, low_part], axis=0)
+    dims = (((1,), (1,)), ((), ()))
+    added = lax.dot_general(both_parts, matched, dims, preferred_element_type=jnp.float32)
+    return added[:rows] + added[rows:]
+
+
+def first_kernel(flags, *refs, first_slot, n_slots, columns, places, step, fresh):
+    n_chunks = len(columns)
+    w_refs = [refs[5 * i : 5 * i + 5] for i in range(n_chunks)]
+    rest = refs[5 * n_chunks :]
+    of_end, of_mid = rest[:n_slots], rest[n_slots : 2 * n_slots]
+    rest = rest[2 * n_slots :]
+    if not fresh:
+        rest = rest[1:]
+    left, flags_out, w_buf, m_buf, out_buf, w_sems, m_sems, out_sems = rest
+    depth = w_buf.shape[1]
+    _, k_count, both, _ = m_buf.shape
+    base = columns[0][0]
+    copies, used = [], 0
+    for i in range(n_chunks):
+        for at in range(0, columns[i][1], step):
+            copies.append(w_copies(w_refs[i], places[i], flags[0], w_buf, at, used, step, w_sems.at[used // step]))
+            used += step
+    total = n_slots * (used // step)
+    for copy in copies[0]:
+        copy.start()
+    for s in range(n_slots):
+        either(at_end(flags), of_end[s], of_mid[s], m_buf.at[s], m_sems.at[s])
+    for here in copies[1:]:
+        for copy in here:
+            copy.start()
+    keep_flags(flags, flags_out)
+
+    def out_copy(t):
+        start = pl.multiple_of(base + (t // n_slots) * step, STEP)
+        target = left.at[first_slot + t % n_slots, :, :, pl.ds(start, step)]
+        return pltpu.make_async_copy(out_buf.at[t % 2], target, out_sems.at[t % 2])
+
+    def one_step(t, carry):
+        @pl.when(t >= 2)
+        def _():
+            out_copy(t - 2).wait()
+
+        tile_number, s = t // n_slots, t % n_slots
+        start = pl.multiple_of(tile_number * step, step)
+
+        @pl.when(s == 0)
+        def _():
+            for copy in w_copies(w_refs[0], places[0], flags[0], w_buf, 0, 0, step, w_sems.at[tile_number]):
+                copy.wait()
+
+        @pl.when(tile_number == 0)
+        def _():
+            pltpu.make_async_copy(of_end[0], m_buf.at[s], m_sems.at[s]).wait()
+
+        lhs = m_buf[s].reshape(k_count * both, depth)
+        out_buf[t % 2] = left_tile(lhs, w_buf[0, :, pl.ds(start, step)], w_buf[1, :, pl.ds(start, step)], k_count, both)
+        out_copy(t).start()
+        return carry
+
+    lax.fori_loop(0, total, one_step, 0)
+    for t in range(max(total - 2, 0), total):
+        out_copy(t).wait()
+
+
+def first_product(flags, chunks, first_slot, n_slots, of_end, of_mid, left, all_columns):
+    depth = 4 * chunks[0][2][0].shape[0]
+    k_count, both, _ = of_end[first_slot].shape
+    columns = tuple((first, width) for first, width, _, _ in chunks)
+    span = sum(width for _, width in columns)
+    slots = range(first_slot, first_slot + n_slots)
+    step = WIDE_STEP if all(width % WIDE_STEP == 0 for _, width in columns) else STEP
+    operands = [ref for _, _, blocks, _ in chunks for ref in blocks]
+    operands += [of_end[s] for s in slots] + [of_mid[s] for s in slots]
+    aliases = {}
+    if left is not None:
+        operands.append(left)
+        aliases = {len(operands): 0}
+    whole = jax.ShapeDtypeStruct((4, k_count, both, all_columns), jnp.float32)
+    return pl.pallas_call(
+        functools.partial(
+            first_kernel, first_slot=first_slot, n_slots=n_slots, columns=columns, step=step, fresh=left is None,
+            places=tuple(places for _, _, _, places in chunks),
+        ),
+        out_shape=(whole, FLAGS),
+        in_specs=[IN_SMEM] + [ANYWHERE] * len(operands),
+        out_specs=(ANYWHERE, IN_SMEM),
+        input_output_aliases=aliases,
+        scratch_shapes=[
+            pltpu.VMEM((2, depth, span), jnp.bfloat16),
+            pltpu.VMEM((n_slots, k_count, both, depth), jnp.bfloat16),
+            pltpu.VMEM((2, k_count, both, step), jnp.float32),
+            pltpu.SemaphoreType.DMA((span // step, 8)),
+            pltpu.SemaphoreType.DMA((n_slots,)),
+            pltpu.SemaphoreType.DMA((2,)),
+        ],
+        compiler_params=PARAMS,
+        cost_estimate=COST,
+        name="first_product",
+    )(flags, *operands)
+
+
+def second_kernel(flags, left, *refs, base, width):
+    matched = refs[:8]
+    sums, flags_out, left_buf, c_buf, left_sems, c_sems = refs[8:]
+    shift = flags[3]
+    n_slots, k_count = c_buf.shape[:2]
+    window = slice(base, base + width)
+
+    def left_copy(t):
+        source = left.at[t // k_count, t % k_count, :, window]
+        return pltpu.make_async_copy(source, left_buf.at[t % 4], left_sems.at[t % 4])
+
+    for t in range(4):
+        left_copy(t).start()
+    matched_copies(flags, matched, c_buf, base, width, c_sems)
+    keep_flags(flags, flags_out)
+
+    def step(t, carry):
+        s, k = t // k_count, t % k_count
+
+        @pl.when(k == 0)
+        def _():
+            matched_wait(c_buf, s, c_sems)
+
+        left_copy(t).wait()
+        sums[s, k] = times_matched(left_buf[t % 4], c_buf[s, (k + shift) % k_count])
+
+        @pl.when(t + 4 < n_slots * k_count)
+        def _():
+            left_copy(t + 4).start()
+
+        return carry
+
+    lax.fori_loop(0, n_slots * k_count, step, 0)
+
+
+def second_product(flags, left, matched, base, width):
+    n_slots, k_count, both, _ = left.shape
+    return pl.pallas_call(
+        functools.partial(second_kernel, base=base, width=width),
+        out_shape=(jax.ShapeDtypeStruct((n_slots, k_count, both, both), jnp.float32), FLAGS),
+        in_specs=[IN_SMEM] + [ANYWHERE] * (1 + len(matched)),
+        out_specs=(IN_VMEM, IN_SMEM),
+        scratch_shapes=[
+            pltpu.VMEM((4, both, width), jnp.float32),
+            pltpu.VMEM((n_slots, k_count, both, width), jnp.bfloat16),
+            pltpu.SemaphoreType.DMA((4,)),
+            pltpu.SemaphoreType.DMA((n_slots,)),
+        ],
+        compiler_params=PARAMS,
+        cost_estimate=COST,
+        name="second_product",
+    )(flags, left, *matched)
+
+
+def last_kernel(flags, *refs, n_slots, base, places):
+    w_refs, rest = refs[:5], refs[5:]
+    of_end, of_mid, rest = rest[:n_slots], rest[n_slots : 2 * n_slots], rest[2 * n_slots :]
+    matched, rest = rest[:8], rest[8:]
+    sums, blocks, w_buf, m_buf, c_buf, w_sems, m_sems, c_sems = rest
+    shift = flags[3]
+    depth, width = w_buf.shape[1:]
+    _, k_count, both, _ = m_buf.shape
+    pairs = both // 2
+    copies = w_copies(w_refs, places, flags[0], w_buf, 0, 0, width, w_sems)
+    for copy in copies:
+        copy.start()
+    for s in range(n_slots):
+        either(at_end(flags), of_end[s], of_mid[s], m_buf.at[s], m_sems.at[s])
+    matched_copies(flags, matched, c_buf, base, width, c_sems)
+    for copy in copies:
+        copy.wait()
+
+    def step(s, carry):
+        pltpu.make_async_copy(of_end[0], m_buf.at[s], m_sems.at[s]).wait()
+        matched_wait(c_buf, s, c_sems)
+        lhs = m_buf[s].reshape(k_count * both, depth)
+        tile = left_tile(lhs, w_buf[0], w_buf[1], k_count, both)
+        for k in range(k_count):
+            terms = sums[s, k] + times_matched(tile[k], c_buf[s, (k + shift) % k_count])
+            blocks[s, k, :, :pairs] = terms[:pairs, :pairs] - terms[pairs:, pairs:]
+            blocks[s, k, :, pairs:] = terms[:pairs, pairs:] + terms[pairs:, :pairs]
+        return carry
+
+    lax.fori_loop(0, n_slots, step, 0)
+
+
+def last_product(flags, chunk, of_end, of_mid, matched, sums):
+    n_slots, k_count, both, _ = sums.shape
+    base, width, w_blocks, places = chunk
+    depth = 4 * w_blocks[0].shape[0]
+    operands = list(w_blocks) + list(of_end) + list(of_mid) + list(matched)
+    return pl.pallas_call(
+        functools.partial(last_kernel, n_slots=n_slots, base=base, places=places),
+        out_shape=jax.ShapeDtypeStruct((n_slots, k_count, both // 2, both), jnp.float32),
+        in_specs=[IN_SMEM] + [ANYWHERE] * len(operands) + [IN_VMEM],
+        out_specs=IN_VMEM,
+        scratch_shapes=[
+            pltpu.VMEM((2, depth, width), jnp.bfloat16),
+            pltpu.VMEM((n_slots, k_count, both, depth), jnp.bfloat16),
+            pltpu.VMEM((n_slots, k_count, both, width), jnp.bfloat16),
+            pltpu.SemaphoreType.DMA((8,)),
+            pltpu.SemaphoreType.DMA((n_slots,)),
+            pltpu.SemaphoreType.DMA((n_slots,)),
+        ],
+        compiler_params=PARAMS,
+        cost_estimate=COST,
+        name="last_product",
+    )(flags, *operands, sums)
+
+
+def turn_kernel(flags, first, second, first_turned, second_turned):
+    first_turned[0] = first[0].T
+    second_turned[0] = second[0].T
+
+
+def turned_parts(flags, densities):
+    k_count, n_rows, both = densities.shape
+    quarter = n_rows // 4
+    turned = jax.ShapeDtypeStruct((k_count, both, quarter), densities.dtype)
+
+    def part(which):
+        return pl.BlockSpec((1, quarter, both), lambda k, flags: (k, flags[which], 0))
+
+    out = pl.BlockSpec((1, both, quarter), lambda k, flags: (k, 0, 0))
+    return pl.pallas_call(
+        turn_kernel,
+        out_shape=(turned, turned),
+        grid_spec=pltpu.PrefetchScalarGridSpec(
+            num_scalar_prefetch=1, grid=(k_count,), in_specs=[part(6), part(7)], out_specs=[out, out]
+        ),
+        compiler_params=PARAMS,
+        cost_estimate=COST,
+        name="turned_parts",
+    )(flags, densities, densities)
+
+
+def body(densities, screened, partner, pair_order):
+    k_count, n_rows, both = densities.shape
+    pair_count = both // 2
+    quarter = n_rows // 4
+    panel = screened.shape[2]
+    widths = (panel // 4, 5 * panel // 12, panel // 4, panel // 12)
+    firsts = [sum(widths[:n]) for n in range(4)]
+    k_owner = lax.axis_index("ka")
+    c = lax.axis_index("ga")
+    z, b = k_owner // 4, k_owner % 4
+    half, odd = z // 2, z % 2
+    offset = partner[0] % k_count
+    ends = (z == 0) | (z == 3)
+    flags = jnp.stack([b, c == odd, half, offset, ends, c, 2 * (1 - odd) + c, 2 * odd + c]).astype(jnp.int32)
+    rows = screened.shape[1]
+
+    part = (k_count, both, quarter)
+
+    def own_pieces(n, when, at=0):
+        first, width = firsts[n], widths[n]
+        return [
+            (when, screened, real(first, width), columns_of(at, width)),
+            (when, screened, imaginary(first, width), columns_of(at + width, width)),
+        ]
+
+    def far_part(*numbers):
+        pieces, at = [], 0
+        for n in numbers:
+            pieces += own_pieces(n, own_far, at)
+            at += 2 * widths[n]
+        return (rows, at), pieces
+
+    def sent_far(value):
+        return moved(value, lambda z, b, c: (z ^ 1, b, 1 - c) if c != z % 2 else None)
+
+    def panel_parts(n, arrived, at=0, before=None):
+        pieces = own_pieces(n, own_near) + [(own_far, arrived, columns_of(at, 2 * widths[n]), columns_of(0, 2 * widths[n]))]
+        if before is None:
+            return (((rows, 2 * widths[n]), pieces),)
+        x_side, y_side = before
+        passed = widths[n - 1]
+        shape, place = (rows, 2 * widths[n] + passed), columns_of(2 * widths[n], passed)
+        return (
+            (shape, pieces + [(always, y_side, columns_of(passed, passed), place)]),
+            (shape, pieces + [(always, x_side, columns_of(0, passed), place)]),
+        )
+
+    def end_or_mid(end, mid):
+        return part, [(at_end, end, whole, whole), (at_mid, mid, whole, whole)]
+
+    flags, sent_0, sent_1 = moves(flags, (), far_part(0), far_part(1))
+    arrived_0, arrived_1 = sent_far(sent_0), sent_far(sent_1)
+    own_first, own_second = turned_parts(flags, densities)
+    pair_a, mid_a = end_with_mid(own_first), mid_with_mid(own_second)
+    swapped_0 = other_core(own_second)
+
+    flags, panel_0 = moves(flags, (swapped_0,), *panel_parts(0, arrived_0))
+    x_0, y_0 = along_x(panel_0), along_y(panel_0)
+
+    flags, to_x, to_y, sent_2, to_mid = moves(
+        flags,
+        (mid_a,),
+        *panel_parts(1, arrived_1, 0, (x_0, y_0)),
+        far_part(2, 3),
+        (part, [(always, own_first, whole, whole)]),
+    )
+    x_1, y_1 = along_x(to_x), along_y(to_y)
+    panel_1 = to_x
+    arrived_2 = sent_far(sent_2)
+    mid_d = mid_with_mid(to_mid)
+
+    flags, to_pair, pair_a = moves(flags, (), end_or_mid(own_second, mid_a), passing=(pair_a,))
+    pair_b = end_with_mid(to_pair)
+
+    flags, to_mid = moves(flags, (mid_d,), (part, [(always, pair_a, whole, whole)]))
+    mid_b = mid_with_mid(to_mid)
+
+    flags, to_x, to_y, pair_a = moves(flags, (), *panel_parts(2, arrived_2, 0, (x_1, y_1)), passing=(pair_a,))
+    x_2, y_2 = along_x(to_x), along_y(to_y)
+    panel_2 = to_x
+    swapped_a = other_core(pair_a)
+    chunk_0 = (firsts[0], widths[0], (panel_0, x_0, y_0, y_1, x_1), (widths[0], 2 * widths[1], 2 * widths[1]))
+    of_end, of_mid = [own_second, pair_a, None, None], [own_first, mid_a, None, None]
+    left, flags = first_product(flags, [chunk_0], 0, 2, of_end, of_mid, None, panel)
+
+    flags, pair_b, mid_b = moves(flags, (), passing=(pair_b, mid_b))
+    of_end[2], of_mid[2], of_mid[3] = pair_b, mid_b, pair_b
+    pair_c, mid_c = mid_to_end(mid_b), mid_with_mid(pair_b)
+    left, flags = first_product(flags, [chunk_0], 2, 1, of_end, of_mid, left, panel)
+
+    flags, to_x, to_y = moves(flags, (swapped_a,), *panel_parts(3, arrived_2, 2 * widths[2], (x_2, y_2)))
+    x_3, y_3 = along_x(to_x), along_y(to_y)
+    panel_3 = to_x
+    chunk_1 = (firsts[1], widths[1], (panel_1, x_1, y_1, y_2, x_2), (widths[1], 2 * widths[2], 2 * widths[2]))
+    left, flags = first_product(flags, [chunk_1], 0, 3, of_end, of_mid, left, panel)
+
+    flags, carried_2, carried_3 = moves(flags, (), end_or_mid(pair_b, mid_c), end_or_mid(pair_c, mid_d))
+    swapped_2, swapped_3 = other_core(carried_2), other_core(carried_3)
+    of_end[3] = pair_c
+    left, flags = first_product(flags, [chunk_0, chunk_1], 3, 1, of_end, of_mid, left, panel)
+
+    shape = (rows, widths[3])
+    flags, to_x, to_y = moves(
+        flags,
+        (),
+        (shape, [(always, y_3, columns_of(widths[3], widths[3]), whole)]),
+        (shape, [(always, x_3, columns_of(0, widths[3]), whole)]),
+    )
+    x_4, y_4 = along_x(to_x), along_y(to_y)
+    chunk_2 = (firsts[2], widths[2], (panel_2, x_2, y_2, y_3, x_3), (widths[2], 2 * widths[3], 2 * widths[3]))
+    left, flags = first_product(flags, [chunk_2], 0, 4, of_end, of_mid, left, panel)
+    matched = [own_second, swapped_0, carried_2, swapped_2, pair_a, swapped_a, carried_3, swapped_3]
+    sums, flags = second_product(flags, left, matched, 0, firsts[3])
+    last = (firsts[3], widths[3], (panel_3, x_3, y_3, y_4, x_4), (widths[3], 0, 0))
+    blocks = last_product(flags, last, of_end, of_mid, matched, sums)
+
+    blocks = blocks + other_core(blocks)
+    total = blocks[0]
+    for shift in (1, 2, 3):
+        sent = jnp.where(half == 0, blocks[shift], blocks[4 - shift])
+        total = total + moved(sent, lambda z, b, c: ((z + shift) % 4, b, c))
+    order_table = (jnp.arange(pair_count)[:, None] == pair_order[None, :]).astype(jnp.float32)
+    direct = reorder(total[:, :, :pair_count], total[:, :, pair_count:], order_table)
+    received = moved(direct, lambda z, b, c: ((z + 1) % 4, b, c))
+    sources = (jnp.arange(k_count) - offset) % k_count
+    mirror = conjugate_side(jnp.take(received, sources, axis=0), pair_count)
+    return (direct, mirror)
+
+
 def solution(mesh):
     in_specs = (P("ka", None, None), P(None, "ka", "ga"), P(), P())
     out_specs = (P("ka", None, None), P("ka", None, None))
-    return jax.shard_map(body, mesh=mesh, in_specs=in_specs, out_specs=out_specs, check_vma=False)
+    planes = mesh.shape["ka"] == 16 and mesh.shape["ga"] == 2
+    chosen = body if planes else general_body
+    return jax.shard_map(chosen, mesh=mesh, in_specs=in_specs, out_specs=out_specs, check_vma=False)

time: 908 us -> 311 us (0.34)
  waiting for transfers between devices: 819 us -> 83.9 us
  Pallas kernels: 0 us -> 142 us
  starting transfers between devices: 6.97 us -> 65.9 us
  matrix products: 54.6 us -> 0.46 us
  between operations: 14.2 us -> 3.15 us
    all_gather x1 -> x0, waiting for transfers between devices: 631 us -> none  [body(): lax.all_gather(screened, 'ka', axis=1, tiled=True)]
    pallas_call x0 -> x18, Pallas kernels: none -> 142 us  [the longest x5 73.4 us: first_product(): pl.pallas_call(functools.partial(first_kernel, first_slot=first_slot, n_s...]
    ppermute x2 -> x29, waiting for transfers between devices: 171 us -> 83.9 us  [moved(): return lax.ppermute(value, AXES, pairs)]
    ppermute x2 -> x29, starting transfers between devices: 6.9 us -> 65.9 us  [moved(): return lax.ppermute(value, AXES, pairs)]
    dot_general x4 -> x2, matrix products: 54.6 us -> 0.46 us  [the longest x1 0.26 us: reorder(): jnp.einsum('kpq,qj->kpj', block_im, order_table, precision=lax.Precision....]
    psum x1 -> x0, waiting for transfers between devices: 16.6 us -> none  [body(): summed = lax.psum(partial_value, 'ga')]
    unnamed x7 -> x31, local copies, waits for them, and re-layouts: 0.79 us -> 11.5 us
  transfers between devices with their start and end apart: 4 -> 29, of which waited for: 4 -> 7; matrix products, arithmetic and copies ran while one was open for 1% -> 0% of each run, Pallas kernels for 0% -> 39%
where the time goes in v2:
time: 311 us; the launch traced here: 310 us
  Pallas kernels  142 us (46%)
  waiting for transfers between devices  83.9 us (27%)
  starting transfers between devices  65.9 us (21%)
  local copies, waits for them, and re-layouts  12.7 us (4%)
  between operations  3.15 us (1%)
    ppermute x29, waiting for transfers between devices, moved(): return lax.ppermute(value, AXES, pairs)  83.9 us
    pallas_call x5, Pallas kernels, first_product(): pl.pallas_call(functools.partial(first_kernel, first_slot=first_slot, n_s...  73.4 us
    ppermute x29, starting transfers between devices, moved(): return lax.ppermute(value, AXES, pairs)  65.9 us
    pallas_call x10, Pallas kernels, moves(): pl.pallas_call(functools.partial(moves_kernel, plan=tuple(plan), n_source...  37 us
    pallas_call x1, Pallas kernels, second_product(): pl.pallas_call(functools.partial(second_kernel, base=base, width=width),...  15.3 us
    pallas_call x1, Pallas kernels, last_product(): pl.pallas_call(functools.partial(last_kernel, n_slots=n_slots, base=base,...  11.6 us
    unnamed x31, local copies, waits for them, and re-layouts  11.5 us
  transfers between devices with their start and end apart: 29, of which 7 were waited for; matrix products, arithmetic and copies ran while one was open for 0% of the time, Pallas kernels for 39%

profile of v2, /device:TPU:0, one launch (start us, length us, event | category | flops | bytes accessed | tf_op | source)
XLA Modules:
  0.0 310.0 jit_solution(4269482654722302094)
XLA Ops:
  4.6 5.1 %turned_parts.1 = (bf16[4,128,1536]{2,1,0:T(8,128)(2,1)}, bf16[4,128,1536]{2,1,0:T(8,128)(2,1)}) custom-call(s32[8]{0:T(128)} %get-tuple-element.47.flags, bf16[4,6144,128]{2,1,0:T(8,128)(2,1)} %second.1, bf16[4,6144,128]{2,1,0:T(8,128)(2,1)} %second.1), custom_call_target="tpu_custom_call" | custom-call | flops 1000 | bytes 1000 | tf_op jit(solution)/shard_map/turned_parts/pallas_call | solution.py:514
  9.7 3.3 %collective-permute-start.1 = (bf16[4,128,1536]{2,1,0:T(8,128)(2,1)}, bf16[4,128,1536]{2,1,0:T(8,128)(2,1)S(1)}, u32[]{:S(2)}, u32[]{:S(2)}) collective-permute-start(bf16[4,128,1536]{2,1,0:T(8,128)(2,1)} %get-tuple-element.49.refs_0_.refs_5_.refs_13_), channel_id=1, source_target_pairs={{0,1},{1,0},{2,3},{3,2},{4,5},{5,4},{6,7},{7,6},{8,9},{9,8},{10,11... | collective-permute-start | bytes 4718600 | tf_op jit(solution)/shard_map/ppermute | solution.py:89
  14.7 1.9 collective-permute-start.2
  18.6 3.3 %moves.11 = (bf16[384,1536]{1,0:T(8,128)(2,1)}, s32[8]{0:T(128)}) custom-call(s32[8]{0:T(128)} %get-tuple-element.47.flags, bf16[2,384,3072]{2,1,0:T(8,128)(2,1)} %refs_5_.5, bf16[2,384,3072]{2,1,0:T(8,128)(2,1)} %refs_5_.5, bf16[384,1536]{1,0:T(8,128)(2,1)} %collective-permute-done.refs_2_, bf16[4,128,1536]{2,1,0:T(8,128)(2,1)} %copy-done.5), custom_call_target="tpu_custom_call" | custom-call | flops 1000 | bytes 1000 | tf_op jit(solution)/shard_map/moves/pallas_call | solution.py:205
  21.9 2.4 collective-permute-start.3
  25.8 15.4 %collective-permute-start.6 = (bf16[4,128,1536]{2,1,0:T(8,128)(2,1)}, bf16[4,128,1536]{2,1,0:T(8,128)(2,1)S(1)}, u32[]{:S(2)}, u32[]{:S(2)}) collective-permute-start(bf16[4,128,1536]{2,1,0:T(8,128)(2,1)} %get-tuple-element.53.refs_12_.refs_7_.refs_8_.refs_9_), channel_id=1, source_target_pairs={{0,8},{1,9},{2,10},{3,11},{4,12},{5,13},{6,14},{7,15},{8,0},{9,1},... | collective-permute-start | bytes 4718600 | tf_op jit(solution)/shard_map/ppermute | solution.py:89
  42.4 7.4 %moves.12 = (bf16[384,3328]{1,0:T(8,128)(2,1)}, bf16[384,3328]{1,0:T(8,128)(2,1)}, bf16[384,2048]{1,0:T(8,128)(2,1)}, bf16[4,128,1536]{2,1,0:T(8,128)(2,1)}, s32[8]{0:T(128)}) custom-call(s32[8]{0:T(128)} %get-tuple-element.50.flags, bf16[2,384,3072]{2,1,0:T(8,128)(2,1)} %refs_5_.5, bf16[2,384,3072]{2,1,0:T(8,128)(2,1)} %refs_5_.5, ...), custom_call_target="tpu_custom_call" | custom-call | flops 1000 | bytes 1000 | tf_op jit(solution)/shard_map/moves/pallas_call | solution.py:205
  53.5 33.1 %collective-permute-done.6.refs_2_ = bf16[4,128,1536]{2,1,0:T(8,128)(2,1)S(1)} collective-permute-done((bf16[4,128,1536]{2,1,0:T(8,128)(2,1)}, bf16[4,128,1536]{2,1,0:T(8,128)(2,1)S(1)}, u32[]{:S(2)}, u32[]{:S(2)}) %collective-permute-start.6) | collective-permute-done | bytes 1572896 | tf_op jit(solution)/shard_map/ppermute | solution.py:89
  87.9 3.8 %moves.13 = (bf16[4,128,1536]{2,1,0:T(8,128)(2,1)}, bf16[4,128,1536]{2,1,0:T(8,128)(2,1)}, s32[8]{0:T(128)}) custom-call(s32[8]{0:T(128)} %get-tuple-element.54.flags, bf16[4,128,1536]{2,1,0:T(8,128)(2,1)} %get-tuple-element.49.refs_0_.refs_5_.refs_13_, bf16[4,128,1536]{2,1,0:T(8,128)(2,1)} %copy-done.2, ...), custom_call_target="tpu_custom_call", output_to_operand_aliasing={{1}: (3, {})} | custom-call | flops 1000 | bytes 1000 | tf_op jit(solution)/shard_map/moves/pallas_call | solution.py:205
  93.0 3.8 %moves.14 = (bf16[4,128,1536]{2,1,0:T(8,128)(2,1)}, s32[8]{0:T(128)}) custom-call(s32[8]{0:T(128)} %get-tuple-element.55.flags, bf16[4,128,1536]{2,1,0:T(8,128)(2,1)} %get-tuple-element.56.refs_0_.refs_8_, bf16[4,128,1536]{2,1,0:T(8,128)(2,1)} %copy-done.9), custom_call_target="tpu_custom_call" | custom-call | flops 1000 | bytes 1000 | tf_op jit(solution)/shard_map/moves/pallas_call | solution.py:205
  97.5 5.2 %moves.15 = (bf16[384,2816]{1,0:T(8,128)(2,1)}, bf16[384,2816]{1,0:T(8,128)(2,1)}, bf16[4,128,1536]{2,1,0:T(8,128)(2,1)}, s32[8]{0:T(128)}) custom-call(s32[8]{0:T(128)} %get-tuple-element.58.flags, bf16[2,384,3072]{2,1,0:T(8,128)(2,1)} %refs_5_.5, bf16[2,384,3072]{2,1,0:T(8,128)(2,1)} %refs_5_.5, ...), custom_call_target="tpu_custom_call", output_to_operand_aliasing={{2}: (9, {})} | custom-call | flops 1000 | bytes 1000 | tf_op jit(solution)/shard_map/moves/pallas_call | solution.py:205
  105.8 14.1 %collective-permute-start.15 = (bf16[4,128,1536]{2,1,0:T(8,128)(2,1)}, bf16[4,128,1536]{2,1,0:T(8,128)(2,1)}, u32[]{:S(2)}, u32[]{:S(2)}) collective-permute-start(bf16[4,128,1536]{2,1,0:T(8,128)(2,1)} %get-tuple-element.63.refs_6_.refs_4_.refs_17_), channel_id=1, source_target_pairs={{0,1},{1,0},{2,3},{3,2},{4,5},{5,4},{6,7},{7,6},{8,9},{9,8},{10,11... | collective-permute-start | bytes 4718600 | tf_op jit(solution)/shard_map/ppermute | solution.py:89
  119.8 11.1 %first_product.5 = (f32[4,4,128,3072]{3,2,1,0:T(8,128)}, s32[8]{0:T(128)}) custom-call(s32[8]{0:T(128)} %get-tuple-element.62.flags, bf16[384,1536]{1,0:T(8,128)(2,1)} %get-tuple-element.52.refs_0_, bf16[384,1536]{1,0:T(8,128)(2,1)} %collective-permute-done.4.refs_7_.refs_1_, bf16[384,1536]{1,0:T(8,128)(2,1)} %collective-permute-done.3.refs_3_.refs_2_, ...), custom_call_target="tpu_custom_call" | custom-call | flops 1000 | bytes 1000 | tf_op jit(solution)/shard_map/first_product/pallas_call | solution.py:367
  130.9 6.3 %collective-permute-done.11.refs_0_ = bf16[4,128,1536]{2,1,0:T(8,128)(2,1)S(1)} collective-permute-done((bf16[4,128,1536]{2,1,0:T(8,128)(2,1)}, bf16[4,128,1536]{2,1,0:T(8,128)(2,1)S(1)}, u32[]{:S(2)}, u32[]{:S(2)}) %collective-permute-start.11) | collective-permute-done | bytes 1572896 | tf_op jit(solution)/shard_map/ppermute | solution.py:89
  142.1 8.3 %first_product.6 = (f32[4,4,128,3072]{3,2,1,0:T(8,128)}, s32[8]{0:T(128)}) custom-call(s32[8]{0:T(128)} %get-tuple-element.67.flags, bf16[384,1536]{1,0:T(8,128)(2,1)} %get-tuple-element.52.refs_0_, bf16[384,1536]{1,0:T(8,128)(2,1)} %collective-permute-done.4.refs_7_.refs_1_, ...), custom_call_target="tpu_custom_call", output_to_operand_aliasing={{0}: (8, {})} | custom-call | flops 1000 | bytes 1000 | tf_op jit(solution)/shard_map/first_product/pallas_call | solution.py:367
  150.4 3.8 %moves.17 = (bf16[384,1280]{1,0:T(8,128)(2,1)}, bf16[384,1280]{1,0:T(8,128)(2,1)}, s32[8]{0:T(128)}) custom-call(s32[8]{0:T(128)} %get-tuple-element.71.flags, bf16[2,384,3072]{2,1,0:T(8,128)(2,1)} %refs_5_.5, bf16[2,384,3072]{2,1,0:T(8,128)(2,1)} %refs_5_.5, bf16[384,2048]{1,0:T(8,128)(2,1)} %collective-permute-done.8.refs_2_.refs_6_, ...), custom_call_target="tpu_custom_call" | custom-call | flops 1000 | bytes 1000 | tf_op jit(solution)/shard_map/moves/pallas_call | solution.py:205
  154.3 21.2 %first_product.7 = (f32[4,4,128,3072]{3,2,1,0:T(8,128)}, s32[8]{0:T(128)}) custom-call(s32[8]{0:T(128)} %get-tuple-element.74.flags, bf16[384,3328]{1,0:T(8,128)(2,1)} %get-tuple-element.61.refs_0_.refs_5_, bf16[384,3328]{1,0:T(8,128)(2,1)} %collective-permute-done.10.refs_7_.refs_4_.refs_1_.refs_6_, ...), custom_call_target="tpu_custom_call", output_to_operand_aliasing={{0}: (12, {})} | custom-call | flops 1000 | bytes 1000 | tf_op jit(solution)/shard_map/first_product/pallas_call | solution.py:367
  175.5 24.1 %collective-permute-done.17.refs_2_.refs_10_.refs_8_ = bf16[4,128,1536]{2,1,0:T(8,128)(2,1)S(1)} collective-permute-done((bf16[4,128,1536]{2,1,0:T(8,128)(2,1)}, bf16[4,128,1536]{2,1,0:T(8,128)(2,1)S(1)}, u32[]{:S(2)}, u32[]{:S(2)}) %collective-permute-start.17) | collective-permute-done | bytes 1572896 | tf_op jit(solution)/shard_map/ppermute | solution.py:89
  200.8 4.3 %moves.18 = (bf16[4,128,1536]{2,1,0:T(8,128)(2,1)}, bf16[4,128,1536]{2,1,0:T(8,128)(2,1)}, s32[8]{0:T(128)}) custom-call(s32[8]{0:T(128)} %get-tuple-element.76.flags, bf16[4,128,1536]{2,1,0:T(8,128)(2,1)} %get-tuple-element.68.refs_5_.refs_7_.refs_0_.refs_11_.refs_12_, bf16[4,128,1536]{2,1,0:T(8,128)(2,1)} %copy-done.10, bf16[4,128,1536]{2,1,0:T(8,128)(2,1)} %copy-done.4, ...), custom_call_target="tpu_custom_call" | custom-call | flops 1000 | bytes 1000 | tf_op jit(solution)/shard_map/moves/pallas_call | solution.py:205
  206.2 16.1 %first_product.8 = (f32[4,4,128,3072]{3,2,1,0:T(8,128)}, s32[8]{0:T(128)}) custom-call(s32[8]{0:T(128)} %get-tuple-element.77.flags, bf16[384,1536]{1,0:T(8,128)(2,1)} %get-tuple-element.52.refs_0_, bf16[384,1536]{1,0:T(8,128)(2,1)} %collective-permute-done.4.refs_7_.refs_1_, ...), custom_call_target="tpu_custom_call", output_to_operand_aliasing={{0}: (13, {})} | custom-call | flops 1000 | bytes 1000 | tf_op jit(solution)/shard_map/first_product/pallas_call | solution.py:367
  222.2 7.4 %collective-permute-done.18.refs_0_.refs_3_.refs_2_ = bf16[384,1280]{1,0:T(8,128)(2,1)S(1)} collective-permute-done((bf16[384,1280]{1,0:T(8,128)(2,1)}, bf16[384,1280]{1,0:T(8,128)(2,1)S(1)}, u32[]{:S(2)}, u32[]{:S(2)}) %collective-permute-start.18) | collective-permute-done | bytes 983072 | tf_op jit(solution)/shard_map/ppermute | solution.py:89
  230.9 2.9 moves.19
  235.6 16.8 %first_product.9 = (f32[4,4,128,3072]{3,2,1,0:T(8,128)}, s32[8]{0:T(128)}) custom-call(s32[8]{0:T(128)} %get-tuple-element.82.flags, bf16[384,2816]{1,0:T(8,128)(2,1)} %get-tuple-element.73.refs_0_, bf16[384,2816]{1,0:T(8,128)(2,1)} %collective-permute-done.14.refs_7_.refs_4_.refs_9_.refs_1_, ...), custom_call_target="tpu_custom_call", output_to_operand_aliasing={{0}: (14, {})} | custom-call | flops 1000 | bytes 1000 | tf_op jit(solution)/shard_map/first_product/pallas_call | solution.py:367
  253.6 15.3 %second_product.1 = (f32[4,4,128,128]{3,2,1,0:T(8,128)}, s32[8]{0:T(128)}) custom-call(s32[8]{0:T(128)} %get-tuple-element.84.flags, f32[4,4,128,3072]{3,2,1,0:T(8,128)} %get-tuple-element.85.left, bf16[4,128,1536]{2,1,0:T(8,128)(2,1)} %get-tuple-element.49.refs_0_.refs_5_.refs_13_, bf16[4,128,1536]{2,1,0:T(8,128)(2,1)} %copy-done.5, ...), custom_call_target="tpu_custom_call" | custom-call | flops 1000 | bytes 1000 | tf_op jit(solution)/shard_map/second_product/pallas_call | solution.py:427
  269.7 11.6 %last_product.1 = f32[4,4,64,128]{3,2,1,0:T(8,128)} custom-call(s32[8]{0:T(128)} %get-tuple-element.88.flags, bf16[384,1280]{1,0:T(8,128)(2,1)} %get-tuple-element.81.refs_0_, bf16[384,1280]{1,0:T(8,128)(2,1)} %copy-done.7, bf16[384,1280]{1,0:T(8,128)(2,1)} %copy-done.6, bf16[384,256]{1,0:T(8,128)(2,1)} %copy-done.11, bf16[384,256]{1,0:T(8,128)(2,1)} %copy-done.12, ...), custom_call_target="tpu_custom_call" | custom-call | flops 1000 | bytes 1000 | tf_op jit(solution)/shard_map/last_product/pallas_call | solution.py:481
  281.4 2.1 collective-permute-done.24
  284.6 3.2 %collective-permute-start.25 = (f32[4,64,128]{2,1,0:T(8,128)S(1)}, f32[4,64,128]{2,1,0:T(8,128)S(1)}, u32[]{:S(2)}, u32[]{:S(2)}) collective-permute-start(f32[4,64,128]{2,1,0:T(8,128)S(1)} %get-tuple-element.94), channel_id=1, source_target_pairs={{0,8},{1,9},{2,10},{3,11},{4,12},{5,13},{6,14},{7,15},{8,16},{9,17... | collective-permute-start | bytes 393224 | tf_op jit(solution)/shard_map/ppermute | solution.py:89
  287.8 2.2 collective-permute-start.26
  290.0 2.8 collective-permute-start.27
  292.8 5.1 %collective-permute-done.26 = f32[4,64,128]{2,1,0:T(8,128)S(1)} collective-permute-done((f32[4,64,128]{2,1,0:T(8,128)S(1)}, f32[4,64,128]{2,1,0:T(8,128)S(1)}, u32[]{:S(2)}, u32[]{:S(2)}) %collective-permute-start.26) | collective-permute-done | bytes 131104 | tf_op jit(solution)/shard_map/ppermute | solution.py:89
  298.5 4.1 %collective-permute-start.28 = (f32[4,64,128]{2,1,0:T(8,128)S(1)}, f32[4,64,128]{2,1,0:T(8,128)S(1)}, u32[]{:S(2)}, u32[]{:S(2)}) collective-permute-start(f32[4,64,128]{2,1,0:T(8,128)S(1)} %pad_maximum_fusion.1), channel_id=1, source_target_pairs={{0,8},{1,9},{2,10},{3,11},{4,12},{5,13},{6,14},{7,15},{8,16},{9,17... | collective-permute-start | bytes 393224 | tf_op jit(solution)/shard_map/ppermute | solution.py:89
  302.7 5.8 %collective-permute-done.28 = f32[4,64,128]{2,1,0:T(8,128)S(1)} collective-permute-done((f32[4,64,128]{2,1,0:T(8,128)S(1)}, f32[4,64,128]{2,1,0:T(8,128)S(1)}, u32[]{:S(2)}, u32[]{:S(2)}) %collective-permute-start.28) | collective-permute-done | bytes 131104 | tf_op jit(solution)/shard_map/ppermute | solution.py:89
  (89 shorter events, 33.7 us)
Async XLA Ops:
  9.7 7.7 %collective-permute-start.1 = (bf16[4,128,1536]{2,1,0:T(8,128)(2,1)}, bf16[4,128,1536]{2,1,0:T(8,128)(2,1)S(1)}, u32[]{:S(2)}, u32[]{:S(2)}) collective-permute-start(bf16[4,128,1536]{2,1,0:T(8,128)(2,1)} %get-tuple-element.49.refs_0_.refs_5_.refs_13_), channel_id=1, source_target_pairs={{0,1},{1,0},{2,3},{3,2},{4,5},{5,4},{6,7},{7,6},{8,9},{9,8},{10,11... | collective-permute-start | bytes 4718600 | tf_op jit(solution)/shard_map/ppermute | solution.py:89
  13.0 4.4 %collective-permute-start = (bf16[384,1536]{1,0:T(8,128)(2,1)}, bf16[384,1536]{1,0:T(8,128)(2,1)}, u32[]{:S(2)}, u32[]{:S(2)}) collective-permute-start(bf16[384,1536]{1,0:T(8,128)(2,1)} %get-tuple-element.48), channel_id=1, source_target_pairs={{1,8},{3,10},{5,12},{7,14},{8,1},{10,3},{12,5},{14,7},{17,24},{19,... | collective-permute-start | bytes 3538952 | tf_op jit(solution)/shard_map/ppermute | solution.py:89
  14.7 26.5 %collective-permute-start.2 = (bf16[384,2560]{1,0:T(8,128)(2,1)}, bf16[384,2560]{1,0:T(8,128)(2,1)}, u32[]{:S(2)}, u32[]{:S(2)}) collective-permute-start(bf16[384,2560]{1,0:T(8,128)(2,1)} %get-tuple-element.51), channel_id=1, source_target_pairs={{1,8},{3,10},{5,12},{7,14},{8,1},{10,3},{12,5},{14,7},{17,24},{19,... | collective-permute-start | bytes 5898248 | tf_op jit(solution)/shard_map/ppermute | solution.py:89
  16.6 24.6 %collective-permute-start.5 = (bf16[4,128,1536]{2,1,0:T(8,128)(2,1)}, bf16[4,128,1536]{2,1,0:T(8,128)(2,1)S(1)}, u32[]{:S(2)}, u32[]{:S(2)}) collective-permute-start(bf16[4,128,1536]{2,1,0:T(8,128)(2,1)} %get-tuple-element.49.refs_0_.refs_5_.refs_13_), channel_id=1, source_target_pairs={{8,16},{9,17},{10,18},{11,19},{12,20},{13,21},{14,22},{15,23},{16,... | collective-permute-start | bytes 4718600 | tf_op jit(solution)/shard_map/ppermute | solution.py:89
  21.9 19.3 %collective-permute-start.3 = (bf16[384,1536]{1,0:T(8,128)(2,1)}, bf16[384,1536]{1,0:T(8,128)(2,1)}, u32[]{:S(2)}, u32[]{:S(2)}) collective-permute-start(bf16[384,1536]{1,0:T(8,128)(2,1)} %get-tuple-element.52.refs_0_), channel_id=1, source_target_pairs={{0,4},{1,5},{2,6},{3,7},{4,0},{5,1},{6,2},{7,3},{8,12},{9,13},{10,... | collective-permute-start | bytes 3538952 | tf_op jit(solution)/shard_map/ppermute | solution.py:89
  24.3 16.9 %collective-permute-start.4 = (bf16[384,1536]{1,0:T(8,128)(2,1)}, bf16[384,1536]{1,0:T(8,128)(2,1)}, u32[]{:S(2)}, u32[]{:S(2)}) collective-permute-start(bf16[384,1536]{1,0:T(8,128)(2,1)} %get-tuple-element.52.refs_0_), channel_id=1, source_target_pairs={{0,2},{1,3},{2,0},{3,1},{4,6},{5,7},{6,4},{7,5},{8,10},{9,11},{10,... | collective-permute-start | bytes 3538952 | tf_op jit(solution)/shard_map/ppermute | solution.py:89
  25.8 60.8 %collective-permute-start.6 = (bf16[4,128,1536]{2,1,0:T(8,128)(2,1)}, bf16[4,128,1536]{2,1,0:T(8,128)(2,1)S(1)}, u32[]{:S(2)}, u32[]{:S(2)}) collective-permute-start(bf16[4,128,1536]{2,1,0:T(8,128)(2,1)} %get-tuple-element.53.refs_12_.refs_7_.refs_8_.refs_9_), channel_id=1, source_target_pairs={{0,8},{1,9},{2,10},{3,11},{4,12},{5,13},{6,14},{7,15},{8,0},{9,1},... | collective-permute-start | bytes 4718600 | tf_op jit(solution)/shard_map/ppermute | solution.py:89
  49.8 47.7 %collective-permute-start.10 = (bf16[384,3328]{1,0:T(8,128)(2,1)}, bf16[384,3328]{1,0:T(8,128)(2,1)}, u32[]{:S(2)}, u32[]{:S(2)}) collective-permute-start(bf16[384,3328]{1,0:T(8,128)(2,1)} %get-tuple-element.61.refs_0_.refs_5_), channel_id=1, source_target_pairs={{0,2},{1,3},{2,0},{3,1},{4,6},{5,7},{6,4},{7,5},{8,10},{9,11},{10,... | collective-permute-start | bytes 7667720 | tf_op jit(solution)/shard_map/ppermute | solution.py:89
  50.4 47.2 %collective-permute-start.9 = (bf16[384,3328]{1,0:T(8,128)(2,1)}, bf16[384,3328]{1,0:T(8,128)(2,1)}, u32[]{:S(2)}, u32[]{:S(2)}) collective-permute-start(bf16[384,3328]{1,0:T(8,128)(2,1)} %get-tuple-element.60), channel_id=1, source_target_pairs={{0,4},{1,5},{2,6},{3,7},{4,0},{5,1},{6,2},{7,3},{8,12},{9,13},{10,... | collective-permute-start | bytes 7667720 | tf_op jit(solution)/shard_map/ppermute | solution.py:89
  50.9 40.9 %collective-permute-start.7 = (bf16[4,128,1536]{2,1,0:T(8,128)(2,1)}, bf16[4,128,1536]{2,1,0:T(8,128)(2,1)S(1)}, u32[]{:S(2)}, u32[]{:S(2)}) collective-permute-start(bf16[4,128,1536]{2,1,0:T(8,128)(2,1)} %get-tuple-element.57), channel_id=1, source_target_pairs={{8,16},{9,17},{10,18},{11,19},{12,20},{13,21},{14,22},{15,23},{16,... | collective-permute-start | bytes 4718600 | tf_op jit(solution)/shard_map/ppermute | solution.py:89
  51.6 45.9 %collective-permute-start.8 = (bf16[384,2048]{1,0:T(8,128)(2,1)}, bf16[384,2048]{1,0:T(8,128)(2,1)}, u32[]{:S(2)}, u32[]{:S(2)}) collective-permute-start(bf16[384,2048]{1,0:T(8,128)(2,1)} %get-tuple-element.59), channel_id=1, source_target_pairs={{1,8},{3,10},{5,12},{7,14},{8,1},{10,3},{12,5},{14,7},{17,24},{19,... | collective-permute-start | bytes 4718600 | tf_op jit(solution)/shard_map/ppermute | solution.py:89
  91.7 45.5 %collective-permute-start.11 = (bf16[4,128,1536]{2,1,0:T(8,128)(2,1)}, bf16[4,128,1536]{2,1,0:T(8,128)(2,1)S(1)}, u32[]{:S(2)}, u32[]{:S(2)}) collective-permute-start(bf16[4,128,1536]{2,1,0:T(8,128)(2,1)} %get-tuple-element.65), channel_id=1, source_target_pairs={{0,8},{1,9},{2,10},{3,11},{4,12},{5,13},{6,14},{7,15},{8,0},{9,1},... | collective-permute-start | bytes 4718600 | tf_op jit(solution)/shard_map/ppermute | solution.py:89
  96.7 40.5 %collective-permute-start.12 = (bf16[4,128,1536]{2,1,0:T(8,128)(2,1)}, bf16[4,128,1536]{2,1,0:T(8,128)(2,1)S(1)}, u32[]{:S(2)}, u32[]{:S(2)}) collective-permute-start(bf16[4,128,1536]{2,1,0:T(8,128)(2,1)} %get-tuple-element.66), channel_id=1, source_target_pairs={{8,16},{9,17},{10,18},{11,19},{12,20},{13,21},{14,22},{15,23},{16,... | collective-permute-start | bytes 4718600 | tf_op jit(solution)/shard_map/ppermute | solution.py:89
  102.7 47.7 %collective-permute-start.13 = (bf16[384,2816]{1,0:T(8,128)(2,1)}, bf16[384,2816]{1,0:T(8,128)(2,1)}, u32[]{:S(2)}, u32[]{:S(2)}) collective-permute-start(bf16[384,2816]{1,0:T(8,128)(2,1)} %get-tuple-element.72), channel_id=1, source_target_pairs={{0,4},{1,5},{2,6},{3,7},{4,0},{5,1},{6,2},{7,3},{8,12},{9,13},{10,... | collective-permute-start | bytes 6488072 | tf_op jit(solution)/shard_map/ppermute | solution.py:89
  104.3 46.1 %collective-permute-start.14 = (bf16[384,2816]{1,0:T(8,128)(2,1)}, bf16[384,2816]{1,0:T(8,128)(2,1)}, u32[]{:S(2)}, u32[]{:S(2)}) collective-permute-start(bf16[384,2816]{1,0:T(8,128)(2,1)} %get-tuple-element.73.refs_0_), channel_id=1, source_target_pairs={{0,2},{1,3},{2,0},{3,1},{4,6},{5,7},{6,4},{7,5},{8,10},{9,11},{10,... | collective-permute-start | bytes 6488072 | tf_op jit(solution)/shard_map/ppermute | solution.py:89
  105.8 44.6 %collective-permute-start.15 = (bf16[4,128,1536]{2,1,0:T(8,128)(2,1)}, bf16[4,128,1536]{2,1,0:T(8,128)(2,1)}, u32[]{:S(2)}, u32[]{:S(2)}) collective-permute-start(bf16[4,128,1536]{2,1,0:T(8,128)(2,1)} %get-tuple-element.63.refs_6_.refs_4_.refs_17_), channel_id=1, source_target_pairs={{0,1},{1,0},{2,3},{3,2},{4,5},{5,4},{6,7},{7,6},{8,9},{9,8},{10,11... | collective-permute-start | bytes 4718600 | tf_op jit(solution)/shard_map/ppermute | solution.py:89
  140.0 35.4 %collective-permute-start.16 = (bf16[4,128,1536]{2,1,0:T(8,128)(2,1)}, bf16[4,128,1536]{2,1,0:T(8,128)(2,1)S(1)}, u32[]{:S(2)}, u32[]{:S(2)}) collective-permute-start(bf16[4,128,1536]{2,1,0:T(8,128)(2,1)} %get-tuple-element.68.refs_5_.refs_7_.refs_0_.refs_11_.refs_12_), channel_id=1, source_target_pairs={{8,16},{9,17},{10,18},{11,19},{12,20},{13,21},{14,22},{15,23},{16,... | collective-permute-start | bytes 4718600 | tf_op jit(solution)/shard_map/ppermute | solution.py:89
  140.8 58.7 %collective-permute-start.17 = (bf16[4,128,1536]{2,1,0:T(8,128)(2,1)}, bf16[4,128,1536]{2,1,0:T(8,128)(2,1)S(1)}, u32[]{:S(2)}, u32[]{:S(2)}) collective-permute-start(bf16[4,128,1536]{2,1,0:T(8,128)(2,1)} %get-tuple-element.69.refs_6_.refs_10_.refs_11_), channel_id=1, source_target_pairs={{8,0},{9,1},{10,2},{11,3},{12,4},{13,5},{14,6},{15,7},{16,24},{17,... | collective-permute-start | bytes 4718600 | tf_op jit(solution)/shard_map/ppermute | solution.py:89
  175.4 24.1 %copy-start.10 = (bf16[4,128,1536]{2,1,0:T(8,128)(2,1)}, bf16[4,128,1536]{2,1,0:T(8,128)(2,1)S(1)}, u32[]{:S(2)}) copy-start(bf16[4,128,1536]{2,1,0:T(8,128)(2,1)S(1)} %collective-permute-done.16.refs_1_) | copy-start | bytes 4718596
  205.1 47.3 %collective-permute-start.20 = (bf16[4,128,1536]{2,1,0:T(8,128)(2,1)}, bf16[4,128,1536]{2,1,0:T(8,128)(2,1)S(1)}, u32[]{:S(2)}, u32[]{:S(2)}) collective-permute-start(bf16[4,128,1536]{2,1,0:T(8,128)(2,1)} %get-tuple-element.86.refs_2_.refs_15_), channel_id=1, source_target_pairs={{0,1},{1,0},{2,3},{3,2},{4,5},{5,4},{6,7},{7,6},{8,9},{9,8},{10,11... | collective-permute-start | bytes 4718600 | tf_op jit(solution)/shard_map/ppermute | solution.py:89
  205.2 47.3 %collective-permute-start.21 = (bf16[4,128,1536]{2,1,0:T(8,128)(2,1)}, bf16[4,128,1536]{2,1,0:T(8,128)(2,1)}, u32[]{:S(2)}, u32[]{:S(2)}) collective-permute-start(bf16[4,128,1536]{2,1,0:T(8,128)(2,1)} %get-tuple-element.87.refs_6_.refs_19_), channel_id=1, source_target_pairs={{0,1},{1,0},{2,3},{3,2},{4,5},{5,4},{6,7},{7,6},{8,9},{9,8},{10,11... | collective-permute-start | bytes 4718600 | tf_op jit(solution)/shard_map/ppermute | solution.py:89
  205.7 23.9 %collective-permute-start.18 = (bf16[384,1280]{1,0:T(8,128)(2,1)}, bf16[384,1280]{1,0:T(8,128)(2,1)S(1)}, u32[]{:S(2)}, u32[]{:S(2)}) collective-permute-start(bf16[384,1280]{1,0:T(8,128)(2,1)} %get-tuple-element.80), channel_id=1, source_target_pairs={{0,4},{1,5},{2,6},{3,7},{4,0},{5,1},{6,2},{7,3},{8,12},{9,13},{10,... | collective-permute-start | bytes 2949128 | tf_op jit(solution)/shard_map/ppermute | solution.py:89
  205.8 23.8 %collective-permute-start.19 = (bf16[384,1280]{1,0:T(8,128)(2,1)}, bf16[384,1280]{1,0:T(8,128)(2,1)S(1)}, u32[]{:S(2)}, u32[]{:S(2)}) collective-permute-start(bf16[384,1280]{1,0:T(8,128)(2,1)} %get-tuple-element.81.refs_0_), channel_id=1, source_target_pairs={{0,2},{1,3},{2,0},{3,1},{4,6},{5,7},{6,4},{7,5},{8,10},{9,11},{10,... | collective-permute-start | bytes 2949128 | tf_op jit(solution)/shard_map/ppermute | solution.py:89
  233.8 35.2 %collective-permute-start.22 = (bf16[384,256]{1,0:T(8,128)(2,1)}, bf16[384,256]{1,0:T(8,128)(2,1)S(1)}, u32[]{:S(2)}, u32[]{:S(2)}) collective-permute-start(bf16[384,256]{1,0:T(8,128)(2,1)} %get-tuple-element.89), channel_id=1, source_target_pairs={{0,4},{1,5},{2,6},{3,7},{4,0},{5,1},{6,2},{7,3},{8,12},{9,13},{10,... | collective-permute-start | bytes 589832 | tf_op jit(solution)/shard_map/ppermute | solution.py:89
  235.3 33.7 %collective-permute-start.23 = (bf16[384,256]{1,0:T(8,128)(2,1)}, bf16[384,256]{1,0:T(8,128)(2,1)S(1)}, u32[]{:S(2)}, u32[]{:S(2)}) collective-permute-start(bf16[384,256]{1,0:T(8,128)(2,1)} %get-tuple-element.90), channel_id=1, source_target_pairs={{0,2},{1,3},{2,0},{3,1},{4,6},{5,7},{6,4},{7,5},{8,10},{9,11},{10,... | collective-permute-start | bytes 589832 | tf_op jit(solution)/shard_map/ppermute | solution.py:89
  281.3 16.6 %copy-start.14 = (s32[64]{0:T(128)S(1)}, s32[64]{0:T(128)}, u32[]{:S(2)}) copy-start(s32[64]{0:T(128)} %param.7) | copy-start | bytes 772
  281.3 2.2 collective-permute-start.24
  284.6 8.2 %collective-permute-start.25 = (f32[4,64,128]{2,1,0:T(8,128)S(1)}, f32[4,64,128]{2,1,0:T(8,128)S(1)}, u32[]{:S(2)}, u32[]{:S(2)}) collective-permute-start(f32[4,64,128]{2,1,0:T(8,128)S(1)} %get-tuple-element.94), channel_id=1, source_target_pairs={{0,8},{1,9},{2,10},{3,11},{4,12},{5,13},{6,14},{7,15},{8,16},{9,17... | collective-permute-start | bytes 393224 | tf_op jit(solution)/shard_map/ppermute | solution.py:89
  287.8 10.1 %collective-permute-start.26 = (f32[4,64,128]{2,1,0:T(8,128)S(1)}, f32[4,64,128]{2,1,0:T(8,128)S(1)}, u32[]{:S(2)}, u32[]{:S(2)}) collective-permute-start(f32[4,64,128]{2,1,0:T(8,128)S(1)} %get-tuple-element.95), channel_id=1, source_target_pairs={{0,16},{1,17},{2,18},{3,19},{4,20},{5,21},{6,22},{7,23},{8,24},{9,... | collective-permute-start | bytes 393224 | tf_op jit(solution)/shard_map/ppermute | solution.py:89
  290.0 7.9 %collective-permute-start.27 = (f32[4,64,128]{2,1,0:T(8,128)S(1)}, f32[4,64,128]{2,1,0:T(8,128)S(1)}, u32[]{:S(2)}, u32[]{:S(2)}) collective-permute-start(f32[4,64,128]{2,1,0:T(8,128)S(1)} %get-tuple-element.96), channel_id=1, source_target_pairs={{0,24},{1,25},{2,26},{3,27},{4,28},{5,29},{6,30},{7,31},{8,0},{9,1... | collective-permute-start | bytes 393224 | tf_op jit(solution)/shard_map/ppermute | solution.py:89
  298.5 11.5 %copy-start.13 = (f32[4,64,128]{2,1,0:T(8,128)}, f32[4,64,128]{2,1,0:T(8,128)S(1)}, u32[]{:S(2)}) copy-start(f32[4,64,128]{2,1,0:T(8,128)S(1)} %pad_maximum_fusion.1) | copy-start | bytes 393220
  298.5 9.9 %collective-permute-start.28 = (f32[4,64,128]{2,1,0:T(8,128)S(1)}, f32[4,64,128]{2,1,0:T(8,128)S(1)}, u32[]{:S(2)}, u32[]{:S(2)}) collective-permute-start(f32[4,64,128]{2,1,0:T(8,128)S(1)} %pad_maximum_fusion.1), channel_id=1, source_target_pairs={{0,8},{1,9},{2,10},{3,11},{4,12},{5,13},{6,14},{7,15},{8,16},{9,17... | collective-permute-start | bytes 393224 | tf_op jit(solution)/shard_map/ppermute | solution.py:89
  (12 other events, 13.6 us)

commit v3 on v2

v3 whole, which is shorter than its diff:
```python
import functools

import jax
import jax.numpy as jnp
from jax import lax
from jax.experimental import pallas as pl
from jax.experimental.pallas import tpu as pltpu
from jax.sharding import PartitionSpec as P


def passed_along(value, axis, steps):
    count = lax.axis_size(axis)
    pairs = [(source, (source + steps) % count) for source in range(count)]
    return lax.ppermute(value, axis, pairs)


def conjugate_side(blocks, pair_count):
    real_half = jnp.swapaxes(blocks[:, :, :pair_count], 1, 2)
    imag_half = jnp.swapaxes(blocks[:, :, pair_count:], 1, 2)
    return jnp.concatenate([real_half, -imag_half], axis=2)


def combine_terms(partial_value, order_table, pair_count):
    block_re = partial_value[:, 0, :, :pair_count] - partial_value[:, 1, :, pair_count:]
    block_im = partial_value[:, 0, :, pair_count:] + partial_value[:, 1, :, :pair_count]
    return reorder(block_re, block_im, order_table)


def reorder(block_re, block_im, order_table):
    block_re = jnp.einsum("kpq,qj->kpj", block_re, order_table, precision=lax.Precision.HIGHEST)
    block_im = jnp.einsum("kpq,qj->kpj", block_im, order_table, precision=lax.Precision.HIGHEST)
    return jnp.concatenate([block_re, block_im], axis=2)


def finish_terms(left_sums, matched, pair_count):
    left_re = left_sums[:, 0, :pair_count] + left_sums[:, 1, pair_count:]
    left_im = left_sums[:, 1, :pair_count] - left_sums[:, 0, pair_count:]
    left_factor = jnp.stack([left_re, left_im], axis=1)
    return jnp.einsum(
        "kwpc,kcq->kwpq", left_factor, matched.astype(jnp.float32), precision=lax.Precision.HIGHEST
    )


def general_body(densities, screened, partner, pair_order):
    k_count = densities.shape[0]
    pair_count = densities.shape[2] // 2
    panel_width = screened.shape[2]
    k_owner = lax.axis_index("ka")
    column = lax.axis_index("ga")
    own_columns = lax.dynamic_slice_in_dim(densities, column * panel_width, panel_width, 1)
    arrived = passed_along(own_columns, "ka", -4)
    own_partner = lax.dynamic_slice_in_dim(partner, k_owner * k_count, k_count, 0)
    slot_index = own_partner % k_count
    offset = slot_index[0]
    matched = jnp.take(arrived, slot_index, axis=0)
    left_sums = jnp.einsum(
        "kgp,wgc->kwpc",
        densities,
        lax.all_gather(screened, "ka", axis=1, tiled=True),
        preferred_element_type=jnp.float32,
    )
    partial_value = finish_terms(left_sums, matched, pair_count)
    order_table = (jnp.arange(pair_count)[:, None] == pair_order[None, :]).astype(jnp.float32)
    sources = (jnp.arange(k_count) - offset) % k_count
    summed = lax.psum(partial_value, "ga")
    direct = combine_terms(summed, order_table, pair_count)
    received = passed_along(direct, "ka", 4)
    mirror = conjugate_side(jnp.take(received, sources, axis=0), pair_count)
    return (direct, mirror)


AXES = ("ka", "ga")
STEP = 256
WIDE_STEP = 512


def device(z, b, c):
    return (z * 4 + b) * 2 + c


def moved(value, rule):
    pairs = []
    for z in range(4):
        for b in range(4):
            for c in range(2):
                target = rule(z, b, c)
                if target is not None:
                    pairs.append((device(z, b, c), device(*target)))
    return lax.ppermute(value, AXES, pairs)


def along_x(value):
    return moved(value, lambda z, b, c: (z, b ^ 1, c))


def along_y(value):
    return moved(value, lambda z, b, c: (z, b ^ 2, c))


def other_core(value):
    return moved(value, lambda z, b, c: (z, b, 1 - c))


def end_with_mid(value):
    return moved(value, lambda z, b, c: (z ^ 1, b, c))


def mid_to_end(value):
    return moved(value, lambda z, b, c: (z ^ 1, b, c) if z in (1, 2) else None)


def mid_with_mid(value):
    return moved(value, lambda z, b, c: (3 - z, b, c) if z in (1, 2) else None)


ANYWHERE = pl.BlockSpec(memory_space=pltpu.HBM)
IN_SMEM = pl.BlockSpec(memory_space=pltpu.SMEM)
IN_VMEM = pl.BlockSpec(memory_space=pltpu.VMEM)
PARAMS = pltpu.CompilerParams(vmem_limit_bytes=60 * 1024 * 1024)
COST = pl.CostEstimate(flops=1000, bytes_accessed=1000, transcendentals=0)
FLAGS = jax.ShapeDtypeStruct((8,), jnp.int32)


def keep_flags(flags, out):
    for i in range(flags.shape[0]):
        out[i] = flags[i]


def always(flags):
    return None


def at_end(flags):
    return flags[4] == 1


def at_mid(flags):
    return flags[4] == 0


def own_near(flags):
    return flags[1] == 1


def own_far(flags):
    return flags[1] == 0


def whole(ref):
    return ref


def real(first, width):
    return lambda ref: ref.at[0, :, first : first + width]


def imaginary(first, width):
    return lambda ref: ref.at[1, :, first : first + width]


def columns_of(first, width):
    return lambda ref: ref.at[:, first : first + width]


def slots_from(first, count):
    return lambda ref: ref.at[first : first + count]


def moves_kernel(flags, *refs, plan, n_sources, n_outs, n_passing):
    sources, outs = refs[:n_sources], refs[n_sources : n_sources + n_outs]
    flags_out, *stages = refs[n_sources + n_outs + n_passing : -2]
    in_sems, out_sems = refs[-2:]

    def run(chosen, act):
        if chosen is None:
            act()
        else:
            pl.when(chosen)(act)

    copies = []
    for i, (when, number, view, out_numbers, target) in enumerate(plan):
        stage = target(stages[out_numbers[0]])
        load = pltpu.make_async_copy(view(sources[number]), stage, in_sems.at[i])
        stores = [
            pltpu.make_async_copy(stage, target(outs[out_number]), out_sems.at[i, j])
            for j, out_number in enumerate(out_numbers)
        ]
        copies.append((when(flags), load, stores))
        run(when(flags), load.start)
    keep_flags(flags, flags_out)
    for chosen, load, stores in copies:
        def forward():
            load.wait()
            for store in stores:
                store.start()

        run(chosen, forward)
    for chosen, _, stores in copies:
        for store in stores:
            run(chosen, store.wait)


def moves(flags, waits, *outputs, passing=()):
    sources, plan = [], []
    for number, (_, pieces) in enumerate(outputs):
        for when, source, view, target, *more in pieces:
            plan.append((when, len(sources), view, tuple(range(number, number + 1 + sum(more))), target))
            sources.append(source)
    operands = sources + list(waits)
    shapes = [jax.ShapeDtypeStruct(shape, jnp.bfloat16) for shape, _ in outputs]
    aliases = {1 + len(operands) + i: len(outputs) + i for i in range(len(passing))}
    operands += list(passing)
    shapes += [jax.ShapeDtypeStruct(value.shape, value.dtype) for value in passing]
    results = pl.pallas_call(
        functools.partial(
            moves_kernel, plan=tuple(plan), n_sources=len(operands), n_outs=len(outputs), n_passing=len(passing)
        ),
        out_shape=tuple(shapes) + (FLAGS,),
        in_specs=[IN_SMEM] + [ANYWHERE] * len(operands),
        out_specs=(ANYWHERE,) * len(shapes) + (IN_SMEM,),
        input_output_aliases=aliases,
        scratch_shapes=[pltpu.VMEM(shape, jnp.bfloat16) for shape, _ in outputs]
        + [pltpu.SemaphoreType.DMA((max(len(plan), 1),)), pltpu.SemaphoreType.DMA((max(len(plan), 1), 2))],
        compiler_params=PARAMS,
        cost_estimate=COST,
        name="moves",
    )(flags, *operands)
    return results[-1], *results[:-1]


def w_copies(blocks, places, turns, w_buf, source_at, target_at, step, sems):
    width, real_at, imaginary_at = places
    rows = w_buf.shape[1] // len(turns)
    copies = []
    for i, turn in enumerate(turns):
        for part in range(2):
            source = blocks[turn] if turn < 3 else blocks[3 + part]
            first = (real_at, imaginary_at)[part] if turn == 3 else part * width
            target = w_buf.at[part, i * rows : (i + 1) * rows, target_at : target_at + step]
            source = source.at[:, first + source_at : first + source_at + step]
            copies.append(pltpu.make_async_copy(source, target, sems.at[len(copies)]))
    return copies


def m_copies(flags, turns, end_part, mid_part, target, sem):
    rows = target.shape[2] // len(turns)
    for i, turn in enumerate(turns):
        start = pl.multiple_of((flags[0] ^ turn) * rows, rows)
        window = pl.ds(start, rows)
        place = target.at[:, :, i * rows : (i + 1) * rows]
        either(at_end(flags), end_part.at[:, :, window], mid_part.at[:, :, window], place, sem)


def part_of(ref, lead, count):
    return ref.at[lead : lead + count]


def either(chosen, first, second, target, sem):
    a = pltpu.make_async_copy(first, target, sem)
    b = pltpu.make_async_copy(second, target, sem)
    pl.when(chosen)(a.start)
    pl.when(jnp.logical_not(chosen))(b.start)
    return a


def matched_copies(flags, matched, leads, c_buf, first_slot, first, width, sems):
    n_slots, k_count = c_buf.shape[:2]
    pairs = [[part_of(matched[2 * i + j], leads[2 * i + j], k_count) for j in range(2)] for i in range(4)]
    quarter = matched[0].shape[2]
    for s in range(n_slots):
        for half, s_matched in ((0, (first_slot + s + 1) % 4), (1, (first_slot + s - 1) % 4)):
            for end, order in ((1, (0, 1, 2, 3)), (0, (0, 2, 3, 1))):
                for number in range(2):
                    low, high = max(first, number * quarter), min(first + width, (number + 1) * quarter)
                    if low >= high:
                        continue
                    for core in range(2):
                        source = pairs[order[s_matched]][0 if core == number else 1]
                        copy = pltpu.make_async_copy(
                            source.at[:, :, low - number * quarter : high - number * quarter],
                            c_buf.at[s, :, :, low - first : high - first],
                            sems.at[s],
                        )
                        pl.when((flags[2] == half) & (flags[4] == end) & (flags[5] == core))(copy.start)


def matched_wait(c_buf, s, sems):
    pltpu.make_async_copy(c_buf.at[s], c_buf.at[s], sems.at[s]).wait()


def left_tile(lhs, w_re, w_im, k_count, both):
    re_side = jnp.dot(lhs, w_re, preferred_element_type=jnp.float32).reshape(k_count, both, -1)
    im_side = jnp.dot(lhs, w_im, preferred_element_type=jnp.float32).reshape(k_count, both, -1)
    pairs = both // 2
    left_re = re_side[:, :pairs] + im_side[:, pairs:]
    left_im = im_side[:, :pairs] - re_side[:, pairs:]
    return jnp.concatenate([left_re, left_im], axis=1)


def times_matched(left, matched):
    high_part = left.astype(jnp.bfloat16)
    low_part = (left - high_part.astype(jnp.float32)).astype(jnp.bfloat16)
    rows = left.shape[0]
    both_parts = jnp.concatenate([high_part, low_part], axis=0)
    dims = (((1,), (1,)), ((), ()))
    added = lax.dot_general(both_parts, matched, dims, preferred_element_type=jnp.float32)
    return added[:rows] + added[rows:]


def first_kernel(flags, *refs, first_slot, n_slots, columns, places, leads, turns, step):
    n_chunks = len(columns)
    w_refs = [refs[5 * i : 5 * i + 5] for i in range(n_chunks)]
    rest = refs[5 * n_chunks :]
    of_end, of_mid = rest[:n_slots], rest[n_slots : 2 * n_slots]
    left, flags_out, w_buf, m_buf, out_buf, w_sems, m_sems, out_sems = rest[2 * n_slots :]
    depth = w_buf.shape[1]
    _, k_count, both, _ = m_buf.shape
    copies, used = [], 0
    for i in range(n_chunks):
        for at in range(0, columns[i][1], step):
            copies.append(w_copies(w_refs[i], places[i], turns, w_buf, at, used, step, w_sems.at[used // step]))
            used += step
    total = used // step
    for copy in copies[0]:
        copy.start()
    for s in range(n_slots):
        end_part, mid_part = part_of(of_end[s], leads[s], k_count), part_of(of_mid[s], leads[n_slots + s], k_count)
        m_copies(flags, turns, end_part, mid_part, m_buf.at[s], m_sems.at[s])
    for here in copies[1:]:
        for copy in here:
            copy.start()
    keep_flags(flags, flags_out)

    def out_copy(t):
        start = pl.multiple_of(t * step, STEP)
        target = left.at[:, :, :, pl.ds(start, step)]
        return pltpu.make_async_copy(out_buf.at[t % 2], target, out_sems.at[t % 2])

    def one_step(t, carry):
        @pl.when(t >= 2)
        def _():
            out_copy(t - 2).wait()

        for copy in w_copies(w_refs[0], places[0], turns, w_buf, 0, 0, step, w_sems.at[t]):
            copy.wait()
        for s in range(n_slots):
            @pl.when(t == 0)
            def _():
                pltpu.make_async_copy(m_buf.at[s], m_buf.at[s], m_sems.at[s]).wait()

        for at in range(0, step, STEP):
            start = pl.multiple_of(t * step + at, STEP)
            for s in range(n_slots):
                lhs = m_buf[s].reshape(k_count * both, depth)
                w_re, w_im = w_buf[0, :, pl.ds(start, STEP)], w_buf[1, :, pl.ds(start, STEP)]
                out_buf[t % 2, s, :, :, at : at + STEP] = left_tile(lhs, w_re, w_im, k_count, both)
        out_copy(t).start()
        return carry

    lax.fori_loop(0, total, one_step, 0)
    for t in range(max(total - 2, 0), total):
        out_copy(t).wait()


def first_product(flags, chunks, turns, first_slot, n_slots, of_end, of_mid):
    depth = len(turns) * chunks[0][2][0].shape[0]
    both, k_count = of_end[first_slot][0].shape[1], 4
    columns = tuple((first, width) for first, width, _, _ in chunks)
    span = sum(width for _, width in columns)
    slots = range(first_slot, first_slot + n_slots)
    step = WIDE_STEP if n_slots == 1 and all(width % WIDE_STEP == 0 for _, width in columns) else STEP
    chosen = [of_end[s] for s in slots] + [of_mid[s] for s in slots]
    operands = [ref for _, _, blocks, _ in chunks for ref in blocks] + [ref for ref, _ in chosen]
    return pl.pallas_call(
        functools.partial(
            first_kernel,
            first_slot=first_slot,
            n_slots=n_slots,
            columns=columns,
            places=tuple(places for _, _, _, places in chunks),
            leads=tuple(lead for _, lead in chosen),
            turns=turns,
            step=step,
        ),
        out_shape=(jax.ShapeDtypeStruct((n_slots, k_count, both, span), jnp.float32), FLAGS),
        in_specs=[IN_SMEM] + [ANYWHERE] * len(operands),
        out_specs=(ANYWHERE, IN_SMEM),
        scratch_shapes=[
            pltpu.VMEM((2, depth, span), jnp.bfloat16),
            pltpu.VMEM((n_slots, k_count, both, depth), jnp.bfloat16),
            pltpu.VMEM((2, n_slots, k_count, both, step), jnp.float32),
            pltpu.SemaphoreType.DMA((span // step, 8)),
            pltpu.SemaphoreType.DMA((n_slots,)),
            pltpu.SemaphoreType.DMA((2,)),
        ],
        compiler_params=PARAMS,
        cost_estimate=COST,
        name="first_product",
    )(flags, *operands)


def second_kernel(flags, *refs, n_lefts, leads, base, width):
    lefts, matched = refs[:n_lefts], refs[n_lefts : n_lefts + 8]
    sums, flags_out, left_buf, c_buf, left_sems, c_sems = refs[n_lefts + 8 :]
    n_slots, k_count = c_buf.shape[:2]

    def left_start(t):
        s, k, at = t // k_count, t % k_count, 0
        for left in lefts:
            here = s - at

            @pl.when((here >= 0) & (here < left.shape[0]))
            def _():
                pltpu.make_async_copy(left.at[here, k], left_buf.at[t % 4], left_sems.at[t % 4]).start()

            at += left.shape[0]

    for t in range(4):
        left_start(t)
    matched_copies(flags, matched, leads, c_buf, 0, base, width, c_sems)
    keep_flags(flags, flags_out)

    def step(t, carry):
        s, k = t // k_count, t % k_count

        @pl.when(k == 0)
        def _():
            matched_wait(c_buf, s, c_sems)

        pltpu.make_async_copy(lefts[0].at[0, 0], left_buf.at[t % 4], left_sems.at[t % 4]).wait()
        sums[s, k] = times_matched(left_buf[t % 4], c_buf[s, (k + flags[3]) % k_count])

        @pl.when(t + 4 < n_slots * k_count)
        def _():
            left_start(t + 4)

        return carry

    lax.fori_loop(0, n_slots * k_count, step, 0)


def second_product(flags, lefts, matched, base, width):
    n_slots = sum(left.shape[0] for left in lefts)
    _, k_count, both, _ = lefts[0].shape
    return pl.pallas_call(
        functools.partial(
            second_kernel, n_lefts=len(lefts), leads=tuple(lead for _, lead in matched), base=base, width=width
        ),
        out_shape=(jax.ShapeDtypeStruct((n_slots, k_count, both, both), jnp.float32), FLAGS),
        in_specs=[IN_SMEM] + [ANYWHERE] * (len(lefts) + len(matched)),
        out_specs=(IN_VMEM, IN_SMEM),
        scratch_shapes=[
            pltpu.VMEM((4, both, width), jnp.float32),
            pltpu.VMEM((n_slots, k_count, both, width), jnp.bfloat16),
            pltpu.SemaphoreType.DMA((4,)),
            pltpu.SemaphoreType.DMA((n_slots,)),
        ],
        compiler_params=PARAMS,
        cost_estimate=COST,
        name="second_product",
    )(flags, *lefts, *[ref for ref, _ in matched])


def both_kernel(flags, *refs, first_slot, n_slots, columns, places, leads, turns, sums_at, stored, last):
    n_chunks = len(columns)
    w_refs = [refs[5 * i : 5 * i + 5] for i in range(n_chunks)]
    rest = refs[5 * n_chunks :]
    of_end, of_mid, rest = rest[:n_slots], rest[n_slots : 2 * n_slots], rest[2 * n_slots :]
    matched, rest = rest[:8], rest[8:]
    sums_in, rest = rest[: len(sums_at)], rest[len(sums_at) :]
    if stored:
        left, rest = rest[0], rest[1:]
    sums, flags_out, w_buf, m_buf, c_buf, left_buf, acc, w_sems, m_sems, c_sems, left_sems = rest
    depth, span = w_buf.shape[1:]
    _, k_count, both, _ = m_buf.shape
    n_tiles = span // STEP
    copies, used = [], 0
    for i in range(n_chunks):
        for at in range(0, columns[i][1], STEP):
            copies.append(w_copies(w_refs[i], places[i], turns, w_buf, at, used, STEP, w_sems.at[used // STEP]))
            used += STEP
    for copy in copies[0]:
        copy.start()

    def left_copy(s):
        return pltpu.make_async_copy(left.at[s], left_buf.at[s % 2], left_sems.at[s % 2])

    for s in range(n_slots):
        end_part, mid_part = part_of(of_end[s], leads[s], k_count), part_of(of_mid[s], leads[n_slots + s], k_count)
        m_copies(flags, turns, end_part, mid_part, m_buf.at[s], m_sems.at[s])
        if s == 0 and stored:
            left_copy(0).start()
    for here in copies[1:]:
        for copy in here:
            copy.start()
    matched_copies(flags, matched, leads[2 * n_slots :], c_buf, first_slot, columns[0][0], span, c_sems)
    keep_flags(flags, flags_out)
    acc[...] = jnp.zeros(acc.shape, acc.dtype)
    for at, one in zip(sums_at, sums_in):
        count = one.shape[0]
        acc[at : at + count] = acc[at : at + count] + one[...]

    def one_step(t, carry):
        s, tile_number = t // n_tiles, t % n_tiles
        start = pl.multiple_of(tile_number * STEP, STEP)

        @pl.when(s == 0)
        def _():
            for copy in w_copies(w_refs[0], places[0], turns, w_buf, 0, 0, STEP, w_sems.at[tile_number]):
                copy.wait()

        @pl.when(tile_number == 0)
        def _():
            pltpu.make_async_copy(m_buf.at[s], m_buf.at[s], m_sems.at[s]).wait()
            if stored:
                left_copy(s).wait()

                @pl.when(s + 1 < n_slots)
                def _():
                    left_copy(s + 1).start()

        lhs = m_buf[s].reshape(k_count * both, depth)
        tile = left_tile(lhs, w_buf[0, :, pl.ds(start, STEP)], w_buf[1, :, pl.ds(start, STEP)], k_count, both)
        if stored:
            tile = tile + left_buf[s % 2, :, :, pl.ds(start, STEP)]
        left_buf[s % 2, :, :, pl.ds(start, STEP)] = tile

        @pl.when(tile_number == n_tiles - 1)
        def _():
            matched_wait(c_buf, s, c_sems)
            for k in range(k_count):
                acc[s, k] = acc[s, k] + times_matched(left_buf[s % 2, k], c_buf[s, (k + flags[3]) % k_count])

        return carry

    lax.fori_loop(0, n_slots * n_tiles, one_step, 0)
    if last:
        pairs = both // 2
        sums[:, :, :, :pairs] = acc[:, :, :pairs, :pairs] - acc[:, :, pairs:, pairs:]
        sums[:, :, :, pairs:] = acc[:, :, :pairs, pairs:] + acc[:, :, pairs:, :pairs]
    else:
        sums[...] = acc[...]


def both_products(flags, chunks, turns, first_slot, n_slots, of_end, of_mid, matched, sums=(), left=None, last=False):
    k_count = 4
    both = of_end[0][0].shape[1]
    depth = len(turns) * chunks[0][2][0].shape[0]
    columns = tuple((first, width) for first, width, _, _ in chunks)
    span = sum(width for _, width in columns)
    slots = range(first_slot, first_slot + n_slots)
    chosen = [of_end[s] for s in slots] + [of_mid[s] for s in slots] + list(matched)
    operands = [ref for _, _, blocks, _ in chunks for ref in blocks] + [ref for ref, _ in chosen]
    stored = [] if left is None else [left]
    return pl.pallas_call(
        functools.partial(
            both_kernel,
            first_slot=first_slot,
            n_slots=n_slots,
            columns=columns,
            places=tuple(places for _, _, _, places in chunks),
            leads=tuple(lead for _, lead in chosen),
            turns=turns,
            sums_at=tuple(at for at, _ in sums),
            stored=left is not None,
            last=last,
        ),
        out_shape=(jax.ShapeDtypeStruct((n_slots, k_count, both // 2 if last else both, both), jnp.float32), FLAGS),
        in_specs=[IN_SMEM] + [ANYWHERE] * len(operands) + [IN_VMEM] * len(sums) + [ANYWHERE] * len(stored),
        out_specs=(IN_VMEM, IN_SMEM),
        scratch_shapes=[
            pltpu.VMEM((2, depth, span), jnp.bfloat16),
            pltpu.VMEM((n_slots, k_count, both, depth), jnp.bfloat16),
            pltpu.VMEM((n_slots, k_count, both, span), jnp.bfloat16),
            pltpu.VMEM((2, k_count, both, span), jnp.float32),
            pltpu.VMEM((n_slots, k_count, both, both), jnp.float32),
            pltpu.SemaphoreType.DMA((span // STEP, 8)),
            pltpu.SemaphoreType.DMA((n_slots,)),
            pltpu.SemaphoreType.DMA((n_slots,)),
            pltpu.SemaphoreType.DMA((2,)),
        ],
        compiler_params=PARAMS,
        cost_estimate=COST,
        name="both_products",
    )(flags, *operands, *[one for _, one in sums], *stored)


def turn_kernel(flags, first, second, first_turned, second_turned, turned_pair):
    first_turned[0] = first[0].T
    second_turned[0] = second[0].T
    turned_pair[0, 0] = second_turned[0]
    turned_pair[1, 0] = first_turned[0]


def turned_parts(flags, densities):
    k_count, n_rows, both = densities.shape
    quarter = n_rows // 4

    def part(which):
        return pl.BlockSpec((1, quarter, both), lambda k, flags: (k, flags[which], 0))

    one = pl.BlockSpec((1, both, quarter), lambda k, flags: (k, 0, 0))
    first, second, both_parts = pl.pallas_call(
        turn_kernel,
        out_shape=(
            jax.ShapeDtypeStruct((k_count, both, quarter), densities.dtype),
            jax.ShapeDtypeStruct((k_count, both, quarter), densities.dtype),
            jax.ShapeDtypeStruct((2, k_count, both, quarter), densities.dtype),
        ),
        grid_spec=pltpu.PrefetchScalarGridSpec(
            num_scalar_prefetch=1,
            grid=(k_count,),
            in_specs=[part(6), part(7)],
            out_specs=[
                one,
                one,
                pl.BlockSpec((2, 1, both, quarter), lambda k, flags: (0, k, 0, 0)),
            ],
        ),
        compiler_params=PARAMS,
        cost_estimate=COST,
        name="turned_parts",
    )(flags, densities, densities)
    return first, second, both_parts.reshape(2 * k_count, both, quarter)


def body(densities, screened, partner, pair_order):
    k_count, n_rows, both = densities.shape
    pair_count = both // 2
    quarter = n_rows // 4
    panel = screened.shape[2]
    widths = (panel // 2, panel // 4, panel // 4)
    firsts = [sum(widths[:n]) for n in range(3)]
    k_owner = lax.axis_index("ka")
    c = lax.axis_index("ga")
    z, b = k_owner // 4, k_owner % 4
    half, odd = z // 2, z % 2
    offset = partner[0] % k_count
    ends = (z == 0) | (z == 3)
    flags = jnp.stack([b, c == odd, half, offset, ends, c, 2 * (1 - odd) + c, 2 * odd + c]).astype(jnp.int32)
    rows = screened.shape[1]

    part = (k_count, both, quarter)

    def own_pieces(n, when, at=0):
        first, width = firsts[n], widths[n]
        return [
            (when, screened, real(first, width), columns_of(at, width)),
            (when, screened, imaginary(first, width), columns_of(at + width, width)),
        ]

    def far_part(*numbers):
        pieces, at = [], 0
        for n in numbers:
            pieces += own_pieces(n, own_far, at)
            at += 2 * widths[n]
        return (rows, at), pieces

    def sent_far(value):
        return moved(value, lambda z, b, c: (z ^ 1, b, 1 - c) if c != z % 2 else None)

    def panel_parts(n, arrived, at=0, before=None):
        copies = 0 if before is None else 1
        pieces = [piece + (copies,) for piece in own_pieces(n, own_near)]
        pieces.append((own_far, arrived, columns_of(at, 2 * widths[n]), columns_of(0, 2 * widths[n]), copies))
        if before is None:
            return (((rows, 2 * widths[n]), pieces),)
        x_side, y_side = before
        passed = widths[n - 1]
        shape, place = (rows, 2 * widths[n] + passed), columns_of(2 * widths[n], passed)
        return (
            (shape, pieces + [(always, y_side, columns_of(passed, passed), place)]),
            (shape, [(always, x_side, columns_of(0, passed), place)]),
        )

    first_part, second_part = slots_from(0, k_count), slots_from(k_count, k_count)

    flags, sent_0, sent_1 = moves(flags, (), far_part(0), far_part(1))
    arrived_0, arrived_1 = sent_far(sent_0), sent_far(sent_1)
    own_first, own_second, own_both = turned_parts(flags, densities)
    swapped_0 = other_core(own_second)
    pair_a, mid_ad = end_with_mid(own_first), mid_with_mid(own_both)

    flags, panel_0, sent_2 = moves(flags, (swapped_0,), *panel_parts(0, arrived_0), far_part(2))
    x_0, y_0 = along_x(panel_0), along_y(panel_0)

    flags, to_pair, to_mid = moves(
        flags,
        (),
        (part, [(at_end, own_second, whole, whole), (at_mid, mid_ad, first_part, whole)]),
        (part, [(always, pair_a, whole, whole)]),
    )
    pair_b, mid_b = end_with_mid(to_pair), mid_with_mid(to_mid)

    flags, to_x, to_y, sent_2 = moves(flags, (), *panel_parts(1, arrived_1, 0, (x_0, y_0)), passing=(sent_2,))
    x_1, y_1 = along_x(to_x), along_y(to_y)
    panel_1 = to_x
    arrived_2 = sent_far(sent_2)

    flags, pair_a, pair_b, mid_b = moves(flags, (arrived_2,), passing=(pair_a, pair_b, mid_b))
    swapped_a = other_core(pair_a)
    pair_c, mid_c = mid_to_end(mid_b), mid_with_mid(pair_b)
    of_end = [(own_second, 0), (pair_a, 0), (pair_b, 0), None]
    of_mid = [(own_first, 0), (mid_ad, 0), (mid_b, 0), (pair_b, 0)]
    every = (0, 1, 2, 3)

    flags, to_x, to_y = moves(flags, (), *panel_parts(2, arrived_2, 0, (x_1, y_1)))
    x_2, y_2 = along_x(to_x), along_y(to_y)
    panel_2 = to_x
    chunk_0 = (firsts[0], widths[0], (panel_0, x_0, y_0, y_1, x_1), (widths[0], 2 * widths[1], 2 * widths[1]))
    left_0, flags = first_product(flags, [chunk_0], every, 0, 3, of_end, of_mid)

    flags, late_1, late_2 = moves(
        flags,
        (swapped_a,),
        (part, [(at_end, pair_b, whole, whole), (at_mid, mid_ad, second_part, whole)]),
        (part, [(at_end, pair_c, whole, whole), (at_mid, mid_c, whole, whole)]),
    )
    swapped_1, swapped_2 = other_core(late_1), other_core(late_2)
    of_end[3] = (pair_c, 0)
    matched = [(own_second, 0), (swapped_0, 0), (pair_a, 0), (swapped_a, 0)]
    matched += [(late_1, 0), (swapped_1, 0), (late_2, 0), (swapped_2, 0)]
    left_3, flags = first_product(flags, [chunk_0], every, 3, 1, of_end, of_mid)
    sums_0, flags = second_product(flags, [left_0, left_3], matched, firsts[0], widths[0])

    shape = (rows, widths[2])
    flags, to_x, to_y = moves(
        flags,
        (),
        (shape, [(always, y_2, columns_of(widths[2], widths[2]), whole)]),
        (shape, [(always, x_2, columns_of(0, widths[2]), whole)]),
    )
    x_3, y_3 = along_x(to_x), along_y(to_y)
    chunk_1 = (firsts[1], widths[1], (panel_1, x_1, y_1, y_2, x_2), (widths[1], 2 * widths[2], 2 * widths[2]))
    sums_1, flags = both_products(flags, [chunk_1], every, 0, 4, of_end, of_mid, matched, sums=((0, sums_0),))
    chunk_2 = (firsts[2], widths[2], (panel_2, x_2, y_2, y_3, x_3), (widths[2], 0, 0))
    blocks, flags = both_products(
        flags, [chunk_2], every, 0, 4, of_end, of_mid, matched, sums=((0, sums_1),), last=True
    )

    pairs_of_k = k_count // 2
    mine = lax.dynamic_slice_in_dim(blocks, c * pairs_of_k, pairs_of_k, 1)
    mine = mine + other_core(lax.dynamic_slice_in_dim(blocks, (1 - c) * pairs_of_k, pairs_of_k, 1))
    up_order = jnp.where(half == 0, mine, jnp.stack([mine[0], mine[3], mine[2], mine[1]]))
    total = jnp.stack([up_order[0], up_order[3]])
    for shift in (1, 2, 3):
        sent = jnp.stack([up_order[shift], up_order[shift - 1]])
        total = total + moved(sent, lambda z, b, c: ((z + shift) % 4, b, c))
    theirs = other_core(total)
    total = jnp.where(c == 0, jnp.concatenate([total, theirs], axis=1), jnp.concatenate([theirs, total], axis=1))
    total = total.reshape(2 * k_count, pair_count, both)
    order_table = (jnp.arange(pair_count)[:, None] == pair_order[None, :]).astype(jnp.float32)
    filed = reorder(total[:, :, :pair_count], total[:, :, pair_count:], order_table)
    sources = (jnp.arange(k_count) - offset) % k_count
    mirror = conjugate_side(jnp.take(filed[k_count:], sources, axis=0), pair_count)
    return (filed[:k_count], mirror)


def solution(mesh):
    in_specs = (P("ka", None, None), P(None, "ka", "ga"), P(), P())
    out_specs = (P("ka", None, None), P("ka", None, None))
    planes = mesh.shape["ka"] == 16 and mesh.shape["ga"] == 2
    chosen = body if planes else general_body
    return jax.shard_map(chosen, mesh=mesh, in_specs=in_specs, out_specs=out_specs, check_vma=False)
```

time: 311 us -> 289 us (0.929)
  Pallas kernels: 142 us -> 120 us
  starting transfers between devices: 65.9 us -> 72.8 us
  waiting for transfers between devices: 83.9 us -> 78.2 us
    pallas_call x5 -> x2, Pallas kernels: 73.4 us -> 35.6 us  [first_product(): pl.pallas_call(functools.partial(first_kernel, first_slot=first_slot, n_s...]
    pallas_call x3 -> x4, Pallas kernels: 32 us -> 56.9 us  [the longest x2 40.3 us: both_products(): pl.pallas_call(functools.partial(both_kernel, first_slot=first_slot, n_sl...]
    pallas_call x10 -> x8, Pallas kernels: 37 us -> 27.4 us  [moves(): pl.pallas_call(functools.partial(moves_kernel, plan=tuple(plan), n_source...]
    ppermute x29 -> x26, starting transfers between devices: 65.9 us -> 72.8 us  [moved(): return lax.ppermute(value, AXES, pairs)]
    ppermute x29 -> x26, waiting for transfers between devices: 83.9 us -> 78.2 us  [moved(): return lax.ppermute(value, AXES, pairs)]
    unnamed x31 -> x25, local copies, waits for them, and re-layouts: 11.5 us -> 9.14 us
  transfers between devices with their start and end apart: 29 -> 26, of which waited for: 7 -> 9; matrix products, arithmetic and copies ran while one was open for 0% -> 0% of each run, Pallas kernels for 39% -> 33%
where the time goes in v3:
time: 289 us; the launch traced here: 288 us
  Pallas kernels  120 us (42%)
  waiting for transfers between devices  78.2 us (27%)
  starting transfers between devices  72.8 us (25%)
  local copies, waits for them, and re-layouts  11.4 us (4%)
  between operations  3.08 us (1%)
    ppermute x26, waiting for transfers between devices, moved(): return lax.ppermute(value, AXES, pairs)  78.2 us
    ppermute x26, starting transfers between devices, moved(): return lax.ppermute(value, AXES, pairs)  72.8 us
    pallas_call x2, Pallas kernels, both_products(): pl.pallas_call(functools.partial(both_kernel, first_slot=first_slot, n_sl...  40.3 us
    pallas_call x2, Pallas kernels, first_product(): pl.pallas_call(functools.partial(first_kernel, first_slot=first_slot, n_s...  35.6 us
    pallas_call x8, Pallas kernels, moves(): pl.pallas_call(functools.partial(moves_kernel, plan=tuple(plan), n_source...  27.4 us
    pallas_call x1, Pallas kernels, second_product(): pl.pallas_call(functools.partial(second_kernel, n_lefts=len(lefts), leads...  10.9 us
    unnamed x25, local copies, waits for them, and re-layouts  9.14 us
    pallas_call x1, Pallas kernels, turned_parts(): pl.pallas_call(turn_kernel, out_shape=(jax.ShapeDtypeStruct((k_count, bot...  5.81 us
  transfers between devices with their start and end apart: 26, of which 9 were waited for; matrix products, arithmetic and copies ran while one was open for 0% of the time, Pallas kernels for 33%

profile of v3, /device:TPU:0, one launch (start us, length us, event | category | flops | bytes accessed | tf_op | source)
XLA Modules:
  0.0 288.1 jit_solution(18012667482082448583)
XLA Ops:
  4.6 2.1 collective-permute-start
  6.7 5.8 %turned_parts.1 = (bf16[4,128,1536]{2,1,0:T(8,128)(2,1)}, bf16[4,128,1536]{2,1,0:T(8,128)(2,1)}, bf16[2,4,128,1536]{3,2,1,0:T(8,128)(2,1)}) custom-call(s32[8]{0:T(128)} %get-tuple-element.40.flags, bf16[4,6144,128]{2,1,0:T(8,128)(2,1)} %second.1, bf16[4,6144,128]{2,1,0:T(8,128)(2,1)} %second.1), custom_call_target="tpu_custom_call" | custom-call | flops 1000 | bytes 1000 | tf_op jit(solution)/shard_map/turned_parts/pallas_call | solution.py:603
  12.5 6.0 %collective-permute-start.1 = (bf16[4,128,1536]{2,1,0:T(8,128)(2,1)}, bf16[4,128,1536]{2,1,0:T(8,128)(2,1)S(1)}, u32[]{:S(2)}, u32[]{:S(2)}) collective-permute-start(bf16[4,128,1536]{2,1,0:T(8,128)(2,1)} %get-tuple-element.42.refs_0_.refs_5_.refs_2_.refs_13_), channel_id=1, source_target_pairs={{0,1},{1,0},{2,3},{3,2},{4,5},{5,4},{6,7},{7,6},{8,9},{9,8},{10,11... | collective-permute-start | bytes 4718600 | tf_op jit(solution)/shard_map/ppermute | solution.py:89
  18.6 2.4 collective-permute-start.2
  23.0 4.0 %moves.9 = (bf16[384,3072]{1,0:T(8,128)(2,1)}, bf16[384,1536]{1,0:T(8,128)(2,1)}, s32[8]{0:T(128)}) custom-call(s32[8]{0:T(128)} %get-tuple-element.40.flags, bf16[2,384,3072]{2,1,0:T(8,128)(2,1)} %refs_1_.7, bf16[2,384,3072]{2,1,0:T(8,128)(2,1)} %refs_1_.7, bf16[384,3072]{1,0:T(8,128)(2,1)} %collective-permute-done.refs_2_, bf16[2,384,3072]{2,1,0:T(8,128)(2,1)} %refs_1_.7, ...), custom_call_target="tpu_custom_call" | custom-call | flops 1000 | bytes 1000 | tf_op jit(solution)/shard_map/moves/pallas_call | solution.py:214
  27.1 1.6 collective-permute-start.5
  30.1 18.9 %collective-permute-start.3 = (bf16[4,128,1536]{2,1,0:T(8,128)(2,1)S(1)}, bf16[4,128,1536]{2,1,0:T(8,128)(2,1)S(1)}, u32[]{:S(2)}, u32[]{:S(2)}) collective-permute-start(bf16[4,128,1536]{2,1,0:T(8,128)(2,1)S(1)} %copy-done.6), channel_id=1, source_target_pairs={{0,8},{1,9},{2,10},{3,11},{4,12},{5,13},{6,14},{7,15},{8,0},{9,1},... | collective-permute-start | bytes 4718600 | tf_op jit(solution)/shard_map/ppermute | solution.py:89
  49.1 1.7 collective-permute-start.4
  50.7 33.2 %collective-permute-done.3.refs_2_.refs_1_ = bf16[4,128,1536]{2,1,0:T(8,128)(2,1)S(1)} collective-permute-done((bf16[4,128,1536]{2,1,0:T(8,128)(2,1)S(1)}, bf16[4,128,1536]{2,1,0:T(8,128)(2,1)S(1)}, u32[]{:S(2)}, u32[]{:S(2)}) %collective-permute-start.3) | collective-permute-done | bytes 1572896 | tf_op jit(solution)/shard_map/ppermute | solution.py:89
  85.1 4.4 %moves.10 = (bf16[4,128,1536]{2,1,0:T(8,128)(2,1)}, bf16[4,128,1536]{2,1,0:T(8,128)(2,1)}, s32[8]{0:T(128)}) custom-call(s32[8]{0:T(128)} %get-tuple-element.43.flags, bf16[4,128,1536]{2,1,0:T(8,128)(2,1)} %get-tuple-element.42.refs_0_.refs_5_.refs_2_.refs_13_, bf16[8,128,1536]{2,1,0:T(8,128)(2,1)} %collective-permute-done.2.refs_1_.refs_9_.refs_10_, ...), custom_call_target="tpu_custom_call" | custom-call | flops 1000 | bytes 1000 | tf_op jit(solution)/shard_map/moves/pallas_call | solution.py:214
  89.5 7.3 %collective-permute-start.8 = (bf16[4,128,1536]{2,1,0:T(8,128)(2,1)}, bf16[4,128,1536]{2,1,0:T(8,128)(2,1)S(1)}, u32[]{:S(2)}, u32[]{:S(2)}) collective-permute-start(bf16[4,128,1536]{2,1,0:T(8,128)(2,1)} %get-tuple-element.52), channel_id=1, source_target_pairs={{0,8},{1,9},{2,10},{3,11},{4,12},{5,13},{6,14},{7,15},{8,0},{9,1},... | collective-permute-start | bytes 4718600 | tf_op jit(solution)/shard_map/ppermute | solution.py:89
  97.6 4.7 %moves.11 = (bf16[384,3072]{1,0:T(8,128)(2,1)}, bf16[384,3072]{1,0:T(8,128)(2,1)}, bf16[384,1536]{1,0:T(8,128)(2,1)}, s32[8]{0:T(128)}) custom-call(s32[8]{0:T(128)} %get-tuple-element.46.flags, bf16[2,384,3072]{2,1,0:T(8,128)(2,1)} %refs_1_.7, bf16[2,384,3072]{2,1,0:T(8,128)(2,1)} %refs_1_.7, ...), custom_call_target="tpu_custom_call", output_to_operand_aliasing={{2}: (6, {})} | custom-call | flops 1000 | bytes 1000 | tf_op jit(solution)/shard_map/moves/pallas_call | solution.py:214
  102.3 1.7 collective-permute-start.7
  107.0 25.0 %collective-permute-done.8.refs_2_ = bf16[4,128,1536]{2,1,0:T(8,128)(2,1)S(1)} collective-permute-done((bf16[4,128,1536]{2,1,0:T(8,128)(2,1)}, bf16[4,128,1536]{2,1,0:T(8,128)(2,1)S(1)}, u32[]{:S(2)}, u32[]{:S(2)}) %collective-permute-start.8) | collective-permute-done | bytes 1572896 | tf_op jit(solution)/shard_map/ppermute | solution.py:89
  136.2 1.8 collective-permute-start.13
  138.1 10.2 %collective-permute-start.14 = (bf16[4,128,1536]{2,1,0:T(8,128)(2,1)}, bf16[4,128,1536]{2,1,0:T(8,128)(2,1)S(1)}, u32[]{:S(2)}, u32[]{:S(2)}) collective-permute-start(bf16[4,128,1536]{2,1,0:T(8,128)(2,1)} %get-tuple-element.58.refs_6_.refs_4_.refs_15_), channel_id=1, source_target_pairs={{0,1},{1,0},{2,3},{3,2},{4,5},{5,4},{6,7},{7,6},{8,9},{9,8},{10,11... | collective-permute-start | bytes 4718600 | tf_op jit(solution)/shard_map/ppermute | solution.py:89
  148.3 7.5 %collective-permute-done.10.refs_3_.refs_2_ = bf16[384,3072]{1,0:T(8,128)(2,1)} collective-permute-done((bf16[384,3072]{1,0:T(8,128)(2,1)}, bf16[384,3072]{1,0:T(8,128)(2,1)}, u32[]{:S(2)}, u32[]{:S(2)}) %collective-permute-start.10) | collective-permute-done | bytes 2359328 | tf_op jit(solution)/shard_map/ppermute | solution.py:89
  155.8 1.8 collective-permute-done.11.refs_4_.refs_1_
  157.6 4.2 %moves.13 = (bf16[384,2304]{1,0:T(8,128)(2,1)}, bf16[384,2304]{1,0:T(8,128)(2,1)}, s32[8]{0:T(128)}) custom-call(s32[8]{0:T(128)} %get-tuple-element.54.flags, bf16[2,384,3072]{2,1,0:T(8,128)(2,1)} %refs_1_.7, bf16[2,384,3072]{2,1,0:T(8,128)(2,1)} %refs_1_.7, bf16[384,1536]{1,0:T(8,128)(2,1)} %collective-permute-done.7.refs_0_.refs_2_, ...), custom_call_target="tpu_custom_call" | custom-call | flops 1000 | bytes 1000 | tf_op jit(solution)/shard_map/moves/pallas_call | solution.py:214
  163.8 23.8 %first_product.2 = (f32[3,4,128,1536]{3,2,1,0:T(8,128)}, s32[8]{0:T(128)}) custom-call(s32[8]{0:T(128)} %get-tuple-element.57.flags, bf16[384,3072]{1,0:T(8,128)(2,1)} %get-tuple-element.48.refs_0_, bf16[384,3072]{1,0:T(8,128)(2,1)} %collective-permute-done.6.refs_4_.refs_1_, bf16[384,3072]{1,0:T(8,128)(2,1)} %collective-permute-done.5.refs_3_.refs_2_, ...), custom_call_target="tpu_custom_call" | custom-call | flops 1000 | bytes 1000 | tf_op jit(solution)/shard_map/first_product/pallas_call | solution.py:374
  189.3 4.3 %moves.14 = (bf16[4,128,1536]{2,1,0:T(8,128)(2,1)}, bf16[4,128,1536]{2,1,0:T(8,128)(2,1)}, s32[8]{0:T(128)}) custom-call(s32[8]{0:T(128)} %get-tuple-element.61.flags, bf16[4,128,1536]{2,1,0:T(8,128)(2,1)} %get-tuple-element.59.refs_7_.refs_0_.refs_6_.refs_12_, bf16[8,128,1536]{2,1,0:T(8,128)(2,1)} %collective-permute-done.2.refs_1_.refs_9_.refs_10_, ...), custom_call_target="tpu_custom_call" | custom-call | flops 1000 | bytes 1000 | tf_op jit(solution)/shard_map/moves/pallas_call | solution.py:214
  193.6 2.1 collective-permute-start.15
  195.7 11.8 %first_product.3 = (f32[1,4,128,1536]{3,2,1,0:T(8,128)}, s32[8]{0:T(128)}) custom-call(s32[8]{0:T(128)} %get-tuple-element.62.flags, bf16[384,3072]{1,0:T(8,128)(2,1)} %get-tuple-element.48.refs_0_, bf16[384,3072]{1,0:T(8,128)(2,1)} %collective-permute-done.6.refs_4_.refs_1_, bf16[384,3072]{1,0:T(8,128)(2,1)} %collective-permute-done.5.refs_3_.refs_2_, ...), custom_call_target="tpu_custom_call" | custom-call | flops 1000 | bytes 1000 | tf_op jit(solution)/shard_map/first_product/pallas_call | solution.py:374
  209.2 10.9 %second_product.1 = (f32[4,4,128,128]{3,2,1,0:T(8,128)}, s32[8]{0:T(128)}) custom-call(s32[8]{0:T(128)} %get-tuple-element.63.flags, f32[3,4,128,1536]{3,2,1,0:T(8,128)} %get-tuple-element.64.refs_0_, f32[1,4,128,1536]{3,2,1,0:T(8,128)} %get-tuple-element.65.refs_1_, bf16[4,128,1536]{2,1,0:T(8,128)(2,1)} %get-tuple-element.42.refs_0_.refs_5_.refs_2_.refs_13_, ...), custom_call_target="tpu_custom_call" | custom-call | flops 1000 | bytes 1000 | tf_op jit(solution)/shard_map/second_product/pallas_call | solution.py:445
  220.1 3.3 %moves.15 = (bf16[384,768]{1,0:T(8,128)(2,1)}, bf16[384,768]{1,0:T(8,128)(2,1)}, s32[8]{0:T(128)}) custom-call(s32[8]{0:T(128)} %get-tuple-element.68.flags, bf16[384,2304]{1,0:T(8,128)(2,1)} %collective-permute-done.17.refs_0_.refs_3_.refs_2_, bf16[384,2304]{1,0:T(8,128)(2,1)} %collective-permute-done.18.refs_1_.refs_4_), custom_call_target="tpu_custom_call" | custom-call | flops 1000 | bytes 1000 | tf_op jit(solution)/shard_map/moves/pallas_call | solution.py:214
  223.4 1.6 collective-permute-start.19
  225.6 20.1 %both_products.2 = (f32[4,4,128,128]{3,2,1,0:T(8,128)}, s32[8]{0:T(128)}) custom-call(s32[8]{0:T(128)} %get-tuple-element.71.flags, bf16[384,3072]{1,0:T(8,128)(2,1)} %get-tuple-element.56.refs_0_, bf16[384,3072]{1,0:T(8,128)(2,1)} %collective-permute-done.11.refs_4_.refs_1_, bf16[384,3072]{1,0:T(8,128)(2,1)} %collective-permute-done.10.refs_3_.refs_2_, ...), custom_call_target="tpu_custom_call" | custom-call | flops 1000 | bytes 1000 | tf_op jit(solution)/shard_map/both_products/pallas_call | solution.py:555
  246.7 20.2 %both_products.3 = (f32[4,4,64,128]{3,2,1,0:T(8,128)}, s32[8]{0:T(128)}) custom-call(s32[8]{0:T(128)} %get-tuple-element.73.flags, bf16[384,2304]{1,0:T(8,128)(2,1)} %get-tuple-element.70.refs_0_, bf16[384,2304]{1,0:T(8,128)(2,1)} %collective-permute-done.18.refs_1_.refs_4_, bf16[384,2304]{1,0:T(8,128)(2,1)} %collective-permute-done.17.refs_0_.refs_3_.refs_2_, ...), custom_call_target="tpu_custom_call" | custom-call | flops 1000 | bytes 1000 | tf_op jit(solution)/shard_map/both_products/pallas_call | solution.py:555
  270.6 1.8 collective-permute-start.22
  273.8 2.8 collective-permute-start.24
  276.7 2.2 collective-permute-done.22
  278.9 4.8 %collective-permute-done.23 = f32[2,2,64,128]{3,2,1,0:T(8,128)S(1)} collective-permute-done((f32[2,2,64,128]{3,2,1,0:T(8,128)S(1)}, f32[2,2,64,128]{3,2,1,0:T(8,128)S(1)}, u32[]{:S(2)}, u32[]{:S(2)}) %collective-permute-start.23) | collective-permute-done | bytes 131104 | tf_op jit(solution)/shard_map/ppermute | solution.py:89
  (78 shorter events, 31.1 us)
Async XLA Ops:
  4.6 17.2 %collective-permute-start = (bf16[384,3072]{1,0:T(8,128)(2,1)}, bf16[384,3072]{1,0:T(8,128)(2,1)}, u32[]{:S(2)}, u32[]{:S(2)}) collective-permute-start(bf16[384,3072]{1,0:T(8,128)(2,1)} %get-tuple-element.41), channel_id=1, source_target_pairs={{1,8},{3,10},{5,12},{7,14},{8,1},{10,3},{12,5},{14,7},{17,24},{19,... | collective-permute-start | bytes 7077896 | tf_op jit(solution)/shard_map/ppermute | solution.py:89
  12.5 9.3 %collective-permute-start.1 = (bf16[4,128,1536]{2,1,0:T(8,128)(2,1)}, bf16[4,128,1536]{2,1,0:T(8,128)(2,1)S(1)}, u32[]{:S(2)}, u32[]{:S(2)}) collective-permute-start(bf16[4,128,1536]{2,1,0:T(8,128)(2,1)} %get-tuple-element.42.refs_0_.refs_5_.refs_2_.refs_13_), channel_id=1, source_target_pairs={{0,1},{1,0},{2,3},{3,2},{4,5},{5,4},{6,7},{7,6},{8,9},{9,8},{10,11... | collective-permute-start | bytes 4718600 | tf_op jit(solution)/shard_map/ppermute | solution.py:89
  18.6 11.6 %copy-start.6 = (bf16[4,128,1536]{2,1,0:T(8,128)(2,1)S(1)}, bf16[4,128,1536]{2,1,0:T(8,128)(2,1)}, u32[]{:S(2)}) copy-start(bf16[4,128,1536]{2,1,0:T(8,128)(2,1)} %get-tuple-element.45.refs_8_.refs_9_) | copy-start | bytes 4718596
  18.6 65.4 %collective-permute-start.2 = (bf16[8,128,1536]{2,1,0:T(8,128)(2,1)}, bf16[8,128,1536]{2,1,0:T(8,128)(2,1)}, u32[]{:S(2)}, u32[]{:S(2)}) collective-permute-start(bf16[8,128,1536]{2,1,0:T(8,128)(2,1)} %bitcast.27), channel_id=1, source_target_pairs={{8,16},{9,17},{10,18},{11,19},{12,20},{13,21},{14,22},{15,23},{16,... | collective-permute-start | bytes 9437192 | tf_op jit(solution)/shard_map/ppermute | solution.py:89
  21.8 1.2 copy-start.4
  27.1 70.5 %collective-permute-start.5 = (bf16[384,3072]{1,0:T(8,128)(2,1)}, bf16[384,3072]{1,0:T(8,128)(2,1)}, u32[]{:S(2)}, u32[]{:S(2)}) collective-permute-start(bf16[384,3072]{1,0:T(8,128)(2,1)} %get-tuple-element.48.refs_0_), channel_id=1, source_target_pairs={{0,4},{1,5},{2,6},{3,7},{4,0},{5,1},{6,2},{7,3},{8,12},{9,13},{10,... | collective-permute-start | bytes 7077896 | tf_op jit(solution)/shard_map/ppermute | solution.py:89
  28.7 68.9 %collective-permute-start.6 = (bf16[384,3072]{1,0:T(8,128)(2,1)}, bf16[384,3072]{1,0:T(8,128)(2,1)}, u32[]{:S(2)}, u32[]{:S(2)}) collective-permute-start(bf16[384,3072]{1,0:T(8,128)(2,1)} %get-tuple-element.48.refs_0_), channel_id=1, source_target_pairs={{0,2},{1,3},{2,0},{3,1},{4,6},{5,7},{6,4},{7,5},{8,10},{9,11},{10,... | collective-permute-start | bytes 7077896 | tf_op jit(solution)/shard_map/ppermute | solution.py:89
  30.1 53.8 %collective-permute-start.3 = (bf16[4,128,1536]{2,1,0:T(8,128)(2,1)S(1)}, bf16[4,128,1536]{2,1,0:T(8,128)(2,1)S(1)}, u32[]{:S(2)}, u32[]{:S(2)}) collective-permute-start(bf16[4,128,1536]{2,1,0:T(8,128)(2,1)S(1)} %copy-done.6), channel_id=1, source_target_pairs={{0,8},{1,9},{2,10},{3,11},{4,12},{5,13},{6,14},{7,15},{8,0},{9,1},... | collective-permute-start | bytes 4718600 | tf_op jit(solution)/shard_map/ppermute | solution.py:89
  49.1 48.5 %collective-permute-start.4 = (bf16[384,1536]{1,0:T(8,128)(2,1)}, bf16[384,1536]{1,0:T(8,128)(2,1)}, u32[]{:S(2)}, u32[]{:S(2)}) collective-permute-start(bf16[384,1536]{1,0:T(8,128)(2,1)} %get-tuple-element.47), channel_id=1, source_target_pairs={{1,8},{3,10},{5,12},{7,14},{8,1},{10,3},{12,5},{14,7},{17,24},{19,... | collective-permute-start | bytes 3538952 | tf_op jit(solution)/shard_map/ppermute | solution.py:89
  89.5 42.4 %collective-permute-start.8 = (bf16[4,128,1536]{2,1,0:T(8,128)(2,1)}, bf16[4,128,1536]{2,1,0:T(8,128)(2,1)S(1)}, u32[]{:S(2)}, u32[]{:S(2)}) collective-permute-start(bf16[4,128,1536]{2,1,0:T(8,128)(2,1)} %get-tuple-element.52), channel_id=1, source_target_pairs={{0,8},{1,9},{2,10},{3,11},{4,12},{5,13},{6,14},{7,15},{8,0},{9,1},... | collective-permute-start | bytes 4718600 | tf_op jit(solution)/shard_map/ppermute | solution.py:89
  96.8 35.2 %collective-permute-start.9 = (bf16[4,128,1536]{2,1,0:T(8,128)(2,1)}, bf16[4,128,1536]{2,1,0:T(8,128)(2,1)S(1)}, u32[]{:S(2)}, u32[]{:S(2)}) collective-permute-start(bf16[4,128,1536]{2,1,0:T(8,128)(2,1)} %get-tuple-element.53), channel_id=1, source_target_pairs={{8,16},{9,17},{10,18},{11,19},{12,20},{13,21},{14,22},{15,23},{16,... | collective-permute-start | bytes 4718600 | tf_op jit(solution)/shard_map/ppermute | solution.py:89
  102.3 29.7 %collective-permute-start.7 = (bf16[384,1536]{1,0:T(8,128)(2,1)}, bf16[384,1536]{1,0:T(8,128)(2,1)}, u32[]{:S(2)}, u32[]{:S(2)}) collective-permute-start(bf16[384,1536]{1,0:T(8,128)(2,1)} %get-tuple-element.51), channel_id=1, source_target_pairs={{1,8},{3,10},{5,12},{7,14},{8,1},{10,3},{12,5},{14,7},{17,24},{19,... | collective-permute-start | bytes 3538952 | tf_op jit(solution)/shard_map/ppermute | solution.py:89
  104.0 51.8 %collective-permute-start.10 = (bf16[384,3072]{1,0:T(8,128)(2,1)}, bf16[384,3072]{1,0:T(8,128)(2,1)}, u32[]{:S(2)}, u32[]{:S(2)}) collective-permute-start(bf16[384,3072]{1,0:T(8,128)(2,1)} %get-tuple-element.55), channel_id=1, source_target_pairs={{0,4},{1,5},{2,6},{3,7},{4,0},{5,1},{6,2},{7,3},{8,12},{9,13},{10,... | collective-permute-start | bytes 7077896 | tf_op jit(solution)/shard_map/ppermute | solution.py:89
  105.5 52.1 %collective-permute-start.11 = (bf16[384,3072]{1,0:T(8,128)(2,1)}, bf16[384,3072]{1,0:T(8,128)(2,1)}, u32[]{:S(2)}, u32[]{:S(2)}) collective-permute-start(bf16[384,3072]{1,0:T(8,128)(2,1)} %get-tuple-element.56.refs_0_), channel_id=1, source_target_pairs={{0,2},{1,3},{2,0},{3,1},{4,6},{5,7},{6,4},{7,5},{8,10},{9,11},{10,... | collective-permute-start | bytes 7077896 | tf_op jit(solution)/shard_map/ppermute | solution.py:89
  132.0 1.7 copy-start.3
  134.9 52.7 %collective-permute-start.12 = (bf16[4,128,1536]{2,1,0:T(8,128)(2,1)}, bf16[4,128,1536]{2,1,0:T(8,128)(2,1)S(1)}, u32[]{:S(2)}, u32[]{:S(2)}) collective-permute-start(bf16[4,128,1536]{2,1,0:T(8,128)(2,1)} %get-tuple-element.60.refs_10_.refs_11_), channel_id=1, source_target_pairs={{8,0},{9,1},{10,2},{11,3},{12,4},{13,5},{14,6},{15,7},{16,24},{17,... | collective-permute-start | bytes 4718600 | tf_op jit(solution)/shard_map/ppermute | solution.py:89
  136.2 51.4 %collective-permute-start.13 = (bf16[4,128,1536]{2,1,0:T(8,128)(2,1)}, bf16[4,128,1536]{2,1,0:T(8,128)(2,1)}, u32[]{:S(2)}, u32[]{:S(2)}) collective-permute-start(bf16[4,128,1536]{2,1,0:T(8,128)(2,1)} %get-tuple-element.59.refs_7_.refs_0_.refs_6_.refs_12_), channel_id=1, source_target_pairs={{8,16},{9,17},{10,18},{11,19},{12,20},{13,21},{14,22},{15,23},{16,... | collective-permute-start | bytes 4718600 | tf_op jit(solution)/shard_map/ppermute | solution.py:89
  138.1 49.6 %collective-permute-start.14 = (bf16[4,128,1536]{2,1,0:T(8,128)(2,1)}, bf16[4,128,1536]{2,1,0:T(8,128)(2,1)S(1)}, u32[]{:S(2)}, u32[]{:S(2)}) collective-permute-start(bf16[4,128,1536]{2,1,0:T(8,128)(2,1)} %get-tuple-element.58.refs_6_.refs_4_.refs_15_), channel_id=1, source_target_pairs={{0,1},{1,0},{2,3},{3,2},{4,5},{5,4},{6,7},{7,6},{8,9},{9,8},{10,11... | collective-permute-start | bytes 4718600 | tf_op jit(solution)/shard_map/ppermute | solution.py:89
  161.8 58.3 %collective-permute-start.17 = (bf16[384,2304]{1,0:T(8,128)(2,1)}, bf16[384,2304]{1,0:T(8,128)(2,1)}, u32[]{:S(2)}, u32[]{:S(2)}) collective-permute-start(bf16[384,2304]{1,0:T(8,128)(2,1)} %get-tuple-element.69), channel_id=1, source_target_pairs={{0,4},{1,5},{2,6},{3,7},{4,0},{5,1},{6,2},{7,3},{8,12},{9,13},{10,... | collective-permute-start | bytes 5308424 | tf_op jit(solution)/shard_map/ppermute | solution.py:89
  162.3 57.8 %collective-permute-start.18 = (bf16[384,2304]{1,0:T(8,128)(2,1)}, bf16[384,2304]{1,0:T(8,128)(2,1)}, u32[]{:S(2)}, u32[]{:S(2)}) collective-permute-start(bf16[384,2304]{1,0:T(8,128)(2,1)} %get-tuple-element.70.refs_0_), channel_id=1, source_target_pairs={{0,2},{1,3},{2,0},{3,1},{4,6},{5,7},{6,4},{7,5},{8,10},{9,11},{10,... | collective-permute-start | bytes 5308424 | tf_op jit(solution)/shard_map/ppermute | solution.py:89
  187.7 1.6 copy-start.5
  193.6 14.0 %collective-permute-start.15 = (bf16[4,128,1536]{2,1,0:T(8,128)(2,1)}, bf16[4,128,1536]{2,1,0:T(8,128)(2,1)S(1)}, u32[]{:S(2)}, u32[]{:S(2)}) collective-permute-start(bf16[4,128,1536]{2,1,0:T(8,128)(2,1)} %get-tuple-element.66.refs_6_.refs_17_), channel_id=1, source_target_pairs={{0,1},{1,0},{2,3},{3,2},{4,5},{5,4},{6,7},{7,6},{8,9},{9,8},{10,11... | collective-permute-start | bytes 4718600 | tf_op jit(solution)/shard_map/ppermute | solution.py:89
  195.7 11.9 %collective-permute-start.16 = (bf16[4,128,1536]{2,1,0:T(8,128)(2,1)}, bf16[4,128,1536]{2,1,0:T(8,128)(2,1)S(1)}, u32[]{:S(2)}, u32[]{:S(2)}) collective-permute-start(bf16[4,128,1536]{2,1,0:T(8,128)(2,1)} %get-tuple-element.67.refs_8_.refs_19_), channel_id=1, source_target_pairs={{0,1},{1,0},{2,3},{3,2},{4,5},{5,4},{6,7},{7,6},{8,9},{9,8},{10,11... | collective-permute-start | bytes 4718600 | tf_op jit(solution)/shard_map/ppermute | solution.py:89
  207.6 1.6 copy-start.8
  223.4 22.2 %collective-permute-start.19 = (bf16[384,768]{1,0:T(8,128)(2,1)}, bf16[384,768]{1,0:T(8,128)(2,1)S(1)}, u32[]{:S(2)}, u32[]{:S(2)}) collective-permute-start(bf16[384,768]{1,0:T(8,128)(2,1)} %get-tuple-element.74), channel_id=1, source_target_pairs={{0,4},{1,5},{2,6},{3,7},{4,0},{5,1},{6,2},{7,3},{8,12},{9,13},{10,... | collective-permute-start | bytes 1769480 | tf_op jit(solution)/shard_map/ppermute | solution.py:89
  225.0 20.7 %collective-permute-start.20 = (bf16[384,768]{1,0:T(8,128)(2,1)}, bf16[384,768]{1,0:T(8,128)(2,1)S(1)}, u32[]{:S(2)}, u32[]{:S(2)}) collective-permute-start(bf16[384,768]{1,0:T(8,128)(2,1)} %get-tuple-element.75), channel_id=1, source_target_pairs={{0,2},{1,3},{2,0},{3,1},{4,6},{5,7},{6,4},{7,5},{8,10},{9,11},{10,... | collective-permute-start | bytes 1769480 | tf_op jit(solution)/shard_map/ppermute | solution.py:89
  267.8 1.6 collective-permute-start.21
  270.5 14.7 %copy-start.11 = (s32[64]{0:T(128)S(1)}, s32[64]{0:T(128)}, u32[]{:S(2)}) copy-start(s32[64]{0:T(128)} %param.7) | copy-start | bytes 772
  270.6 8.3 %collective-permute-start.22 = (f32[2,2,64,128]{3,2,1,0:T(8,128)S(1)}, f32[2,2,64,128]{3,2,1,0:T(8,128)S(1)}, u32[]{:S(2)}, u32[]{:S(2)}) collective-permute-start(f32[2,2,64,128]{3,2,1,0:T(8,128)S(1)} %get-tuple-element.92), channel_id=1, source_target_pairs={{0,8},{1,9},{2,10},{3,11},{4,12},{5,13},{6,14},{7,15},{8,16},{9,17... | collective-permute-start | bytes 393224 | tf_op jit(solution)/shard_map/ppermute | solution.py:89
  272.4 11.3 %collective-permute-start.23 = (f32[2,2,64,128]{3,2,1,0:T(8,128)S(1)}, f32[2,2,64,128]{3,2,1,0:T(8,128)S(1)}, u32[]{:S(2)}, u32[]{:S(2)}) collective-permute-start(f32[2,2,64,128]{3,2,1,0:T(8,128)S(1)} %get-tuple-element.93), channel_id=1, source_target_pairs={{0,16},{1,17},{2,18},{3,19},{4,20},{5,21},{6,22},{7,23},{8,24},{9,... | collective-permute-start | bytes 393224 | tf_op jit(solution)/shard_map/ppermute | solution.py:89
  273.8 9.8 %collective-permute-start.24 = (f32[2,2,64,128]{3,2,1,0:T(8,128)S(1)}, f32[2,2,64,128]{3,2,1,0:T(8,128)S(1)}, u32[]{:S(2)}, u32[]{:S(2)}) collective-permute-start(f32[2,2,64,128]{3,2,1,0:T(8,128)S(1)} %get-tuple-element.94), channel_id=1, source_target_pairs={{0,24},{1,25},{2,26},{3,27},{4,28},{5,29},{6,30},{7,31},{8,0},{9,1... | collective-permute-start | bytes 393224 | tf_op jit(solution)/shard_map/ppermute | solution.py:89
  283.7 1.4 collective-permute-start.25
  (6 other events, 6.5 us)

commit v4 on v3

--- a/solution.py
+++ b/solution.py
@@ -116,7 +116,7 @@
 ANYWHERE = pl.BlockSpec(memory_space=pltpu.HBM)
 IN_SMEM = pl.BlockSpec(memory_space=pltpu.SMEM)
 IN_VMEM = pl.BlockSpec(memory_space=pltpu.VMEM)
-PARAMS = pltpu.CompilerParams(vmem_limit_bytes=60 * 1024 * 1024)
+PARAMS = pltpu.CompilerParams(vmem_limit_bytes=64 * 1024 * 1024)
 COST = pl.CostEstimate(flops=1000, bytes_accessed=1000, transcendentals=0)
 FLAGS = jax.ShapeDtypeStruct((8,), jnp.int32)
 
@@ -263,11 +263,11 @@
     return a
 
 
-def matched_copies(flags, matched, leads, c_buf, first_slot, first, width, sems):
-    n_slots, k_count = c_buf.shape[:2]
+def matched_copies(flags, matched, leads, c_buf, slots, first, width, sems, first_slot=0):
+    k_count = c_buf.shape[1]
     pairs = [[part_of(matched[2 * i + j], leads[2 * i + j], k_count) for j in range(2)] for i in range(4)]
     quarter = matched[0].shape[2]
-    for s in range(n_slots):
+    for s in slots:
         for half, s_matched in ((0, (first_slot + s + 1) % 4), (1, (first_slot + s - 1) % 4)):
             for end, order in ((1, (0, 1, 2, 3)), (0, (0, 2, 3, 1))):
                 for number in range(2):
@@ -321,14 +321,13 @@
             copies.append(w_copies(w_refs[i], places[i], turns, w_buf, at, used, step, w_sems.at[used // step]))
             used += step
     total = used // step
-    for copy in copies[0]:
-        copy.start()
-    for s in range(n_slots):
-        end_part, mid_part = part_of(of_end[s], leads[s], k_count), part_of(of_mid[s], leads[n_slots + s], k_count)
-        m_copies(flags, turns, end_part, mid_part, m_buf.at[s], m_sems.at[s])
-    for here in copies[1:]:
-        for copy in here:
-            copy.start()
+    for s in range(max(n_slots, len(copies))):
+        if s < len(copies):
+            for copy in copies[s]:
+                copy.start()
+        if s < n_slots:
+            end_part, mid_part = part_of(of_end[s], leads[s], k_count), part_of(of_mid[s], leads[n_slots + s], k_count)
+            m_copies(flags, turns, end_part, mid_part, m_buf.at[s], m_sems.at[s])
     keep_flags(flags, flags_out)
 
     def out_copy(t):
@@ -343,9 +342,9 @@
 
         for copy in w_copies(w_refs[0], places[0], turns, w_buf, 0, 0, step, w_sems.at[t]):
             copy.wait()
-        for s in range(n_slots):
-            @pl.when(t == 0)
-            def _():
+        @pl.when(t == 0)
+        def _():
+            for s in range(n_slots):
                 pltpu.make_async_copy(m_buf.at[s], m_buf.at[s], m_sems.at[s]).wait()
 
         for at in range(0, step, STEP):
@@ -399,106 +398,132 @@
     )(flags, *operands)
 
 
-def second_kernel(flags, *refs, n_lefts, leads, base, width):
-    lefts, matched = refs[:n_lefts], refs[n_lefts : n_lefts + 8]
-    sums, flags_out, left_buf, c_buf, left_sems, c_sems = refs[n_lefts + 8 :]
-    n_slots, k_count = c_buf.shape[:2]
-
-    def left_start(t):
-        s, k, at = t // k_count, t % k_count, 0
-        for left in lefts:
-            here = s - at
-
-            @pl.when((here >= 0) & (here < left.shape[0]))
-            def _():
-                pltpu.make_async_copy(left.at[here, k], left_buf.at[t % 4], left_sems.at[t % 4]).start()
-
-            at += left.shape[0]
-
-    for t in range(4):
-        left_start(t)
-    matched_copies(flags, matched, leads, c_buf, 0, base, width, c_sems)
+def stored_kernel(flags, *refs, n_slots, n_lefts, columns, places, leads):
+    first, width = columns
+    w_refs, of_end, of_mid = refs[:5], refs[5 : 5 + n_slots], refs[5 + n_slots : 5 + 2 * n_slots]
+    matched, rest = refs[5 + 2 * n_slots : 13 + 2 * n_slots], refs[13 + 2 * n_slots :]
+    lefts, (sums, flags_out, w_buf, m_buf, c_buf, left_buf, w_sems, m_sems, c_sems, left_sems) = rest[:n_lefts], rest[n_lefts:]
+    depth = w_buf.shape[1]
+    all_slots, k_count, both, _ = c_buf.shape
+    n_tiles = width // STEP
+    sources = [left.at[i] for left in lefts for i in range(left.shape[0])]
+    w_loads = w_copies(w_refs, places, (3,), w_buf, 0, 0, width, w_sems)
+    for copy in w_loads:
+        copy.start()
+    for s in range(all_slots):
+        if s < n_slots:
+            end_part, mid_part = part_of(of_end[s], leads[s], k_count), part_of(of_mid[s], leads[n_slots + s], k_count)
+            m_copies(flags, (3,), end_part, mid_part, m_buf.at[s], m_sems.at[s])
+        pltpu.make_async_copy(sources[s], left_buf.at[s], left_sems.at[s]).start()
+        matched_copies(flags, matched, leads[2 * n_slots :], c_buf, (s,), first, width, c_sems)
     keep_flags(flags, flags_out)
-
-    def step(t, carry):
-        s, k = t // k_count, t % k_count
-
-        @pl.when(k == 0)
+    for copy in w_loads:
+        copy.wait()
+
+    def second(s):
+        matched_wait(c_buf, s, c_sems)
+        for k in range(k_count):
+            sums[s, k] = times_matched(left_buf[s, k], c_buf[s, (k + flags[3]) % k_count])
+
+    def one_step(t, carry):
+        s, tile_number = t // n_tiles, t % n_tiles
+        start = pl.multiple_of(tile_number * STEP, STEP)
+
+        @pl.when(tile_number == 0)
         def _():
-            matched_wait(c_buf, s, c_sems)
-
-        pltpu.make_async_copy(lefts[0].at[0, 0], left_buf.at[t % 4], left_sems.at[t % 4]).wait()
-        sums[s, k] = times_matched(left_buf[t % 4], c_buf[s, (k + flags[3]) % k_count])
-
-        @pl.when(t + 4 < n_slots * k_count)
+            pltpu.make_async_copy(m_buf.at[s], m_buf.at[s], m_sems.at[s]).wait()
+            pltpu.make_async_copy(left_buf.at[s], left_buf.at[s], left_sems.at[s]).wait()
+
+        lhs = m_buf[s].reshape(k_count * both, depth)
+        tile = left_tile(lhs, w_buf[0, :, pl.ds(start, STEP)], w_buf[1, :, pl.ds(start, STEP)], k_count, both)
+        left_buf[s, :, :, pl.ds(start, STEP)] = left_buf[s, :, :, pl.ds(start, STEP)] + tile
+
+        @pl.when(tile_number == n_tiles - 1)
         def _():
-            left_start(t + 4)
+            second(s)
 
         return carry
 
-    lax.fori_loop(0, n_slots * k_count, step, 0)
-
-
-def second_product(flags, lefts, matched, base, width):
-    n_slots = sum(left.shape[0] for left in lefts)
-    _, k_count, both, _ = lefts[0].shape
+    lax.fori_loop(0, n_slots * n_tiles, one_step, 0)
+
+    def only_second(s, carry):
+        pltpu.make_async_copy(left_buf.at[s], left_buf.at[s], left_sems.at[s]).wait()
+        second(s)
+        return carry
+
+    lax.fori_loop(n_slots, all_slots, only_second, 0)
+
+
+def stored_products(flags, chunk, of_end, of_mid, matched, lefts):
+    n_slots, k_count, both, _ = lefts[0].shape
+    all_slots = sum(left.shape[0] for left in lefts)
+    first, width, blocks, places = chunk
+    rows = blocks[0].shape[0]
+    chosen = list(of_end[:n_slots]) + list(of_mid[:n_slots]) + list(matched)
+    operands = list(blocks) + [ref for ref, _ in chosen] + list(lefts)
     return pl.pallas_call(
         functools.partial(
-            second_kernel, n_lefts=len(lefts), leads=tuple(lead for _, lead in matched), base=base, width=width
+            stored_kernel,
+            n_slots=n_slots,
+            n_lefts=len(lefts),
+            columns=(first, width),
+            places=places,
+            leads=tuple(lead for _, lead in chosen),
         ),
-        out_shape=(jax.ShapeDtypeStruct((n_slots, k_count, both, both), jnp.float32), FLAGS),
-        in_specs=[IN_SMEM] + [ANYWHERE] * (len(lefts) + len(matched)),
+        out_shape=(jax.ShapeDtypeStruct((all_slots, k_count, both, both), jnp.float32), FLAGS),
+        in_specs=[IN_SMEM] + [ANYWHERE] * len(operands),
         out_specs=(IN_VMEM, IN_SMEM),
         scratch_shapes=[
-            pltpu.VMEM((4, both, width), jnp.float32),
-            pltpu.VMEM((n_slots, k_count, both, width), jnp.bfloat16),
-            pltpu.SemaphoreType.DMA((4,)),
+            pltpu.VMEM((2, rows, width), jnp.bfloat16),
+            pltpu.VMEM((n_slots, k_count, both, rows), jnp.bfloat16),
+            pltpu.VMEM((all_slots, k_count, both, width), jnp.bfloat16),
+            pltpu.VMEM((all_slots, k_count, both, width), jnp.float32),
+            pltpu.SemaphoreType.DMA((2,)),
             pltpu.SemaphoreType.DMA((n_slots,)),
+            pltpu.SemaphoreType.DMA((all_slots,)),
+            pltpu.SemaphoreType.DMA((all_slots,)),
         ],
         compiler_params=PARAMS,
         cost_estimate=COST,
-        name="second_product",
-    )(flags, *lefts, *[ref for ref, _ in matched])
-
-
-def both_kernel(flags, *refs, first_slot, n_slots, columns, places, leads, turns, sums_at, stored, last):
+        name="stored_products",
+    )(flags, *operands)
+
+
+def both_kernel(flags, *refs, n_slots, columns, places, leads):
     n_chunks = len(columns)
-    w_refs = [refs[5 * i : 5 * i + 5] for i in range(n_chunks)]
-    rest = refs[5 * n_chunks :]
+    first = columns[0][0]
+    w_refs, rest = [refs[5 * i : 5 * i + 5] for i in range(n_chunks)], refs[5 * n_chunks :]
     of_end, of_mid, rest = rest[:n_slots], rest[n_slots : 2 * n_slots], rest[2 * n_slots :]
-    matched, rest = rest[:8], rest[8:]
-    sums_in, rest = rest[: len(sums_at)], rest[len(sums_at) :]
-    if stored:
-        left, rest = rest[0], rest[1:]
-    sums, flags_out, w_buf, m_buf, c_buf, left_buf, acc, w_sems, m_sems, c_sems, left_sems = rest
+    matched, sums_in, kept, given = rest[:8], rest[8], rest[9], rest[10]
+    w_buf, m_buf, c_buf, left_buf, acc, w_sems, m_sems, c_sems, sums_sem = rest[11:]
     depth, span = w_buf.shape[1:]
     _, k_count, both, _ = m_buf.shape
     n_tiles = span // STEP
-    copies, used = [], 0
-    for i in range(n_chunks):
-        for at in range(0, columns[i][1], STEP):
-            copies.append(w_copies(w_refs[i], places[i], turns, w_buf, at, used, STEP, w_sems.at[used // STEP]))
-            used += STEP
-    for copy in copies[0]:
-        copy.start()
-
-    def left_copy(s):
-        return pltpu.make_async_copy(left.at[s], left_buf.at[s % 2], left_sems.at[s % 2])
-
-    for s in range(n_slots):
+    turns = (0, 1, 2, 3)
+
+    tiles = [(i, at) for i in range(n_chunks) for at in range(0, columns[i][1], STEP)]
+
+    def w_tile(number):
+        i, at = tiles[number]
+        return w_copies(w_refs[i], places[i], turns, w_buf, at, number * STEP, STEP, w_sems.at[number])
+
+    def m_start(s):
         end_part, mid_part = part_of(of_end[s], leads[s], k_count), part_of(of_mid[s], leads[n_slots + s], k_count)
         m_copies(flags, turns, end_part, mid_part, m_buf.at[s], m_sems.at[s])
-        if s == 0 and stored:
-            left_copy(0).start()
-    for here in copies[1:]:
-        for copy in here:
+
+    def c_start(s):
+        matched_copies(flags, matched, leads[2 * n_slots :], c_buf, (s,), first, span, c_sems)
+
+    for copy in w_tile(0):
+        copy.start()
+    m_start(0)
+    for i in range(1, n_tiles):
+        for copy in w_tile(i):
             copy.start()
-    matched_copies(flags, matched, leads[2 * n_slots :], c_buf, first_slot, columns[0][0], span, c_sems)
-    keep_flags(flags, flags_out)
-    acc[...] = jnp.zeros(acc.shape, acc.dtype)
-    for at, one in zip(sums_at, sums_in):
-        count = one.shape[0]
-        acc[at : at + count] = acc[at : at + count] + one[...]
+    m_start(1)
+    c_start(0)
+    sums_copy = pltpu.make_async_copy(sums_in, acc, sums_sem)
+    sums_copy.start()
 
     def one_step(t, carry):
         s, tile_number = t // n_tiles, t % n_tiles
@@ -512,77 +537,83 @@
         @pl.when(tile_number == 0)
         def _():
             pltpu.make_async_copy(m_buf.at[s], m_buf.at[s], m_sems.at[s]).wait()
-            if stored:
-                left_copy(s).wait()
-
-                @pl.when(s + 1 < n_slots)
-                def _():
-                    left_copy(s + 1).start()
+
+        for j in range(n_slots - 1):
+            @pl.when(t == j * n_tiles)
+            def _():
+                if j + 2 < n_slots:
+                    m_start(j + 2)
+                c_start(j + 1)
 
         lhs = m_buf[s].reshape(k_count * both, depth)
         tile = left_tile(lhs, w_buf[0, :, pl.ds(start, STEP)], w_buf[1, :, pl.ds(start, STEP)], k_count, both)
-        if stored:
-            tile = tile + left_buf[s % 2, :, :, pl.ds(start, STEP)]
-        left_buf[s % 2, :, :, pl.ds(start, STEP)] = tile
+        left_buf[:, :, pl.ds(start, STEP)] = tile
+
+        @pl.when(t == n_tiles - 1)
+        def _():
+            sums_copy.wait()
 
         @pl.when(tile_number == n_tiles - 1)
         def _():
             matched_wait(c_buf, s, c_sems)
             for k in range(k_count):
-                acc[s, k] = acc[s, k] + times_matched(left_buf[s % 2, k], c_buf[s, (k + flags[3]) % k_count])
+                acc[s, k] = acc[s, k] + times_matched(left_buf[k], c_buf[s, (k + flags[3]) % k_count])
 
         return carry
 
     lax.fori_loop(0, n_slots * n_tiles, one_step, 0)
-    if last:
-        pairs = both // 2
-        sums[:, :, :, :pairs] = acc[:, :, :pairs, :pairs] - acc[:, :, pairs:, pairs:]
-        sums[:, :, :, pairs:] = acc[:, :, :pairs, pairs:] + acc[:, :, pairs:, :pairs]
-    else:
-        sums[...] = acc[...]
-
-
-def both_products(flags, chunks, turns, first_slot, n_slots, of_end, of_mid, matched, sums=(), left=None, last=False):
-    k_count = 4
-    both = of_end[0][0].shape[1]
-    depth = len(turns) * chunks[0][2][0].shape[0]
+    pairs, own_k = both // 2, k_count // 2
+    for s in range(n_slots):
+        above = jnp.where(flags[2] == 0, s, (n_slots - s) % n_slots)
+        for k in range(k_count):
+            terms = acc[s, k]
+            real_part = terms[:pairs, :pairs] - terms[pairs:, pairs:]
+            imaginary_part = terms[:pairs, pairs:] + terms[pairs:, :pairs]
+            block = jnp.concatenate([real_part, imaginary_part], axis=1)
+
+            @pl.when(flags[5] == k // own_k)
+            def _():
+                kept[above, k % own_k] = block
+
+            @pl.when(flags[5] != k // own_k)
+            def _():
+                given[above, k % own_k] = block
+
+
+def both_products(flags, chunks, of_end, of_mid, matched, sums):
+    n_slots, k_count, both, _ = sums.shape
+    depth = 4 * chunks[0][2][0].shape[0]
     columns = tuple((first, width) for first, width, _, _ in chunks)
     span = sum(width for _, width in columns)
-    slots = range(first_slot, first_slot + n_slots)
-    chosen = [of_end[s] for s in slots] + [of_mid[s] for s in slots] + list(matched)
-    operands = [ref for _, _, blocks, _ in chunks for ref in blocks] + [ref for ref, _ in chosen]
-    stored = [] if left is None else [left]
+    chosen = list(of_end) + list(of_mid) + list(matched)
+    operands = [ref for _, _, blocks, _ in chunks for ref in blocks] + [ref for ref, _ in chosen] + [sums]
+    halves = jax.ShapeDtypeStruct((n_slots, k_count // 2, both // 2, both), jnp.float32)
     return pl.pallas_call(
         functools.partial(
             both_kernel,
-            first_slot=first_slot,
             n_slots=n_slots,
             columns=columns,
             places=tuple(places for _, _, _, places in chunks),
             leads=tuple(lead for _, lead in chosen),
-            turns=turns,
-            sums_at=tuple(at for at, _ in sums),
-            stored=left is not None,
-            last=last,
         ),
-        out_shape=(jax.ShapeDtypeStruct((n_slots, k_count, both // 2 if last else both, both), jnp.float32), FLAGS),
-        in_specs=[IN_SMEM] + [ANYWHERE] * len(operands) + [IN_VMEM] * len(sums) + [ANYWHERE] * len(stored),
-        out_specs=(IN_VMEM, IN_SMEM),
+        out_shape=(halves, halves),
+        in_specs=[IN_SMEM] + [ANYWHERE] * len(operands),
+        out_specs=(IN_VMEM, IN_VMEM),
         scratch_shapes=[
             pltpu.VMEM((2, depth, span), jnp.bfloat16),
             pltpu.VMEM((n_slots, k_count, both, depth), jnp.bfloat16),
             pltpu.VMEM((n_slots, k_count, both, span), jnp.bfloat16),
-            pltpu.VMEM((2, k_count, both, span), jnp.float32),
+            pltpu.VMEM((k_count, both, span), jnp.float32),
             pltpu.VMEM((n_slots, k_count, both, both), jnp.float32),
             pltpu.SemaphoreType.DMA((span // STEP, 8)),
             pltpu.SemaphoreType.DMA((n_slots,)),
             pltpu.SemaphoreType.DMA((n_slots,)),
-            pltpu.SemaphoreType.DMA((2,)),
+            pltpu.SemaphoreType.DMA,
         ],
         compiler_params=PARAMS,
         cost_estimate=COST,
         name="both_products",
-    )(flags, *operands, *[one for _, one in sums], *stored)
+    )(flags, *operands)
 
 
 def turn_kernel(flags, first, second, first_turned, second_turned, turned_pair):
@@ -697,7 +728,11 @@
     panel_1 = to_x
     arrived_2 = sent_far(sent_2)
 
-    flags, pair_a, pair_b, mid_b = moves(flags, (arrived_2,), passing=(pair_a, pair_b, mid_b))
+    chunk_0 = (firsts[0], widths[0], (panel_0, x_0, y_0, y_0, x_0), (widths[0], 0, 0))
+    early_end, early_mid = [(own_second, 0), (pair_a, 0)], [(own_first, 0), (mid_ad, 0)]
+    left_0, flags = first_product(flags, [chunk_0], (0, 1, 2), 0, 2, early_end, early_mid)
+
+    flags, pair_b, mid_b = moves(flags, (arrived_2,), passing=(pair_b, mid_b))
     swapped_a = other_core(pair_a)
     pair_c, mid_c = mid_to_end(mid_b), mid_with_mid(pair_b)
     of_end = [(own_second, 0), (pair_a, 0), (pair_b, 0), None]
@@ -708,7 +743,7 @@
     x_2, y_2 = along_x(to_x), along_y(to_y)
     panel_2 = to_x
     chunk_0 = (firsts[0], widths[0], (panel_0, x_0, y_0, y_1, x_1), (widths[0], 2 * widths[1], 2 * widths[1]))
-    left_0, flags = first_product(flags, [chunk_0], every, 0, 3, of_end, of_mid)
+    left_2, flags = first_product(flags, [chunk_0], every, 2, 1, of_end, of_mid)
 
     flags, late_1, late_2 = moves(
         flags,
@@ -721,7 +756,6 @@
     matched = [(own_second, 0), (swapped_0, 0), (pair_a, 0), (swapped_a, 0)]
     matched += [(late_1, 0), (swapped_1, 0), (late_2, 0), (swapped_2, 0)]
     left_3, flags = first_product(flags, [chunk_0], every, 3, 1, of_end, of_mid)
-    sums_0, flags = second_product(flags, [left_0, left_3], matched, firsts[0], widths[0])
 
     shape = (rows, widths[2])
     flags, to_x, to_y = moves(
@@ -732,19 +766,14 @@
     )
     x_3, y_3 = along_x(to_x), along_y(to_y)
     chunk_1 = (firsts[1], widths[1], (panel_1, x_1, y_1, y_2, x_2), (widths[1], 2 * widths[2], 2 * widths[2]))
-    sums_1, flags = both_products(flags, [chunk_1], every, 0, 4, of_end, of_mid, matched, sums=((0, sums_0),))
+    sums_0, flags = stored_products(flags, chunk_0, of_end, of_mid, matched, [left_0, left_2, left_3])
     chunk_2 = (firsts[2], widths[2], (panel_2, x_2, y_2, y_3, x_3), (widths[2], 0, 0))
-    blocks, flags = both_products(
-        flags, [chunk_2], every, 0, 4, of_end, of_mid, matched, sums=((0, sums_1),), last=True
-    )
-
-    pairs_of_k = k_count // 2
-    mine = lax.dynamic_slice_in_dim(blocks, c * pairs_of_k, pairs_of_k, 1)
-    mine = mine + other_core(lax.dynamic_slice_in_dim(blocks, (1 - c) * pairs_of_k, pairs_of_k, 1))
-    up_order = jnp.where(half == 0, mine, jnp.stack([mine[0], mine[3], mine[2], mine[1]]))
-    total = jnp.stack([up_order[0], up_order[3]])
+    mine, given = both_products(flags, [chunk_1, chunk_2], of_end, of_mid, matched, sums_0)
+
+    mine = mine + other_core(given)
+    total = jnp.stack([mine[0], mine[3]])
     for shift in (1, 2, 3):
-        sent = jnp.stack([up_order[shift], up_order[shift - 1]])
+        sent = jnp.stack([mine[shift], mine[shift - 1]])
         total = total + moved(sent, lambda z, b, c: ((z + shift) % 4, b, c))
     theirs = other_core(total)
     total = jnp.where(c == 0, jnp.concatenate([total, theirs], axis=1), jnp.concatenate([theirs, total], axis=1))

time: 289 us -> 283 us (0.979)
  local copies, waits for them, and re-layouts: 11.4 us -> 2.02 us
  starting transfers between devices: 72.8 us -> 66.3 us
  Pallas kernels: 120 us -> 126 us
  waiting for transfers between devices: 78.2 us -> 81.7 us
    unnamed x25 -> x3, local copies, waits for them, and re-layouts: 9.14 us -> 0.78 us
    ppermute x26, starting transfers between devices: 72.8 us -> 66.3 us  [moved(): return lax.ppermute(value, AXES, pairs)]
    pallas_call x2 -> x3, Pallas kernels: 35.6 us -> 39.4 us  [first_product(): pl.pallas_call(functools.partial(first_kernel, first_slot=first_slot, n_s...]
    ppermute x26, waiting for transfers between devices: 78.2 us -> 81.7 us  [moved(): return lax.ppermute(value, AXES, pairs)]
    pallas_call x3 -> x2, Pallas kernels: 51.1 us -> 53 us  [the longest x1 35.5 us: both_products(): pl.pallas_call(functools.partial(both_kernel, n_slots=n_slots, columns=co...]
  transfers between devices with their start and end apart: 26 -> 26, of which waited for: 9 -> 12; matrix products, arithmetic and copies ran while one was open for 0% -> 0% of each run, Pallas kernels for 33% -> 32%
where the time goes in v4:
time: 283 us; the launch traced here: 281 us
  Pallas kernels  126 us (45%)
  waiting for transfers between devices  81.7 us (29%)
  starting transfers between devices  66.3 us (23%)
  between operations  2.91 us (1%)
    ppermute x26, waiting for transfers between devices, moved(): return lax.ppermute(value, AXES, pairs)  81.7 us
    ppermute x26, starting transfers between devices, moved(): return lax.ppermute(value, AXES, pairs)  66.3 us
    pallas_call x3, Pallas kernels, first_product(): pl.pallas_call(functools.partial(first_kernel, first_slot=first_slot, n_s...  39.4 us
    pallas_call x1, Pallas kernels, both_products(): pl.pallas_call(functools.partial(both_kernel, n_slots=n_slots, columns=co...  35.5 us
    pallas_call x8, Pallas kernels, moves(): pl.pallas_call(functools.partial(moves_kernel, plan=tuple(plan), n_source...  27.3 us
    pallas_call x1, Pallas kernels, stored_products(): pl.pallas_call(functools.partial(stored_kernel, n_slots=n_slots, n_lefts=...  17.5 us
    pallas_call x1, Pallas kernels, turned_parts(): pl.pallas_call(turn_kernel, out_shape=(jax.ShapeDtypeStruct((k_count, bot...  5.8 us
  transfers between devices with their start and end apart: 26, of which 12 were waited for; matrix products, arithmetic and copies ran while one was open for 0% of the time, Pallas kernels for 32%

profile of v4, /device:TPU:0, one launch (start us, length us, event | category | flops | bytes accessed | tf_op | source)
XLA Modules:
  0.0 281.2 jit_solution(5635174888549791302)
XLA Ops:
  4.6 2.0 collective-permute-start
  6.7 5.8 %turned_parts.1 = (bf16[4,128,1536]{2,1,0:T(8,128)(2,1)}, bf16[4,128,1536]{2,1,0:T(8,128)(2,1)}, bf16[2,4,128,1536]{3,2,1,0:T(8,128)(2,1)}) custom-call(s32[8]{0:T(128)} %get-tuple-element.40.flags, bf16[4,6144,128]{2,1,0:T(8,128)(2,1)} %second.1, bf16[4,6144,128]{2,1,0:T(8,128)(2,1)} %second.1), custom_call_target="tpu_custom_call" | custom-call | flops 1000 | bytes 1000 | tf_op jit(solution)/shard_map/turned_parts/pallas_call | solution.py:634
  12.5 6.0 %collective-permute-start.1 = (bf16[4,128,1536]{2,1,0:T(8,128)(2,1)}, bf16[4,128,1536]{2,1,0:T(8,128)(2,1)}, u32[]{:S(2)}, u32[]{:S(2)}) collective-permute-start(bf16[4,128,1536]{2,1,0:T(8,128)(2,1)} %get-tuple-element.42.refs_0_.refs_5_.refs_9_.refs_10_.refs_18_), channel_id=1, source_target_pairs={{0,1},{1,0},{2,3},{3,2},{4,5},{5,4},{6,7},{7,6},{8,9},{9,8},{10,11... | collective-permute-start | bytes 4718600 | tf_op jit(solution)/shard_map/ppermute | solution.py:89
  18.5 2.3 collective-permute-start.2
  21.9 4.0 %moves.9 = (bf16[384,3072]{1,0:T(8,128)(2,1)}, bf16[384,1536]{1,0:T(8,128)(2,1)}, s32[8]{0:T(128)}) custom-call(s32[8]{0:T(128)} %get-tuple-element.40.flags, bf16[2,384,3072]{2,1,0:T(8,128)(2,1)} %refs_1_.7, bf16[2,384,3072]{2,1,0:T(8,128)(2,1)} %refs_1_.7, bf16[384,3072]{1,0:T(8,128)(2,1)} %collective-permute-done.refs_2_, bf16[2,384,3072]{2,1,0:T(8,128)(2,1)} %refs_1_.7, ...), custom_call_target="tpu_custom_call" | custom-call | flops 1000 | bytes 1000 | tf_op jit(solution)/shard_map/moves/pallas_call | solution.py:214
  25.9 1.6 collective-permute-start.5
  29.0 20.0 %collective-permute-start.3 = (bf16[4,128,1536]{2,1,0:T(8,128)(2,1)}, bf16[4,128,1536]{2,1,0:T(8,128)(2,1)}, u32[]{:S(2)}, u32[]{:S(2)}) collective-permute-start(bf16[4,128,1536]{2,1,0:T(8,128)(2,1)} %get-tuple-element.45.refs_7_.refs_14_), channel_id=1, source_target_pairs={{0,8},{1,9},{2,10},{3,11},{4,12},{5,13},{6,14},{7,15},{8,0},{9,1},... | collective-permute-start | bytes 4718600 | tf_op jit(solution)/shard_map/ppermute | solution.py:89
  49.0 1.7 collective-permute-start.4
  50.7 33.5 %collective-permute-done.3.refs_2_.refs_6_.refs_11_.refs_20_ = bf16[4,128,1536]{2,1,0:T(8,128)(2,1)} collective-permute-done((bf16[4,128,1536]{2,1,0:T(8,128)(2,1)}, bf16[4,128,1536]{2,1,0:T(8,128)(2,1)}, u32[]{:S(2)}, u32[]{:S(2)}) %collective-permute-start.3) | collective-permute-done | bytes 1572896 | tf_op jit(solution)/shard_map/ppermute | solution.py:89
  84.2 4.3 %moves.10 = (bf16[4,128,1536]{2,1,0:T(8,128)(2,1)}, bf16[4,128,1536]{2,1,0:T(8,128)(2,1)}, s32[8]{0:T(128)}) custom-call(s32[8]{0:T(128)} %get-tuple-element.43.flags, bf16[4,128,1536]{2,1,0:T(8,128)(2,1)} %get-tuple-element.42.refs_0_.refs_5_.refs_9_.refs_10_.refs_18_, bf16[8,128,1536]{2,1,0:T(8,128)(2,1)} %collective-permute-done.2.refs_1_.refs_8_.refs_15_, ...), custom_call_target="tpu_custom_call" | custom-call | flops 1000 | bytes 1000 | tf_op jit(solution)/shard_map/moves/pallas_call | solution.py:214
  88.5 8.0 %collective-permute-start.8 = (bf16[4,128,1536]{2,1,0:T(8,128)(2,1)}, bf16[4,128,1536]{2,1,0:T(8,128)(2,1)}, u32[]{:S(2)}, u32[]{:S(2)}) collective-permute-start(bf16[4,128,1536]{2,1,0:T(8,128)(2,1)} %get-tuple-element.53), channel_id=1, source_target_pairs={{0,8},{1,9},{2,10},{3,11},{4,12},{5,13},{6,14},{7,15},{8,0},{9,1},... | collective-permute-start | bytes 4718600 | tf_op jit(solution)/shard_map/ppermute | solution.py:89
  96.5 1.9 collective-permute-start.9
  98.4 4.6 %moves.11 = (bf16[384,3072]{1,0:T(8,128)(2,1)}, bf16[384,3072]{1,0:T(8,128)(2,1)}, bf16[384,1536]{1,0:T(8,128)(2,1)}, s32[8]{0:T(128)}) custom-call(s32[8]{0:T(128)} %get-tuple-element.46.flags, bf16[2,384,3072]{2,1,0:T(8,128)(2,1)} %refs_1_.7, bf16[2,384,3072]{2,1,0:T(8,128)(2,1)} %refs_1_.7, ...), custom_call_target="tpu_custom_call", output_to_operand_aliasing={{2}: (6, {})} | custom-call | flops 1000 | bytes 1000 | tf_op jit(solution)/shard_map/moves/pallas_call | solution.py:214
  103.1 1.6 collective-permute-start.10
  106.1 1.7 collective-permute-start.7
  107.9 15.7 %first_product.3 = (f32[2,4,128,1536]{3,2,1,0:T(8,128)}, s32[8]{0:T(128)}) custom-call(s32[8]{0:T(128)} %get-tuple-element.50.flags, bf16[384,3072]{1,0:T(8,128)(2,1)} %get-tuple-element.48.refs_0_, bf16[384,3072]{1,0:T(8,128)(2,1)} %collective-permute-done.6.refs_4_.refs_1_, bf16[384,3072]{1,0:T(8,128)(2,1)} %collective-permute-done.5.refs_3_.refs_2_, ...), custom_call_target="tpu_custom_call" | custom-call | flops 1000 | bytes 1000 | tf_op jit(solution)/shard_map/first_product/pallas_call | solution.py:373
  123.6 8.1 %collective-permute-done.8.refs_1_ = bf16[4,128,1536]{2,1,0:T(8,128)(2,1)} collective-permute-done((bf16[4,128,1536]{2,1,0:T(8,128)(2,1)}, bf16[4,128,1536]{2,1,0:T(8,128)(2,1)}, u32[]{:S(2)}, u32[]{:S(2)}) %collective-permute-start.8) | collective-permute-done | bytes 1572896 | tf_op jit(solution)/shard_map/ppermute | solution.py:89
  134.2 1.8 collective-permute-start.13
  136.1 19.9 %collective-permute-done.10.refs_3_.refs_2_ = bf16[384,3072]{1,0:T(8,128)(2,1)} collective-permute-done((bf16[384,3072]{1,0:T(8,128)(2,1)}, bf16[384,3072]{1,0:T(8,128)(2,1)}, u32[]{:S(2)}, u32[]{:S(2)}) %collective-permute-start.10) | collective-permute-done | bytes 2359328 | tf_op jit(solution)/shard_map/ppermute | solution.py:89
  157.2 4.2 %moves.13 = (bf16[384,2304]{1,0:T(8,128)(2,1)}, bf16[384,2304]{1,0:T(8,128)(2,1)}, s32[8]{0:T(128)}) custom-call(s32[8]{0:T(128)} %get-tuple-element.55.flags, bf16[2,384,3072]{2,1,0:T(8,128)(2,1)} %refs_1_.7, bf16[2,384,3072]{2,1,0:T(8,128)(2,1)} %refs_1_.7, bf16[384,1536]{1,0:T(8,128)(2,1)} %collective-permute-done.7.refs_0_.refs_2_, ...), custom_call_target="tpu_custom_call" | custom-call | flops 1000 | bytes 1000 | tf_op jit(solution)/shard_map/moves/pallas_call | solution.py:214
  163.4 11.9 %first_product.4 = (f32[1,4,128,1536]{3,2,1,0:T(8,128)}, s32[8]{0:T(128)}) custom-call(s32[8]{0:T(128)} %get-tuple-element.58.flags, bf16[384,3072]{1,0:T(8,128)(2,1)} %get-tuple-element.48.refs_0_, bf16[384,3072]{1,0:T(8,128)(2,1)} %collective-permute-done.6.refs_4_.refs_1_, bf16[384,3072]{1,0:T(8,128)(2,1)} %collective-permute-done.5.refs_3_.refs_2_, ...), custom_call_target="tpu_custom_call" | custom-call | flops 1000 | bytes 1000 | tf_op jit(solution)/shard_map/first_product/pallas_call | solution.py:373
  175.4 7.9 %collective-permute-done.12.refs_2_.refs_5_.refs_13_ = bf16[4,128,1536]{2,1,0:T(8,128)(2,1)} collective-permute-done((bf16[4,128,1536]{2,1,0:T(8,128)(2,1)}, bf16[4,128,1536]{2,1,0:T(8,128)(2,1)}, u32[]{:S(2)}, u32[]{:S(2)}) %collective-permute-start.12) | collective-permute-done | bytes 1572896 | tf_op jit(solution)/shard_map/ppermute | solution.py:89
  183.3 4.4 %moves.14 = (bf16[4,128,1536]{2,1,0:T(8,128)(2,1)}, bf16[4,128,1536]{2,1,0:T(8,128)(2,1)}, s32[8]{0:T(128)}) custom-call(s32[8]{0:T(128)} %get-tuple-element.61.flags, bf16[4,128,1536]{2,1,0:T(8,128)(2,1)} %get-tuple-element.59.refs_5_.refs_0_.refs_6_.refs_12_.refs_17_, bf16[8,128,1536]{2,1,0:T(8,128)(2,1)} %collective-permute-done.2.refs_1_.refs_8_.refs_15_, ...), custom_call_target="tpu_custom_call" | custom-call | flops 1000 | bytes 1000 | tf_op jit(solution)/shard_map/moves/pallas_call | solution.py:214
  188.2 11.8 %first_product.5 = (f32[1,4,128,1536]{3,2,1,0:T(8,128)}, s32[8]{0:T(128)}) custom-call(s32[8]{0:T(128)} %get-tuple-element.62.flags, bf16[384,3072]{1,0:T(8,128)(2,1)} %get-tuple-element.48.refs_0_, bf16[384,3072]{1,0:T(8,128)(2,1)} %collective-permute-done.6.refs_4_.refs_1_, bf16[384,3072]{1,0:T(8,128)(2,1)} %collective-permute-done.5.refs_3_.refs_2_, ...), custom_call_target="tpu_custom_call" | custom-call | flops 1000 | bytes 1000 | tf_op jit(solution)/shard_map/first_product/pallas_call | solution.py:373
  200.9 3.3 %moves.15 = (bf16[384,768]{1,0:T(8,128)(2,1)}, bf16[384,768]{1,0:T(8,128)(2,1)}, s32[8]{0:T(128)}) custom-call(s32[8]{0:T(128)} %get-tuple-element.63.flags, bf16[384,2304]{1,0:T(8,128)(2,1)} %collective-permute-done.15.refs_0_.refs_3_.refs_7_, bf16[384,2304]{1,0:T(8,128)(2,1)} %collective-permute-done.16.refs_1_.refs_4_.refs_6_), custom_call_target="tpu_custom_call" | custom-call | flops 1000 | bytes 1000 | tf_op jit(solution)/shard_map/moves/pallas_call | solution.py:214
  204.2 1.5 collective-permute-start.19
  207.2 17.5 %stored_products.1 = (f32[4,4,128,128]{3,2,1,0:T(8,128)}, s32[8]{0:T(128)}) custom-call(s32[8]{0:T(128)} %get-tuple-element.66.flags, bf16[384,3072]{1,0:T(8,128)(2,1)} %get-tuple-element.48.refs_0_, bf16[384,3072]{1,0:T(8,128)(2,1)} %collective-permute-done.6.refs_4_.refs_1_, bf16[384,3072]{1,0:T(8,128)(2,1)} %collective-permute-done.5.refs_3_.refs_2_, ...), custom_call_target="tpu_custom_call" | custom-call | flops 1000 | bytes 1000 | tf_op jit(solution)/shard_map/stored_products/pallas_call | solution.py:464
  224.8 35.5 %both_products.1 = (f32[4,2,64,128]{3,2,1,0:T(8,128)}, f32[4,2,64,128]{3,2,1,0:T(8,128)}) custom-call(s32[8]{0:T(128)} %get-tuple-element.72.flags, bf16[384,3072]{1,0:T(8,128)(2,1)} %get-tuple-element.57.refs_0_, bf16[384,3072]{1,0:T(8,128)(2,1)} %collective-permute-done.11.refs_4_.refs_1_, bf16[384,3072]{1,0:T(8,128)(2,1)} %collective-permute-done.10.refs_3_.refs_2_, ...), custom_call_target="tpu_custom_call" | custom-call | flops 1000 | bytes 1000 | tf_op jit(solution)/shard_map/both_products/pallas_call | solution.py:591
  260.3 1.7 collective-permute-done.21
  263.1 4.4 %collective-permute-start.22 = (f32[2,2,64,128]{3,2,1,0:T(8,128)S(1)}, f32[2,2,64,128]{3,2,1,0:T(8,128)S(1)}, u32[]{:S(2)}, u32[]{:S(2)}) collective-permute-start(f32[2,2,64,128]{3,2,1,0:T(8,128)S(1)} %get-tuple-element.88), channel_id=1, source_target_pairs={{0,8},{1,9},{2,10},{3,11},{4,12},{5,13},{6,14},{7,15},{8,16},{9,17... | collective-permute-start | bytes 393224 | tf_op jit(solution)/shard_map/ppermute | solution.py:89
  267.8 2.8 %collective-permute-start.24 = (f32[2,2,64,128]{3,2,1,0:T(8,128)S(1)}, f32[2,2,64,128]{3,2,1,0:T(8,128)S(1)}, u32[]{:S(2)}, u32[]{:S(2)}) collective-permute-start(f32[2,2,64,128]{3,2,1,0:T(8,128)S(1)} %get-tuple-element.90), channel_id=1, source_target_pairs={{0,24},{1,25},{2,26},{3,27},{4,28},{5,29},{6,30},{7,31},{8,0},{9,1... | collective-permute-start | bytes 393224 | tf_op jit(solution)/shard_map/ppermute | solution.py:89
  271.4 5.4 %collective-permute-done.23 = f32[2,2,64,128]{3,2,1,0:T(8,128)S(1)} collective-permute-done((f32[2,2,64,128]{3,2,1,0:T(8,128)S(1)}, f32[2,2,64,128]{3,2,1,0:T(8,128)S(1)}, u32[]{:S(2)}, u32[]{:S(2)}) %collective-permute-start.23) | collective-permute-done | bytes 131104 | tf_op jit(solution)/shard_map/ppermute | solution.py:89
  (53 shorter events, 21.2 us)
Async XLA Ops:
  4.6 17.3 %collective-permute-start = (bf16[384,3072]{1,0:T(8,128)(2,1)}, bf16[384,3072]{1,0:T(8,128)(2,1)}, u32[]{:S(2)}, u32[]{:S(2)}) collective-permute-start(bf16[384,3072]{1,0:T(8,128)(2,1)} %get-tuple-element.41), channel_id=1, source_target_pairs={{1,8},{3,10},{5,12},{7,14},{8,1},{10,3},{12,5},{14,7},{17,24},{19,... | collective-permute-start | bytes 7077896 | tf_op jit(solution)/shard_map/ppermute | solution.py:89
  12.5 9.4 %collective-permute-start.1 = (bf16[4,128,1536]{2,1,0:T(8,128)(2,1)}, bf16[4,128,1536]{2,1,0:T(8,128)(2,1)}, u32[]{:S(2)}, u32[]{:S(2)}) collective-permute-start(bf16[4,128,1536]{2,1,0:T(8,128)(2,1)} %get-tuple-element.42.refs_0_.refs_5_.refs_9_.refs_10_.refs_18_), channel_id=1, source_target_pairs={{0,1},{1,0},{2,3},{3,2},{4,5},{5,4},{6,7},{7,6},{8,9},{9,8},{10,11... | collective-permute-start | bytes 4718600 | tf_op jit(solution)/shard_map/ppermute | solution.py:89
  18.5 65.7 %collective-permute-start.2 = (bf16[8,128,1536]{2,1,0:T(8,128)(2,1)}, bf16[8,128,1536]{2,1,0:T(8,128)(2,1)}, u32[]{:S(2)}, u32[]{:S(2)}) collective-permute-start(bf16[8,128,1536]{2,1,0:T(8,128)(2,1)} %bitcast.27), channel_id=1, source_target_pairs={{8,16},{9,17},{10,18},{11,19},{12,20},{13,21},{14,22},{15,23},{16,... | collective-permute-start | bytes 9437192 | tf_op jit(solution)/shard_map/ppermute | solution.py:89
  25.9 72.5 %collective-permute-start.5 = (bf16[384,3072]{1,0:T(8,128)(2,1)}, bf16[384,3072]{1,0:T(8,128)(2,1)}, u32[]{:S(2)}, u32[]{:S(2)}) collective-permute-start(bf16[384,3072]{1,0:T(8,128)(2,1)} %get-tuple-element.48.refs_0_), channel_id=1, source_target_pairs={{0,4},{1,5},{2,6},{3,7},{4,0},{5,1},{6,2},{7,3},{8,12},{9,13},{10,... | collective-permute-start | bytes 7077896 | tf_op jit(solution)/shard_map/ppermute | solution.py:89
  27.5 70.9 %collective-permute-start.6 = (bf16[384,3072]{1,0:T(8,128)(2,1)}, bf16[384,3072]{1,0:T(8,128)(2,1)}, u32[]{:S(2)}, u32[]{:S(2)}) collective-permute-start(bf16[384,3072]{1,0:T(8,128)(2,1)} %get-tuple-element.48.refs_0_), channel_id=1, source_target_pairs={{0,2},{1,3},{2,0},{3,1},{4,6},{5,7},{6,4},{7,5},{8,10},{9,11},{10,... | collective-permute-start | bytes 7077896 | tf_op jit(solution)/shard_map/ppermute | solution.py:89
  29.0 55.2 %collective-permute-start.3 = (bf16[4,128,1536]{2,1,0:T(8,128)(2,1)}, bf16[4,128,1536]{2,1,0:T(8,128)(2,1)}, u32[]{:S(2)}, u32[]{:S(2)}) collective-permute-start(bf16[4,128,1536]{2,1,0:T(8,128)(2,1)} %get-tuple-element.45.refs_7_.refs_14_), channel_id=1, source_target_pairs={{0,8},{1,9},{2,10},{3,11},{4,12},{5,13},{6,14},{7,15},{8,0},{9,1},... | collective-permute-start | bytes 4718600 | tf_op jit(solution)/shard_map/ppermute | solution.py:89
  49.0 49.4 %collective-permute-start.4 = (bf16[384,1536]{1,0:T(8,128)(2,1)}, bf16[384,1536]{1,0:T(8,128)(2,1)}, u32[]{:S(2)}, u32[]{:S(2)}) collective-permute-start(bf16[384,1536]{1,0:T(8,128)(2,1)} %get-tuple-element.47), channel_id=1, source_target_pairs={{1,8},{3,10},{5,12},{7,14},{8,1},{10,3},{12,5},{14,7},{17,24},{19,... | collective-permute-start | bytes 3538952 | tf_op jit(solution)/shard_map/ppermute | solution.py:89
  88.5 43.2 %collective-permute-start.8 = (bf16[4,128,1536]{2,1,0:T(8,128)(2,1)}, bf16[4,128,1536]{2,1,0:T(8,128)(2,1)}, u32[]{:S(2)}, u32[]{:S(2)}) collective-permute-start(bf16[4,128,1536]{2,1,0:T(8,128)(2,1)} %get-tuple-element.53), channel_id=1, source_target_pairs={{0,8},{1,9},{2,10},{3,11},{4,12},{5,13},{6,14},{7,15},{8,0},{9,1},... | collective-permute-start | bytes 4718600 | tf_op jit(solution)/shard_map/ppermute | solution.py:89
  96.5 35.2 %collective-permute-start.9 = (bf16[4,128,1536]{2,1,0:T(8,128)(2,1)}, bf16[4,128,1536]{2,1,0:T(8,128)(2,1)}, u32[]{:S(2)}, u32[]{:S(2)}) collective-permute-start(bf16[4,128,1536]{2,1,0:T(8,128)(2,1)} %get-tuple-element.54), channel_id=1, source_target_pairs={{8,16},{9,17},{10,18},{11,19},{12,20},{13,21},{14,22},{15,23},{16,... | collective-permute-start | bytes 4718600 | tf_op jit(solution)/shard_map/ppermute | solution.py:89
  103.1 52.9 %collective-permute-start.10 = (bf16[384,3072]{1,0:T(8,128)(2,1)}, bf16[384,3072]{1,0:T(8,128)(2,1)}, u32[]{:S(2)}, u32[]{:S(2)}) collective-permute-start(bf16[384,3072]{1,0:T(8,128)(2,1)} %get-tuple-element.56), channel_id=1, source_target_pairs={{0,4},{1,5},{2,6},{3,7},{4,0},{5,1},{6,2},{7,3},{8,12},{9,13},{10,... | collective-permute-start | bytes 7077896 | tf_op jit(solution)/shard_map/ppermute | solution.py:89
  104.7 52.5 %collective-permute-start.11 = (bf16[384,3072]{1,0:T(8,128)(2,1)}, bf16[384,3072]{1,0:T(8,128)(2,1)}, u32[]{:S(2)}, u32[]{:S(2)}) collective-permute-start(bf16[384,3072]{1,0:T(8,128)(2,1)} %get-tuple-element.57.refs_0_), channel_id=1, source_target_pairs={{0,2},{1,3},{2,0},{3,1},{4,6},{5,7},{6,4},{7,5},{8,10},{9,11},{10,... | collective-permute-start | bytes 7077896 | tf_op jit(solution)/shard_map/ppermute | solution.py:89
  106.1 25.6 %collective-permute-start.7 = (bf16[384,1536]{1,0:T(8,128)(2,1)}, bf16[384,1536]{1,0:T(8,128)(2,1)}, u32[]{:S(2)}, u32[]{:S(2)}) collective-permute-start(bf16[384,1536]{1,0:T(8,128)(2,1)} %get-tuple-element.52), channel_id=1, source_target_pairs={{1,8},{3,10},{5,12},{7,14},{8,1},{10,3},{12,5},{14,7},{17,24},{19,... | collective-permute-start | bytes 3538952 | tf_op jit(solution)/shard_map/ppermute | solution.py:89
  131.7 43.7 %collective-permute-start.14 = (bf16[4,128,1536]{2,1,0:T(8,128)(2,1)}, bf16[4,128,1536]{2,1,0:T(8,128)(2,1)}, u32[]{:S(2)}, u32[]{:S(2)}) collective-permute-start(bf16[4,128,1536]{2,1,0:T(8,128)(2,1)} %collective-permute-done.3.refs_2_.refs_6_.refs_11_.refs_20_), channel_id=1, source_target_pairs={{0,1},{1,0},{2,3},{3,2},{4,5},{5,4},{6,7},{7,6},{8,9},{9,8},{10,11... | collective-permute-start | bytes 4718600 | tf_op jit(solution)/shard_map/ppermute | solution.py:89
  132.9 50.3 %collective-permute-start.12 = (bf16[4,128,1536]{2,1,0:T(8,128)(2,1)}, bf16[4,128,1536]{2,1,0:T(8,128)(2,1)}, u32[]{:S(2)}, u32[]{:S(2)}) collective-permute-start(bf16[4,128,1536]{2,1,0:T(8,128)(2,1)} %get-tuple-element.60.refs_6_.refs_16_), channel_id=1, source_target_pairs={{8,0},{9,1},{10,2},{11,3},{12,4},{13,5},{14,6},{15,7},{16,24},{17,... | collective-permute-start | bytes 4718600 | tf_op jit(solution)/shard_map/ppermute | solution.py:89
  134.2 49.0 %collective-permute-start.13 = (bf16[4,128,1536]{2,1,0:T(8,128)(2,1)}, bf16[4,128,1536]{2,1,0:T(8,128)(2,1)}, u32[]{:S(2)}, u32[]{:S(2)}) collective-permute-start(bf16[4,128,1536]{2,1,0:T(8,128)(2,1)} %get-tuple-element.59.refs_5_.refs_0_.refs_6_.refs_12_.refs_17_), channel_id=1, source_target_pairs={{8,16},{9,17},{10,18},{11,19},{12,20},{13,21},{14,22},{15,23},{16,... | collective-permute-start | bytes 4718600 | tf_op jit(solution)/shard_map/ppermute | solution.py:89
  161.4 39.2 %collective-permute-start.15 = (bf16[384,2304]{1,0:T(8,128)(2,1)}, bf16[384,2304]{1,0:T(8,128)(2,1)}, u32[]{:S(2)}, u32[]{:S(2)}) collective-permute-start(bf16[384,2304]{1,0:T(8,128)(2,1)} %get-tuple-element.64), channel_id=1, source_target_pairs={{0,4},{1,5},{2,6},{3,7},{4,0},{5,1},{6,2},{7,3},{8,12},{9,13},{10,... | collective-permute-start | bytes 5308424 | tf_op jit(solution)/shard_map/ppermute | solution.py:89
  161.9 38.9 %collective-permute-start.16 = (bf16[384,2304]{1,0:T(8,128)(2,1)}, bf16[384,2304]{1,0:T(8,128)(2,1)}, u32[]{:S(2)}, u32[]{:S(2)}) collective-permute-start(bf16[384,2304]{1,0:T(8,128)(2,1)} %get-tuple-element.65.refs_5_), channel_id=1, source_target_pairs={{0,2},{1,3},{2,0},{3,1},{4,6},{5,7},{6,4},{7,5},{8,10},{9,11},{10,... | collective-permute-start | bytes 5308424 | tf_op jit(solution)/shard_map/ppermute | solution.py:89
  187.6 19.6 %collective-permute-start.17 = (bf16[4,128,1536]{2,1,0:T(8,128)(2,1)}, bf16[4,128,1536]{2,1,0:T(8,128)(2,1)}, u32[]{:S(2)}, u32[]{:S(2)}) collective-permute-start(bf16[4,128,1536]{2,1,0:T(8,128)(2,1)} %get-tuple-element.67.refs_13_.refs_22_), channel_id=1, source_target_pairs={{0,1},{1,0},{2,3},{3,2},{4,5},{5,4},{6,7},{7,6},{8,9},{9,8},{10,11... | collective-permute-start | bytes 4718600 | tf_op jit(solution)/shard_map/ppermute | solution.py:89
  187.9 19.3 %collective-permute-start.18 = (bf16[4,128,1536]{2,1,0:T(8,128)(2,1)}, bf16[4,128,1536]{2,1,0:T(8,128)(2,1)}, u32[]{:S(2)}, u32[]{:S(2)}) collective-permute-start(bf16[4,128,1536]{2,1,0:T(8,128)(2,1)} %get-tuple-element.68.refs_15_.refs_24_), channel_id=1, source_target_pairs={{0,1},{1,0},{2,3},{3,2},{4,5},{5,4},{6,7},{7,6},{8,9},{9,8},{10,11... | collective-permute-start | bytes 4718600 | tf_op jit(solution)/shard_map/ppermute | solution.py:89
  204.2 20.6 %collective-permute-start.19 = (bf16[384,768]{1,0:T(8,128)(2,1)}, bf16[384,768]{1,0:T(8,128)(2,1)}, u32[]{:S(2)}, u32[]{:S(2)}) collective-permute-start(bf16[384,768]{1,0:T(8,128)(2,1)} %get-tuple-element.73), channel_id=1, source_target_pairs={{0,4},{1,5},{2,6},{3,7},{4,0},{5,1},{6,2},{7,3},{8,12},{9,13},{10,... | collective-permute-start | bytes 1769480 | tf_op jit(solution)/shard_map/ppermute | solution.py:89
  205.7 19.0 %collective-permute-start.20 = (bf16[384,768]{1,0:T(8,128)(2,1)}, bf16[384,768]{1,0:T(8,128)(2,1)}, u32[]{:S(2)}, u32[]{:S(2)}) collective-permute-start(bf16[384,768]{1,0:T(8,128)(2,1)} %get-tuple-element.74), channel_id=1, source_target_pairs={{0,2},{1,3},{2,0},{3,1},{4,6},{5,7},{6,4},{7,5},{8,10},{9,11},{10,... | collective-permute-start | bytes 1769480 | tf_op jit(solution)/shard_map/ppermute | solution.py:89
  260.3 1.8 collective-permute-start.21
  262.1 16.2 %copy-start = (s32[64]{0:T(128)S(1)}, s32[64]{0:T(128)}, u32[]{:S(2)}) copy-start(s32[64]{0:T(128)} %param.7) | copy-start | bytes 772
  263.1 8.2 %collective-permute-start.22 = (f32[2,2,64,128]{3,2,1,0:T(8,128)S(1)}, f32[2,2,64,128]{3,2,1,0:T(8,128)S(1)}, u32[]{:S(2)}, u32[]{:S(2)}) collective-permute-start(f32[2,2,64,128]{3,2,1,0:T(8,128)S(1)} %get-tuple-element.88), channel_id=1, source_target_pairs={{0,8},{1,9},{2,10},{3,11},{4,12},{5,13},{6,14},{7,15},{8,16},{9,17... | collective-permute-start | bytes 393224 | tf_op jit(solution)/shard_map/ppermute | solution.py:89
  267.5 9.3 %collective-permute-start.23 = (f32[2,2,64,128]{3,2,1,0:T(8,128)S(1)}, f32[2,2,64,128]{3,2,1,0:T(8,128)S(1)}, u32[]{:S(2)}, u32[]{:S(2)}) collective-permute-start(f32[2,2,64,128]{3,2,1,0:T(8,128)S(1)} %get-tuple-element.89), channel_id=1, source_target_pairs={{0,16},{1,17},{2,18},{3,19},{4,20},{5,21},{6,22},{7,23},{8,24},{9,... | collective-permute-start | bytes 393224 | tf_op jit(solution)/shard_map/ppermute | solution.py:89
  267.8 9.0 %collective-permute-start.24 = (f32[2,2,64,128]{3,2,1,0:T(8,128)S(1)}, f32[2,2,64,128]{3,2,1,0:T(8,128)S(1)}, u32[]{:S(2)}, u32[]{:S(2)}) collective-permute-start(f32[2,2,64,128]{3,2,1,0:T(8,128)S(1)} %get-tuple-element.90), channel_id=1, source_target_pairs={{0,24},{1,25},{2,26},{3,27},{4,28},{5,29},{6,30},{7,31},{8,0},{9,1... | collective-permute-start | bytes 393224 | tf_op jit(solution)/shard_map/ppermute | solution.py:89
  276.8 1.4 collective-permute-start.25

commit v5 on v4

--- a/solution.py
+++ b/solution.py
@@ -405,7 +405,6 @@
     lefts, (sums, flags_out, w_buf, m_buf, c_buf, left_buf, w_sems, m_sems, c_sems, left_sems) = rest[:n_lefts], rest[n_lefts:]
     depth = w_buf.shape[1]
     all_slots, k_count, both, _ = c_buf.shape
-    n_tiles = width // STEP
     sources = [left.at[i] for left in lefts for i in range(left.shape[0])]
     w_loads = w_copies(w_refs, places, (3,), w_buf, 0, 0, width, w_sems)
     for copy in w_loads:
@@ -425,26 +424,30 @@
         for k in range(k_count):
             sums[s, k] = times_matched(left_buf[s, k], c_buf[s, (k + flags[3]) % k_count])
 
+    wide = WIDE_STEP if width % WIDE_STEP == 0 else STEP
+    n_steps = width // wide
+
     def one_step(t, carry):
-        s, tile_number = t // n_tiles, t % n_tiles
-        start = pl.multiple_of(tile_number * STEP, STEP)
-
-        @pl.when(tile_number == 0)
+        s, step = t // n_steps, t % n_steps
+
+        @pl.when(step == 0)
         def _():
             pltpu.make_async_copy(m_buf.at[s], m_buf.at[s], m_sems.at[s]).wait()
             pltpu.make_async_copy(left_buf.at[s], left_buf.at[s], left_sems.at[s]).wait()
 
         lhs = m_buf[s].reshape(k_count * both, depth)
-        tile = left_tile(lhs, w_buf[0, :, pl.ds(start, STEP)], w_buf[1, :, pl.ds(start, STEP)], k_count, both)
-        left_buf[s, :, :, pl.ds(start, STEP)] = left_buf[s, :, :, pl.ds(start, STEP)] + tile
-
-        @pl.when(tile_number == n_tiles - 1)
+        for at in range(0, wide, STEP):
+            start = pl.multiple_of(step * wide + at, STEP)
+            tile = left_tile(lhs, w_buf[0, :, pl.ds(start, STEP)], w_buf[1, :, pl.ds(start, STEP)], k_count, both)
+            left_buf[s, :, :, pl.ds(start, STEP)] = left_buf[s, :, :, pl.ds(start, STEP)] + tile
+
+        @pl.when(step == n_steps - 1)
         def _():
             second(s)
 
         return carry
 
-    lax.fori_loop(0, n_slots * n_tiles, one_step, 0)
+    lax.fori_loop(0, n_slots * n_steps, one_step, 0)
 
     def only_second(s, carry):
         pltpu.make_async_copy(left_buf.at[s], left_buf.at[s], left_sems.at[s]).wait()
@@ -525,43 +528,48 @@
     sums_copy = pltpu.make_async_copy(sums_in, acc, sums_sem)
     sums_copy.start()
 
+    wide = WIDE_STEP if span % WIDE_STEP == 0 else STEP
+    n_steps = span // wide
+
     def one_step(t, carry):
-        s, tile_number = t // n_tiles, t % n_tiles
-        start = pl.multiple_of(tile_number * STEP, STEP)
+        s, step = t // n_steps, t % n_steps
 
         @pl.when(s == 0)
         def _():
-            for copy in w_copies(w_refs[0], places[0], turns, w_buf, 0, 0, STEP, w_sems.at[tile_number]):
-                copy.wait()
-
-        @pl.when(tile_number == 0)
+            for i in range(wide // STEP):
+                number = step * (wide // STEP) + i
+                for copy in w_copies(w_refs[0], places[0], turns, w_buf, 0, 0, STEP, w_sems.at[number]):
+                    copy.wait()
+
+        @pl.when(step == 0)
         def _():
             pltpu.make_async_copy(m_buf.at[s], m_buf.at[s], m_sems.at[s]).wait()
-
-        for j in range(n_slots - 1):
-            @pl.when(t == j * n_tiles)
+            for j in range(n_slots - 1):
+                @pl.when(s == j)
+                def _():
+                    if j + 2 < n_slots:
+                        m_start(j + 2)
+                    c_start(j + 1)
+
+        lhs = m_buf[s].reshape(k_count * both, depth)
+        for at in range(0, wide, STEP):
+            start = pl.multiple_of(step * wide + at, STEP)
+            tile = left_tile(lhs, w_buf[0, :, pl.ds(start, STEP)], w_buf[1, :, pl.ds(start, STEP)], k_count, both)
+            left_buf[:, :, pl.ds(start, STEP)] = tile
+
+        @pl.when(step == n_steps - 1)
+        def _():
+            @pl.when(s == 0)
             def _():
-                if j + 2 < n_slots:
-                    m_start(j + 2)
-                c_start(j + 1)
-
-        lhs = m_buf[s].reshape(k_count * both, depth)
-        tile = left_tile(lhs, w_buf[0, :, pl.ds(start, STEP)], w_buf[1, :, pl.ds(start, STEP)], k_count, both)
-        left_buf[:, :, pl.ds(start, STEP)] = tile
-
-        @pl.when(t == n_tiles - 1)
-        def _():
-            sums_copy.wait()
-
-        @pl.when(tile_number == n_tiles - 1)
-        def _():
+                sums_copy.wait()
+
             matched_wait(c_buf, s, c_sems)
             for k in range(k_count):
                 acc[s, k] = acc[s, k] + times_matched(left_buf[k], c_buf[s, (k + flags[3]) % k_count])
 
         return carry
 
-    lax.fori_loop(0, n_slots * n_tiles, one_step, 0)
+    lax.fori_loop(0, n_slots * n_steps, one_step, 0)
     pairs, own_k = both // 2, k_count // 2
     for s in range(n_slots):
         above = jnp.where(flags[2] == 0, s, (n_slots - s) % n_slots)
@@ -706,13 +714,16 @@
 
     first_part, second_part = slots_from(0, k_count), slots_from(k_count, k_count)
 
-    flags, sent_0, sent_1 = moves(flags, (), far_part(0), far_part(1))
-    arrived_0, arrived_1 = sent_far(sent_0), sent_far(sent_1)
+    flags, sent_0 = moves(flags, (), far_part(0))
+    arrived_0 = sent_far(sent_0)
     own_first, own_second, own_both = turned_parts(flags, densities)
     swapped_0 = other_core(own_second)
     pair_a, mid_ad = end_with_mid(own_first), mid_with_mid(own_both)
 
-    flags, panel_0, sent_2 = moves(flags, (swapped_0,), *panel_parts(0, arrived_0), far_part(2))
+    flags, sent_1, sent_2 = moves(flags, (own_first,), far_part(1), far_part(2))
+
+    flags, panel_0 = moves(flags, (swapped_0,), *panel_parts(0, arrived_0))
+    arrived_1 = sent_far(sent_1)
     x_0, y_0 = along_x(panel_0), along_y(panel_0)
 
     flags, to_pair, to_mid = moves(

time: 283 us -> 280 us (0.989)
    pallas_call x8 -> x9, Pallas kernels: 27.3 us -> 28.6 us  [moves(): pl.pallas_call(functools.partial(moves_kernel, plan=tuple(plan), n_source...]
  transfers between devices with their start and end apart: 26 -> 26, of which waited for: 12 -> 11; matrix products, arithmetic and copies ran while one was open for 0% -> 0% of each run, Pallas kernels for 32% -> 32%
where the time goes in v5:
time: 280 us; the launch traced here: 278 us
  Pallas kernels  124 us (44%)
  waiting for transfers between devices  80.8 us (29%)
  starting transfers between devices  65.7 us (23%)
  between operations  2.93 us (1%)
    ppermute x26, waiting for transfers between devices, moved(): return lax.ppermute(value, AXES, pairs)  80.8 us
    ppermute x26, starting transfers between devices, moved(): return lax.ppermute(value, AXES, pairs)  65.7 us
    pallas_call x3, Pallas kernels, first_product(): pl.pallas_call(functools.partial(first_kernel, first_slot=first_slot, n_s...  39.4 us
    pallas_call x1, Pallas kernels, both_products(): pl.pallas_call(functools.partial(both_kernel, n_slots=n_slots, columns=co...  33.7 us
    pallas_call x9, Pallas kernels, moves(): pl.pallas_call(functools.partial(moves_kernel, plan=tuple(plan), n_source...  28.6 us
    pallas_call x1, Pallas kernels, stored_products(): pl.pallas_call(functools.partial(stored_kernel, n_slots=n_slots, n_lefts=...  16.9 us
    pallas_call x1, Pallas kernels, turned_parts(): pl.pallas_call(turn_kernel, out_shape=(jax.ShapeDtypeStruct((k_count, bot...  5.82 us
  transfers between devices with their start and end apart: 26, of which 11 were waited for; matrix products, arithmetic and copies ran while one was open for 0% of the time, Pallas kernels for 32%

profile of v5, /device:TPU:0, one launch (start us, length us, event | category | flops | bytes accessed | tf_op | source)
XLA Modules:
  0.0 278.5 jit_solution(256535153960130919)
XLA Ops:
  4.5 2.1 collective-permute-start
  6.6 5.8 %turned_parts.1 = (bf16[4,128,1536]{2,1,0:T(8,128)(2,1)}, bf16[4,128,1536]{2,1,0:T(8,128)(2,1)}, bf16[2,4,128,1536]{3,2,1,0:T(8,128)(2,1)}) custom-call(s32[8]{0:T(128)} %get-tuple-element.41.flags, bf16[4,6144,128]{2,1,0:T(8,128)(2,1)} %second.1, bf16[4,6144,128]{2,1,0:T(8,128)(2,1)} %second.1), custom_call_target="tpu_custom_call" | custom-call | flops 1000 | bytes 1000 | tf_op jit(solution)/shard_map/turned_parts/pallas_call | solution.py:642
  12.4 5.7 %collective-permute-start.1 = (bf16[4,128,1536]{2,1,0:T(8,128)(2,1)}, bf16[4,128,1536]{2,1,0:T(8,128)(2,1)}, u32[]{:S(2)}, u32[]{:S(2)}) collective-permute-start(bf16[4,128,1536]{2,1,0:T(8,128)(2,1)} %get-tuple-element.45.refs_0_.refs_5_.refs_9_.refs_10_.refs_18_), channel_id=1, source_target_pairs={{0,1},{1,0},{2,3},{3,2},{4,5},{5,4},{6,7},{7,6},{8,9},{9,8},{10,11... | collective-permute-start | bytes 4718600 | tf_op jit(solution)/shard_map/ppermute | solution.py:89
  18.1 2.3 collective-permute-start.2
  21.7 4.0 %moves.11 = (bf16[384,3072]{1,0:T(8,128)(2,1)}, s32[8]{0:T(128)}) custom-call(s32[8]{0:T(128)} %get-tuple-element.43.flags, bf16[2,384,3072]{2,1,0:T(8,128)(2,1)} %refs_1_.9, bf16[2,384,3072]{2,1,0:T(8,128)(2,1)} %refs_1_.9, bf16[384,3072]{1,0:T(8,128)(2,1)} %collective-permute-done.refs_2_, ...), custom_call_target="tpu_custom_call" | custom-call | flops 1000 | bytes 1000 | tf_op jit(solution)/shard_map/moves/pallas_call | solution.py:214
  25.7 1.6 collective-permute-start.5
  28.8 19.3 %collective-permute-start.3 = (bf16[4,128,1536]{2,1,0:T(8,128)(2,1)}, bf16[4,128,1536]{2,1,0:T(8,128)(2,1)}, u32[]{:S(2)}, u32[]{:S(2)}) collective-permute-start(bf16[4,128,1536]{2,1,0:T(8,128)(2,1)} %get-tuple-element.42.refs_4_.refs_7_.refs_14_), channel_id=1, source_target_pairs={{0,8},{1,9},{2,10},{3,11},{4,12},{5,13},{6,14},{7,15},{8,0},{9,1},... | collective-permute-start | bytes 4718600 | tf_op jit(solution)/shard_map/ppermute | solution.py:89
  48.1 1.7 collective-permute-start.4
  49.8 33.5 %collective-permute-done.3.refs_2_.refs_6_.refs_11_.refs_20_ = bf16[4,128,1536]{2,1,0:T(8,128)(2,1)} collective-permute-done((bf16[4,128,1536]{2,1,0:T(8,128)(2,1)}, bf16[4,128,1536]{2,1,0:T(8,128)(2,1)}, u32[]{:S(2)}, u32[]{:S(2)}) %collective-permute-start.3) | collective-permute-done | bytes 1572896 | tf_op jit(solution)/shard_map/ppermute | solution.py:89
  83.3 4.3 %moves.12 = (bf16[4,128,1536]{2,1,0:T(8,128)(2,1)}, bf16[4,128,1536]{2,1,0:T(8,128)(2,1)}, s32[8]{0:T(128)}) custom-call(s32[8]{0:T(128)} %get-tuple-element.46.flags, bf16[4,128,1536]{2,1,0:T(8,128)(2,1)} %get-tuple-element.45.refs_0_.refs_5_.refs_9_.refs_10_.refs_18_, bf16[8,128,1536]{2,1,0:T(8,128)(2,1)} %collective-permute-done.2.refs_1_.refs_8_.refs_15_, ...), custom_call_target="tpu_custom_call" | custom-call | flops 1000 | bytes 1000 | tf_op jit(solution)/shard_map/moves/pallas_call | solution.py:214
  87.6 8.5 %collective-permute-start.8 = (bf16[4,128,1536]{2,1,0:T(8,128)(2,1)}, bf16[4,128,1536]{2,1,0:T(8,128)(2,1)}, u32[]{:S(2)}, u32[]{:S(2)}) collective-permute-start(bf16[4,128,1536]{2,1,0:T(8,128)(2,1)} %get-tuple-element.55), channel_id=1, source_target_pairs={{0,8},{1,9},{2,10},{3,11},{4,12},{5,13},{6,14},{7,15},{8,0},{9,1},... | collective-permute-start | bytes 4718600 | tf_op jit(solution)/shard_map/ppermute | solution.py:89
  96.1 1.9 collective-permute-start.9
  98.0 4.6 %moves.13 = (bf16[384,3072]{1,0:T(8,128)(2,1)}, bf16[384,3072]{1,0:T(8,128)(2,1)}, bf16[384,1536]{1,0:T(8,128)(2,1)}, s32[8]{0:T(128)}) custom-call(s32[8]{0:T(128)} %get-tuple-element.48.flags, bf16[2,384,3072]{2,1,0:T(8,128)(2,1)} %refs_1_.9, bf16[2,384,3072]{2,1,0:T(8,128)(2,1)} %refs_1_.9, ...), custom_call_target="tpu_custom_call", output_to_operand_aliasing={{2}: (6, {})} | custom-call | flops 1000 | bytes 1000 | tf_op jit(solution)/shard_map/moves/pallas_call | solution.py:214
  102.6 1.6 collective-permute-start.10
  105.7 1.7 collective-permute-start.7
  107.4 15.7 %first_product.3 = (f32[2,4,128,1536]{3,2,1,0:T(8,128)}, s32[8]{0:T(128)}) custom-call(s32[8]{0:T(128)} %get-tuple-element.52.flags, bf16[384,3072]{1,0:T(8,128)(2,1)} %get-tuple-element.50.refs_0_, bf16[384,3072]{1,0:T(8,128)(2,1)} %collective-permute-done.6.refs_4_.refs_1_, bf16[384,3072]{1,0:T(8,128)(2,1)} %collective-permute-done.5.refs_3_.refs_2_, ...), custom_call_target="tpu_custom_call" | custom-call | flops 1000 | bytes 1000 | tf_op jit(solution)/shard_map/first_product/pallas_call | solution.py:373
  123.1 8.2 %collective-permute-done.8.refs_1_ = bf16[4,128,1536]{2,1,0:T(8,128)(2,1)} collective-permute-done((bf16[4,128,1536]{2,1,0:T(8,128)(2,1)}, bf16[4,128,1536]{2,1,0:T(8,128)(2,1)}, u32[]{:S(2)}, u32[]{:S(2)}) %collective-permute-start.8) | collective-permute-done | bytes 1572896 | tf_op jit(solution)/shard_map/ppermute | solution.py:89
  133.8 1.8 collective-permute-start.13
  135.7 19.9 %collective-permute-done.10.refs_3_.refs_2_ = bf16[384,3072]{1,0:T(8,128)(2,1)} collective-permute-done((bf16[384,3072]{1,0:T(8,128)(2,1)}, bf16[384,3072]{1,0:T(8,128)(2,1)}, u32[]{:S(2)}, u32[]{:S(2)}) %collective-permute-start.10) | collective-permute-done | bytes 2359328 | tf_op jit(solution)/shard_map/ppermute | solution.py:89
  156.8 4.2 %moves.15 = (bf16[384,2304]{1,0:T(8,128)(2,1)}, bf16[384,2304]{1,0:T(8,128)(2,1)}, s32[8]{0:T(128)}) custom-call(s32[8]{0:T(128)} %get-tuple-element.57.flags, bf16[2,384,3072]{2,1,0:T(8,128)(2,1)} %refs_1_.9, bf16[2,384,3072]{2,1,0:T(8,128)(2,1)} %refs_1_.9, bf16[384,1536]{1,0:T(8,128)(2,1)} %collective-permute-done.7.refs_0_.refs_2_, ...), custom_call_target="tpu_custom_call" | custom-call | flops 1000 | bytes 1000 | tf_op jit(solution)/shard_map/moves/pallas_call | solution.py:214
  163.1 11.9 %first_product.4 = (f32[1,4,128,1536]{3,2,1,0:T(8,128)}, s32[8]{0:T(128)}) custom-call(s32[8]{0:T(128)} %get-tuple-element.60.flags, bf16[384,3072]{1,0:T(8,128)(2,1)} %get-tuple-element.50.refs_0_, bf16[384,3072]{1,0:T(8,128)(2,1)} %collective-permute-done.6.refs_4_.refs_1_, bf16[384,3072]{1,0:T(8,128)(2,1)} %collective-permute-done.5.refs_3_.refs_2_, ...), custom_call_target="tpu_custom_call" | custom-call | flops 1000 | bytes 1000 | tf_op jit(solution)/shard_map/first_product/pallas_call | solution.py:373
  175.0 7.8 %collective-permute-done.12.refs_2_.refs_5_.refs_13_ = bf16[4,128,1536]{2,1,0:T(8,128)(2,1)} collective-permute-done((bf16[4,128,1536]{2,1,0:T(8,128)(2,1)}, bf16[4,128,1536]{2,1,0:T(8,128)(2,1)}, u32[]{:S(2)}, u32[]{:S(2)}) %collective-permute-start.12) | collective-permute-done | bytes 1572896 | tf_op jit(solution)/shard_map/ppermute | solution.py:89
  182.9 4.4 %moves.16 = (bf16[4,128,1536]{2,1,0:T(8,128)(2,1)}, bf16[4,128,1536]{2,1,0:T(8,128)(2,1)}, s32[8]{0:T(128)}) custom-call(s32[8]{0:T(128)} %get-tuple-element.63.flags, bf16[4,128,1536]{2,1,0:T(8,128)(2,1)} %get-tuple-element.61.refs_5_.refs_0_.refs_6_.refs_12_.refs_17_, bf16[8,128,1536]{2,1,0:T(8,128)(2,1)} %collective-permute-done.2.refs_1_.refs_8_.refs_15_, ...), custom_call_target="tpu_custom_call" | custom-call | flops 1000 | bytes 1000 | tf_op jit(solution)/shard_map/moves/pallas_call | solution.py:214
  187.9 11.8 %first_product.5 = (f32[1,4,128,1536]{3,2,1,0:T(8,128)}, s32[8]{0:T(128)}) custom-call(s32[8]{0:T(128)} %get-tuple-element.64.flags, bf16[384,3072]{1,0:T(8,128)(2,1)} %get-tuple-element.50.refs_0_, bf16[384,3072]{1,0:T(8,128)(2,1)} %collective-permute-done.6.refs_4_.refs_1_, bf16[384,3072]{1,0:T(8,128)(2,1)} %collective-permute-done.5.refs_3_.refs_2_, ...), custom_call_target="tpu_custom_call" | custom-call | flops 1000 | bytes 1000 | tf_op jit(solution)/shard_map/first_product/pallas_call | solution.py:373
  200.6 3.3 %moves.17 = (bf16[384,768]{1,0:T(8,128)(2,1)}, bf16[384,768]{1,0:T(8,128)(2,1)}, s32[8]{0:T(128)}) custom-call(s32[8]{0:T(128)} %get-tuple-element.65.flags, bf16[384,2304]{1,0:T(8,128)(2,1)} %collective-permute-done.15.refs_0_.refs_3_.refs_7_, bf16[384,2304]{1,0:T(8,128)(2,1)} %collective-permute-done.16.refs_1_.refs_4_.refs_6_), custom_call_target="tpu_custom_call" | custom-call | flops 1000 | bytes 1000 | tf_op jit(solution)/shard_map/moves/pallas_call | solution.py:214
  203.9 1.5 collective-permute-start.19
  206.9 16.9 %stored_products.1 = (f32[4,4,128,128]{3,2,1,0:T(8,128)}, s32[8]{0:T(128)}) custom-call(s32[8]{0:T(128)} %get-tuple-element.68.flags, bf16[384,3072]{1,0:T(8,128)(2,1)} %get-tuple-element.50.refs_0_, bf16[384,3072]{1,0:T(8,128)(2,1)} %collective-permute-done.6.refs_4_.refs_1_, bf16[384,3072]{1,0:T(8,128)(2,1)} %collective-permute-done.5.refs_3_.refs_2_, ...), custom_call_target="tpu_custom_call" | custom-call | flops 1000 | bytes 1000 | tf_op jit(solution)/shard_map/stored_products/pallas_call | solution.py:467
  223.9 33.7 %both_products.1 = (f32[4,2,64,128]{3,2,1,0:T(8,128)}, f32[4,2,64,128]{3,2,1,0:T(8,128)}) custom-call(s32[8]{0:T(128)} %get-tuple-element.74.flags, bf16[384,3072]{1,0:T(8,128)(2,1)} %get-tuple-element.59.refs_0_, bf16[384,3072]{1,0:T(8,128)(2,1)} %collective-permute-done.11.refs_4_.refs_1_, bf16[384,3072]{1,0:T(8,128)(2,1)} %collective-permute-done.10.refs_3_.refs_2_, ...), custom_call_target="tpu_custom_call" | custom-call | flops 1000 | bytes 1000 | tf_op jit(solution)/shard_map/both_products/pallas_call | solution.py:599
  257.7 1.7 collective-permute-done.21
  260.5 4.2 %collective-permute-start.22 = (f32[2,2,64,128]{3,2,1,0:T(8,128)S(1)}, f32[2,2,64,128]{3,2,1,0:T(8,128)S(1)}, u32[]{:S(2)}, u32[]{:S(2)}) collective-permute-start(f32[2,2,64,128]{3,2,1,0:T(8,128)S(1)} %get-tuple-element.90), channel_id=1, source_target_pairs={{0,8},{1,9},{2,10},{3,11},{4,12},{5,13},{6,14},{7,15},{8,16},{9,17... | collective-permute-start | bytes 393224 | tf_op jit(solution)/shard_map/ppermute | solution.py:89
  265.1 2.8 %collective-permute-start.24 = (f32[2,2,64,128]{3,2,1,0:T(8,128)S(1)}, f32[2,2,64,128]{3,2,1,0:T(8,128)S(1)}, u32[]{:S(2)}, u32[]{:S(2)}) collective-permute-start(f32[2,2,64,128]{3,2,1,0:T(8,128)S(1)} %get-tuple-element.92), channel_id=1, source_target_pairs={{0,24},{1,25},{2,26},{3,27},{4,28},{5,29},{6,30},{7,31},{8,0},{9,1... | collective-permute-start | bytes 393224 | tf_op jit(solution)/shard_map/ppermute | solution.py:89
  268.6 5.5 %collective-permute-done.23 = f32[2,2,64,128]{3,2,1,0:T(8,128)S(1)} collective-permute-done((f32[2,2,64,128]{3,2,1,0:T(8,128)S(1)}, f32[2,2,64,128]{3,2,1,0:T(8,128)S(1)}, u32[]{:S(2)}, u32[]{:S(2)}) %collective-permute-start.23) | collective-permute-done | bytes 131104 | tf_op jit(solution)/shard_map/ppermute | solution.py:89
  (54 shorter events, 21.5 us)
Async XLA Ops:
  4.5 17.2 %collective-permute-start = (bf16[384,3072]{1,0:T(8,128)(2,1)}, bf16[384,3072]{1,0:T(8,128)(2,1)}, u32[]{:S(2)}, u32[]{:S(2)}) collective-permute-start(bf16[384,3072]{1,0:T(8,128)(2,1)} %get-tuple-element.44), channel_id=1, source_target_pairs={{1,8},{3,10},{5,12},{7,14},{8,1},{10,3},{12,5},{14,7},{17,24},{19,... | collective-permute-start | bytes 7077896 | tf_op jit(solution)/shard_map/ppermute | solution.py:89
  12.4 9.3 %collective-permute-start.1 = (bf16[4,128,1536]{2,1,0:T(8,128)(2,1)}, bf16[4,128,1536]{2,1,0:T(8,128)(2,1)}, u32[]{:S(2)}, u32[]{:S(2)}) collective-permute-start(bf16[4,128,1536]{2,1,0:T(8,128)(2,1)} %get-tuple-element.45.refs_0_.refs_5_.refs_9_.refs_10_.refs_18_), channel_id=1, source_target_pairs={{0,1},{1,0},{2,3},{3,2},{4,5},{5,4},{6,7},{7,6},{8,9},{9,8},{10,11... | collective-permute-start | bytes 4718600 | tf_op jit(solution)/shard_map/ppermute | solution.py:89
  18.1 65.2 %collective-permute-start.2 = (bf16[8,128,1536]{2,1,0:T(8,128)(2,1)}, bf16[8,128,1536]{2,1,0:T(8,128)(2,1)}, u32[]{:S(2)}, u32[]{:S(2)}) collective-permute-start(bf16[8,128,1536]{2,1,0:T(8,128)(2,1)} %bitcast.27), channel_id=1, source_target_pairs={{8,16},{9,17},{10,18},{11,19},{12,20},{13,21},{14,22},{15,23},{16,... | collective-permute-start | bytes 9437192 | tf_op jit(solution)/shard_map/ppermute | solution.py:89
  25.7 72.3 %collective-permute-start.5 = (bf16[384,3072]{1,0:T(8,128)(2,1)}, bf16[384,3072]{1,0:T(8,128)(2,1)}, u32[]{:S(2)}, u32[]{:S(2)}) collective-permute-start(bf16[384,3072]{1,0:T(8,128)(2,1)} %get-tuple-element.50.refs_0_), channel_id=1, source_target_pairs={{0,4},{1,5},{2,6},{3,7},{4,0},{5,1},{6,2},{7,3},{8,12},{9,13},{10,... | collective-permute-start | bytes 7077896 | tf_op jit(solution)/shard_map/ppermute | solution.py:89
  27.3 70.7 %collective-permute-start.6 = (bf16[384,3072]{1,0:T(8,128)(2,1)}, bf16[384,3072]{1,0:T(8,128)(2,1)}, u32[]{:S(2)}, u32[]{:S(2)}) collective-permute-start(bf16[384,3072]{1,0:T(8,128)(2,1)} %get-tuple-element.50.refs_0_), channel_id=1, source_target_pairs={{0,2},{1,3},{2,0},{3,1},{4,6},{5,7},{6,4},{7,5},{8,10},{9,11},{10,... | collective-permute-start | bytes 7077896 | tf_op jit(solution)/shard_map/ppermute | solution.py:89
  28.8 54.5 %collective-permute-start.3 = (bf16[4,128,1536]{2,1,0:T(8,128)(2,1)}, bf16[4,128,1536]{2,1,0:T(8,128)(2,1)}, u32[]{:S(2)}, u32[]{:S(2)}) collective-permute-start(bf16[4,128,1536]{2,1,0:T(8,128)(2,1)} %get-tuple-element.42.refs_4_.refs_7_.refs_14_), channel_id=1, source_target_pairs={{0,8},{1,9},{2,10},{3,11},{4,12},{5,13},{6,14},{7,15},{8,0},{9,1},... | collective-permute-start | bytes 4718600 | tf_op jit(solution)/shard_map/ppermute | solution.py:89
  48.1 49.9 %collective-permute-start.4 = (bf16[384,1536]{1,0:T(8,128)(2,1)}, bf16[384,1536]{1,0:T(8,128)(2,1)}, u32[]{:S(2)}, u32[]{:S(2)}) collective-permute-start(bf16[384,1536]{1,0:T(8,128)(2,1)} %get-tuple-element.49), channel_id=1, source_target_pairs={{1,8},{3,10},{5,12},{7,14},{8,1},{10,3},{12,5},{14,7},{17,24},{19,... | collective-permute-start | bytes 3538952 | tf_op jit(solution)/shard_map/ppermute | solution.py:89
  87.6 43.7 %collective-permute-start.8 = (bf16[4,128,1536]{2,1,0:T(8,128)(2,1)}, bf16[4,128,1536]{2,1,0:T(8,128)(2,1)}, u32[]{:S(2)}, u32[]{:S(2)}) collective-permute-start(bf16[4,128,1536]{2,1,0:T(8,128)(2,1)} %get-tuple-element.55), channel_id=1, source_target_pairs={{0,8},{1,9},{2,10},{3,11},{4,12},{5,13},{6,14},{7,15},{8,0},{9,1},... | collective-permute-start | bytes 4718600 | tf_op jit(solution)/shard_map/ppermute | solution.py:89
  96.1 35.2 %collective-permute-start.9 = (bf16[4,128,1536]{2,1,0:T(8,128)(2,1)}, bf16[4,128,1536]{2,1,0:T(8,128)(2,1)}, u32[]{:S(2)}, u32[]{:S(2)}) collective-permute-start(bf16[4,128,1536]{2,1,0:T(8,128)(2,1)} %get-tuple-element.56), channel_id=1, source_target_pairs={{8,16},{9,17},{10,18},{11,19},{12,20},{13,21},{14,22},{15,23},{16,... | collective-permute-start | bytes 4718600 | tf_op jit(solution)/shard_map/ppermute | solution.py:89
  102.6 52.9 %collective-permute-start.10 = (bf16[384,3072]{1,0:T(8,128)(2,1)}, bf16[384,3072]{1,0:T(8,128)(2,1)}, u32[]{:S(2)}, u32[]{:S(2)}) collective-permute-start(bf16[384,3072]{1,0:T(8,128)(2,1)} %get-tuple-element.58), channel_id=1, source_target_pairs={{0,4},{1,5},{2,6},{3,7},{4,0},{5,1},{6,2},{7,3},{8,12},{9,13},{10,... | collective-permute-start | bytes 7077896 | tf_op jit(solution)/shard_map/ppermute | solution.py:89
  104.2 52.6 %collective-permute-start.11 = (bf16[384,3072]{1,0:T(8,128)(2,1)}, bf16[384,3072]{1,0:T(8,128)(2,1)}, u32[]{:S(2)}, u32[]{:S(2)}) collective-permute-start(bf16[384,3072]{1,0:T(8,128)(2,1)} %get-tuple-element.59.refs_0_), channel_id=1, source_target_pairs={{0,2},{1,3},{2,0},{3,1},{4,6},{5,7},{6,4},{7,5},{8,10},{9,11},{10,... | collective-permute-start | bytes 7077896 | tf_op jit(solution)/shard_map/ppermute | solution.py:89
  105.7 25.6 %collective-permute-start.7 = (bf16[384,1536]{1,0:T(8,128)(2,1)}, bf16[384,1536]{1,0:T(8,128)(2,1)}, u32[]{:S(2)}, u32[]{:S(2)}) collective-permute-start(bf16[384,1536]{1,0:T(8,128)(2,1)} %get-tuple-element.54), channel_id=1, source_target_pairs={{1,8},{3,10},{5,12},{7,14},{8,1},{10,3},{12,5},{14,7},{17,24},{19,... | collective-permute-start | bytes 3538952 | tf_op jit(solution)/shard_map/ppermute | solution.py:89
  131.3 43.7 %collective-permute-start.14 = (bf16[4,128,1536]{2,1,0:T(8,128)(2,1)}, bf16[4,128,1536]{2,1,0:T(8,128)(2,1)}, u32[]{:S(2)}, u32[]{:S(2)}) collective-permute-start(bf16[4,128,1536]{2,1,0:T(8,128)(2,1)} %collective-permute-done.3.refs_2_.refs_6_.refs_11_.refs_20_), channel_id=1, source_target_pairs={{0,1},{1,0},{2,3},{3,2},{4,5},{5,4},{6,7},{7,6},{8,9},{9,8},{10,11... | collective-permute-start | bytes 4718600 | tf_op jit(solution)/shard_map/ppermute | solution.py:89
  132.5 50.3 %collective-permute-start.12 = (bf16[4,128,1536]{2,1,0:T(8,128)(2,1)}, bf16[4,128,1536]{2,1,0:T(8,128)(2,1)}, u32[]{:S(2)}, u32[]{:S(2)}) collective-permute-start(bf16[4,128,1536]{2,1,0:T(8,128)(2,1)} %get-tuple-element.62.refs_6_.refs_16_), channel_id=1, source_target_pairs={{8,0},{9,1},{10,2},{11,3},{12,4},{13,5},{14,6},{15,7},{16,24},{17,... | collective-permute-start | bytes 4718600 | tf_op jit(solution)/shard_map/ppermute | solution.py:89
  133.8 49.0 %collective-permute-start.13 = (bf16[4,128,1536]{2,1,0:T(8,128)(2,1)}, bf16[4,128,1536]{2,1,0:T(8,128)(2,1)}, u32[]{:S(2)}, u32[]{:S(2)}) collective-permute-start(bf16[4,128,1536]{2,1,0:T(8,128)(2,1)} %get-tuple-element.61.refs_5_.refs_0_.refs_6_.refs_12_.refs_17_), channel_id=1, source_target_pairs={{8,16},{9,17},{10,18},{11,19},{12,20},{13,21},{14,22},{15,23},{16,... | collective-permute-start | bytes 4718600 | tf_op jit(solution)/shard_map/ppermute | solution.py:89
  161.0 39.3 %collective-permute-start.15 = (bf16[384,2304]{1,0:T(8,128)(2,1)}, bf16[384,2304]{1,0:T(8,128)(2,1)}, u32[]{:S(2)}, u32[]{:S(2)}) collective-permute-start(bf16[384,2304]{1,0:T(8,128)(2,1)} %get-tuple-element.66), channel_id=1, source_target_pairs={{0,4},{1,5},{2,6},{3,7},{4,0},{5,1},{6,2},{7,3},{8,12},{9,13},{10,... | collective-permute-start | bytes 5308424 | tf_op jit(solution)/shard_map/ppermute | solution.py:89
  161.6 39.0 %collective-permute-start.16 = (bf16[384,2304]{1,0:T(8,128)(2,1)}, bf16[384,2304]{1,0:T(8,128)(2,1)}, u32[]{:S(2)}, u32[]{:S(2)}) collective-permute-start(bf16[384,2304]{1,0:T(8,128)(2,1)} %get-tuple-element.67.refs_5_), channel_id=1, source_target_pairs={{0,2},{1,3},{2,0},{3,1},{4,6},{5,7},{6,4},{7,5},{8,10},{9,11},{10,... | collective-permute-start | bytes 5308424 | tf_op jit(solution)/shard_map/ppermute | solution.py:89
  187.3 19.6 %collective-permute-start.17 = (bf16[4,128,1536]{2,1,0:T(8,128)(2,1)}, bf16[4,128,1536]{2,1,0:T(8,128)(2,1)}, u32[]{:S(2)}, u32[]{:S(2)}) collective-permute-start(bf16[4,128,1536]{2,1,0:T(8,128)(2,1)} %get-tuple-element.69.refs_13_.refs_22_), channel_id=1, source_target_pairs={{0,1},{1,0},{2,3},{3,2},{4,5},{5,4},{6,7},{7,6},{8,9},{9,8},{10,11... | collective-permute-start | bytes 4718600 | tf_op jit(solution)/shard_map/ppermute | solution.py:89
  187.5 19.4 %collective-permute-start.18 = (bf16[4,128,1536]{2,1,0:T(8,128)(2,1)}, bf16[4,128,1536]{2,1,0:T(8,128)(2,1)}, u32[]{:S(2)}, u32[]{:S(2)}) collective-permute-start(bf16[4,128,1536]{2,1,0:T(8,128)(2,1)} %get-tuple-element.70.refs_15_.refs_24_), channel_id=1, source_target_pairs={{0,1},{1,0},{2,3},{3,2},{4,5},{5,4},{6,7},{7,6},{8,9},{9,8},{10,11... | collective-permute-start | bytes 4718600 | tf_op jit(solution)/shard_map/ppermute | solution.py:89
  203.9 20.0 %collective-permute-start.19 = (bf16[384,768]{1,0:T(8,128)(2,1)}, bf16[384,768]{1,0:T(8,128)(2,1)}, u32[]{:S(2)}, u32[]{:S(2)}) collective-permute-start(bf16[384,768]{1,0:T(8,128)(2,1)} %get-tuple-element.75), channel_id=1, source_target_pairs={{0,4},{1,5},{2,6},{3,7},{4,0},{5,1},{6,2},{7,3},{8,12},{9,13},{10,... | collective-permute-start | bytes 1769480 | tf_op jit(solution)/shard_map/ppermute | solution.py:89
  205.4 18.5 %collective-permute-start.20 = (bf16[384,768]{1,0:T(8,128)(2,1)}, bf16[384,768]{1,0:T(8,128)(2,1)}, u32[]{:S(2)}, u32[]{:S(2)}) collective-permute-start(bf16[384,768]{1,0:T(8,128)(2,1)} %get-tuple-element.76), channel_id=1, source_target_pairs={{0,2},{1,3},{2,0},{3,1},{4,6},{5,7},{6,4},{7,5},{8,10},{9,11},{10,... | collective-permute-start | bytes 1769480 | tf_op jit(solution)/shard_map/ppermute | solution.py:89
  257.6 1.8 collective-permute-start.21
  259.4 16.1 %copy-start = (s32[64]{0:T(128)S(1)}, s32[64]{0:T(128)}, u32[]{:S(2)}) copy-start(s32[64]{0:T(128)} %param.7) | copy-start | bytes 772
  260.5 8.1 %collective-permute-start.22 = (f32[2,2,64,128]{3,2,1,0:T(8,128)S(1)}, f32[2,2,64,128]{3,2,1,0:T(8,128)S(1)}, u32[]{:S(2)}, u32[]{:S(2)}) collective-permute-start(f32[2,2,64,128]{3,2,1,0:T(8,128)S(1)} %get-tuple-element.90), channel_id=1, source_target_pairs={{0,8},{1,9},{2,10},{3,11},{4,12},{5,13},{6,14},{7,15},{8,16},{9,17... | collective-permute-start | bytes 393224 | tf_op jit(solution)/shard_map/ppermute | solution.py:89
  264.7 9.3 %collective-permute-start.23 = (f32[2,2,64,128]{3,2,1,0:T(8,128)S(1)}, f32[2,2,64,128]{3,2,1,0:T(8,128)S(1)}, u32[]{:S(2)}, u32[]{:S(2)}) collective-permute-start(f32[2,2,64,128]{3,2,1,0:T(8,128)S(1)} %get-tuple-element.91), channel_id=1, source_target_pairs={{0,16},{1,17},{2,18},{3,19},{4,20},{5,21},{6,22},{7,23},{8,24},{9,... | collective-permute-start | bytes 393224 | tf_op jit(solution)/shard_map/ppermute | solution.py:89
  265.1 9.0 %collective-permute-start.24 = (f32[2,2,64,128]{3,2,1,0:T(8,128)S(1)}, f32[2,2,64,128]{3,2,1,0:T(8,128)S(1)}, u32[]{:S(2)}, u32[]{:S(2)}) collective-permute-start(f32[2,2,64,128]{3,2,1,0:T(8,128)S(1)} %get-tuple-element.92), channel_id=1, source_target_pairs={{0,24},{1,25},{2,26},{3,27},{4,28},{5,29},{6,30},{7,31},{8,0},{9,1... | collective-permute-start | bytes 393224 | tf_op jit(solution)/shard_map/ppermute | solution.py:89
  274.1 1.4 collective-permute-start.25

commit v6 on v5

--- a/solution.py
+++ b/solution.py
@@ -406,34 +406,49 @@
     depth = w_buf.shape[1]
     all_slots, k_count, both, _ = c_buf.shape
     sources = [left.at[i] for left in lefts for i in range(left.shape[0])]
-    w_loads = w_copies(w_refs, places, (3,), w_buf, 0, 0, width, w_sems)
-    for copy in w_loads:
-        copy.start()
+    wide = WIDE_STEP if width % WIDE_STEP == 0 else STEP
+    n_steps = width // wide
+
+    def w_loads(i):
+        return w_copies(w_refs, places, (3,), w_buf, i * wide, i * wide, wide, w_sems.at[i])
+
+    def left_load(source, s, i):
+        span = slice(i * wide, (i + 1) * wide)
+        return pltpu.make_async_copy(source.at[:, :, span], left_buf.at[s, :, :, span], left_sems.at[s, i])
+
     for s in range(all_slots):
         if s < n_slots:
             end_part, mid_part = part_of(of_end[s], leads[s], k_count), part_of(of_mid[s], leads[n_slots + s], k_count)
             m_copies(flags, (3,), end_part, mid_part, m_buf.at[s], m_sems.at[s])
-        pltpu.make_async_copy(sources[s], left_buf.at[s], left_sems.at[s]).start()
+        for i in range(n_steps):
+            if s == 0:
+                for copy in w_loads(i):
+                    copy.start()
+            left_load(sources[s], s, i).start()
         matched_copies(flags, matched, leads[2 * n_slots :], c_buf, (s,), first, width, c_sems)
     keep_flags(flags, flags_out)
-    for copy in w_loads:
-        copy.wait()
 
     def second(s):
         matched_wait(c_buf, s, c_sems)
         for k in range(k_count):
             sums[s, k] = times_matched(left_buf[s, k], c_buf[s, (k + flags[3]) % k_count])
 
-    wide = WIDE_STEP if width % WIDE_STEP == 0 else STEP
-    n_steps = width // wide
+    def left_wait(s, i):
+        some = left_buf.at[s, :, :, :wide]
+        pltpu.make_async_copy(some, some, left_sems.at[s, i]).wait()
 
     def one_step(t, carry):
         s, step = t // n_steps, t % n_steps
+        left_wait(s, step)
 
         @pl.when(step == 0)
         def _():
             pltpu.make_async_copy(m_buf.at[s], m_buf.at[s], m_sems.at[s]).wait()
-            pltpu.make_async_copy(left_buf.at[s], left_buf.at[s], left_sems.at[s]).wait()
+
+        @pl.when(s == 0)
+        def _():
+            for copy in w_copies(w_refs, places, (3,), w_buf, 0, 0, wide, w_sems.at[step]):
+                copy.wait()
 
         lhs = m_buf[s].reshape(k_count * both, depth)
         for at in range(0, wide, STEP):
@@ -450,7 +465,8 @@
     lax.fori_loop(0, n_slots * n_steps, one_step, 0)
 
     def only_second(s, carry):
-        pltpu.make_async_copy(left_buf.at[s], left_buf.at[s], left_sems.at[s]).wait()
+        for i in range(n_steps):
+            left_wait(s, i)
         second(s)
         return carry
 
@@ -481,10 +497,10 @@
             pltpu.VMEM((n_slots, k_count, both, rows), jnp.bfloat16),
             pltpu.VMEM((all_slots, k_count, both, width), jnp.bfloat16),
             pltpu.VMEM((all_slots, k_count, both, width), jnp.float32),
-            pltpu.SemaphoreType.DMA((2,)),
+            pltpu.SemaphoreType.DMA((width // STEP, 2)),
             pltpu.SemaphoreType.DMA((n_slots,)),
             pltpu.SemaphoreType.DMA((all_slots,)),
-            pltpu.SemaphoreType.DMA((all_slots,)),
+            pltpu.SemaphoreType.DMA((all_slots, width // STEP)),
         ],
         compiler_params=PARAMS,
         cost_estimate=COST,
@@ -756,11 +772,10 @@
     chunk_0 = (firsts[0], widths[0], (panel_0, x_0, y_0, y_1, x_1), (widths[0], 2 * widths[1], 2 * widths[1]))
     left_2, flags = first_product(flags, [chunk_0], every, 2, 1, of_end, of_mid)
 
-    flags, late_1, late_2 = moves(
-        flags,
-        (swapped_a,),
-        (part, [(at_end, pair_b, whole, whole), (at_mid, mid_ad, second_part, whole)]),
-        (part, [(at_end, pair_c, whole, whole), (at_mid, mid_c, whole, whole)]),
+    late_pieces = [(at_end, pair_b, whole, whole), (at_mid, mid_ad, second_part, whole)]
+    flags, late_1 = moves(flags, (), (part, late_pieces))
+    flags, late_2, late_1 = moves(
+        flags, (swapped_a,), (part, [(at_end, pair_c, whole, whole), (at_mid, mid_c, whole, whole)]), passing=(late_1,)
     )
     swapped_1, swapped_2 = other_core(late_1), other_core(late_2)
     of_end[3] = (pair_c, 0)

time: 280 us -> 279 us (level)
  Pallas kernels: 124 us -> 127 us
    pallas_call x9 -> x10, Pallas kernels: 28.6 us -> 31.6 us  [moves(): pl.pallas_call(functools.partial(moves_kernel, plan=tuple(plan), n_source...]
  transfers between devices with their start and end apart: 26 -> 26, of which waited for: 11 -> 11; matrix products, arithmetic and copies ran while one was open for 0% -> 0% of each run, Pallas kernels for 32% -> 33%
where the time goes in v6:
time: 279 us; the launch traced here: 278 us
  Pallas kernels  127 us (46%)
  waiting for transfers between devices  78 us (28%)
  starting transfers between devices  64.8 us (23%)
  between operations  2.94 us (1%)
    ppermute x26, waiting for transfers between devices, moved(): return lax.ppermute(value, AXES, pairs)  78 us
    ppermute x26, starting transfers between devices, moved(): return lax.ppermute(value, AXES, pairs)  64.8 us
    pallas_call x3, Pallas kernels, first_product(): pl.pallas_call(functools.partial(first_kernel, first_slot=first_slot, n_s...  39.3 us
    pallas_call x1, Pallas kernels, both_products(): pl.pallas_call(functools.partial(both_kernel, n_slots=n_slots, columns=co...  33.7 us
    pallas_call x10, Pallas kernels, moves(): pl.pallas_call(functools.partial(moves_kernel, plan=tuple(plan), n_source...  31.6 us
    pallas_call x1, Pallas kernels, stored_products(): pl.pallas_call(functools.partial(stored_kernel, n_slots=n_slots, n_lefts=...  16.8 us
    pallas_call x1, Pallas kernels, turned_parts(): pl.pallas_call(turn_kernel, out_shape=(jax.ShapeDtypeStruct((k_count, bot...  5.84 us
  transfers between devices with their start and end apart: 26, of which 11 were waited for; matrix products, arithmetic and copies ran while one was open for 0% of the time, Pallas kernels for 33%

profile of v6, /device:TPU:0, one launch (start us, length us, event | category | flops | bytes accessed | tf_op | source)
XLA Modules:
  0.0 277.7 jit_solution(484582737548316943)
XLA Ops:
  4.6 2.1 collective-permute-start
  6.6 5.8 %turned_parts.1 = (bf16[4,128,1536]{2,1,0:T(8,128)(2,1)}, bf16[4,128,1536]{2,1,0:T(8,128)(2,1)}, bf16[2,4,128,1536]{3,2,1,0:T(8,128)(2,1)}) custom-call(s32[8]{0:T(128)} %get-tuple-element.43.flags, bf16[4,6144,128]{2,1,0:T(8,128)(2,1)} %second.1, bf16[4,6144,128]{2,1,0:T(8,128)(2,1)} %second.1), custom_call_target="tpu_custom_call" | custom-call | flops 1000 | bytes 1000 | tf_op jit(solution)/shard_map/turned_parts/pallas_call | solution.py:658
  12.5 5.6 %collective-permute-start.1 = (bf16[4,128,1536]{2,1,0:T(8,128)(2,1)}, bf16[4,128,1536]{2,1,0:T(8,128)(2,1)}, u32[]{:S(2)}, u32[]{:S(2)}) collective-permute-start(bf16[4,128,1536]{2,1,0:T(8,128)(2,1)} %get-tuple-element.47.refs_0_.refs_5_.refs_9_.refs_10_.refs_18_), channel_id=1, source_target_pairs={{0,1},{1,0},{2,3},{3,2},{4,5},{5,4},{6,7},{7,6},{8,9},{9,8},{10,11... | collective-permute-start | bytes 4718600 | tf_op jit(solution)/shard_map/ppermute | solution.py:89
  18.1 2.3 collective-permute-start.2
  21.7 3.9 %moves.12 = (bf16[384,3072]{1,0:T(8,128)(2,1)}, s32[8]{0:T(128)}) custom-call(s32[8]{0:T(128)} %get-tuple-element.45.flags, bf16[2,384,3072]{2,1,0:T(8,128)(2,1)} %refs_1_.9, bf16[2,384,3072]{2,1,0:T(8,128)(2,1)} %refs_1_.9, bf16[384,3072]{1,0:T(8,128)(2,1)} %collective-permute-done.refs_2_, ...), custom_call_target="tpu_custom_call" | custom-call | flops 1000 | bytes 1000 | tf_op jit(solution)/shard_map/moves/pallas_call | solution.py:214
  25.7 1.6 collective-permute-start.5
  28.7 19.3 %collective-permute-start.3 = (bf16[4,128,1536]{2,1,0:T(8,128)(2,1)}, bf16[4,128,1536]{2,1,0:T(8,128)(2,1)}, u32[]{:S(2)}, u32[]{:S(2)}) collective-permute-start(bf16[4,128,1536]{2,1,0:T(8,128)(2,1)} %get-tuple-element.44.refs_4_.refs_7_.refs_14_), channel_id=1, source_target_pairs={{0,8},{1,9},{2,10},{3,11},{4,12},{5,13},{6,14},{7,15},{8,0},{9,1},... | collective-permute-start | bytes 4718600 | tf_op jit(solution)/shard_map/ppermute | solution.py:89
  48.1 1.7 collective-permute-start.4
  49.8 33.5 %collective-permute-done.3.refs_2_.refs_6_.refs_11_.refs_20_ = bf16[4,128,1536]{2,1,0:T(8,128)(2,1)} collective-permute-done((bf16[4,128,1536]{2,1,0:T(8,128)(2,1)}, bf16[4,128,1536]{2,1,0:T(8,128)(2,1)}, u32[]{:S(2)}, u32[]{:S(2)}) %collective-permute-start.3) | collective-permute-done | bytes 1572896 | tf_op jit(solution)/shard_map/ppermute | solution.py:89
  83.3 4.3 %moves.13 = (bf16[4,128,1536]{2,1,0:T(8,128)(2,1)}, bf16[4,128,1536]{2,1,0:T(8,128)(2,1)}, s32[8]{0:T(128)}) custom-call(s32[8]{0:T(128)} %get-tuple-element.48.flags, bf16[4,128,1536]{2,1,0:T(8,128)(2,1)} %get-tuple-element.47.refs_0_.refs_5_.refs_9_.refs_10_.refs_18_, bf16[8,128,1536]{2,1,0:T(8,128)(2,1)} %collective-permute-done.2.refs_1_.refs_8_.refs_15_, ...), custom_call_target="tpu_custom_call" | custom-call | flops 1000 | bytes 1000 | tf_op jit(solution)/shard_map/moves/pallas_call | solution.py:214
  87.6 8.5 %collective-permute-start.8 = (bf16[4,128,1536]{2,1,0:T(8,128)(2,1)}, bf16[4,128,1536]{2,1,0:T(8,128)(2,1)}, u32[]{:S(2)}, u32[]{:S(2)}) collective-permute-start(bf16[4,128,1536]{2,1,0:T(8,128)(2,1)} %get-tuple-element.57), channel_id=1, source_target_pairs={{0,8},{1,9},{2,10},{3,11},{4,12},{5,13},{6,14},{7,15},{8,0},{9,1},... | collective-permute-start | bytes 4718600 | tf_op jit(solution)/shard_map/ppermute | solution.py:89
  96.1 1.9 collective-permute-start.9
  98.0 4.5 %moves.14 = (bf16[384,3072]{1,0:T(8,128)(2,1)}, bf16[384,3072]{1,0:T(8,128)(2,1)}, bf16[384,1536]{1,0:T(8,128)(2,1)}, s32[8]{0:T(128)}) custom-call(s32[8]{0:T(128)} %get-tuple-element.50.flags, bf16[2,384,3072]{2,1,0:T(8,128)(2,1)} %refs_1_.9, bf16[2,384,3072]{2,1,0:T(8,128)(2,1)} %refs_1_.9, ...), custom_call_target="tpu_custom_call", output_to_operand_aliasing={{2}: (6, {})} | custom-call | flops 1000 | bytes 1000 | tf_op jit(solution)/shard_map/moves/pallas_call | solution.py:214
  102.6 1.6 collective-permute-start.10
  105.6 1.7 collective-permute-start.7
  107.3 15.7 %first_product.3 = (f32[2,4,128,1536]{3,2,1,0:T(8,128)}, s32[8]{0:T(128)}) custom-call(s32[8]{0:T(128)} %get-tuple-element.54.flags, bf16[384,3072]{1,0:T(8,128)(2,1)} %get-tuple-element.52.refs_0_, bf16[384,3072]{1,0:T(8,128)(2,1)} %collective-permute-done.6.refs_4_.refs_1_, bf16[384,3072]{1,0:T(8,128)(2,1)} %collective-permute-done.5.refs_3_.refs_2_, ...), custom_call_target="tpu_custom_call" | custom-call | flops 1000 | bytes 1000 | tf_op jit(solution)/shard_map/first_product/pallas_call | solution.py:373
  123.1 8.2 %collective-permute-done.8.refs_1_ = bf16[4,128,1536]{2,1,0:T(8,128)(2,1)} collective-permute-done((bf16[4,128,1536]{2,1,0:T(8,128)(2,1)}, bf16[4,128,1536]{2,1,0:T(8,128)(2,1)}, u32[]{:S(2)}, u32[]{:S(2)}) %collective-permute-start.8) | collective-permute-done | bytes 1572896 | tf_op jit(solution)/shard_map/ppermute | solution.py:89
  133.8 1.8 collective-permute-start.13
  135.6 19.8 %collective-permute-done.10.refs_3_.refs_2_ = bf16[384,3072]{1,0:T(8,128)(2,1)} collective-permute-done((bf16[384,3072]{1,0:T(8,128)(2,1)}, bf16[384,3072]{1,0:T(8,128)(2,1)}, u32[]{:S(2)}, u32[]{:S(2)}) %collective-permute-start.10) | collective-permute-done | bytes 2359328 | tf_op jit(solution)/shard_map/ppermute | solution.py:89
  156.7 4.2 %moves.16 = (bf16[384,2304]{1,0:T(8,128)(2,1)}, bf16[384,2304]{1,0:T(8,128)(2,1)}, s32[8]{0:T(128)}) custom-call(s32[8]{0:T(128)} %get-tuple-element.59.flags, bf16[2,384,3072]{2,1,0:T(8,128)(2,1)} %refs_1_.9, bf16[2,384,3072]{2,1,0:T(8,128)(2,1)} %refs_1_.9, bf16[384,1536]{1,0:T(8,128)(2,1)} %collective-permute-done.7.refs_0_.refs_2_, ...), custom_call_target="tpu_custom_call" | custom-call | flops 1000 | bytes 1000 | tf_op jit(solution)/shard_map/moves/pallas_call | solution.py:214
  163.0 11.8 %first_product.4 = (f32[1,4,128,1536]{3,2,1,0:T(8,128)}, s32[8]{0:T(128)}) custom-call(s32[8]{0:T(128)} %get-tuple-element.62.flags, bf16[384,3072]{1,0:T(8,128)(2,1)} %get-tuple-element.52.refs_0_, bf16[384,3072]{1,0:T(8,128)(2,1)} %collective-permute-done.6.refs_4_.refs_1_, bf16[384,3072]{1,0:T(8,128)(2,1)} %collective-permute-done.5.refs_3_.refs_2_, ...), custom_call_target="tpu_custom_call" | custom-call | flops 1000 | bytes 1000 | tf_op jit(solution)/shard_map/first_product/pallas_call | solution.py:373
  174.8 3.8 %moves.17 = (bf16[4,128,1536]{2,1,0:T(8,128)(2,1)}, s32[8]{0:T(128)}) custom-call(s32[8]{0:T(128)} %get-tuple-element.65.flags, bf16[4,128,1536]{2,1,0:T(8,128)(2,1)} %get-tuple-element.63.refs_5_.refs_0_.refs_6_.refs_12_.refs_17_, bf16[8,128,1536]{2,1,0:T(8,128)(2,1)} %collective-permute-done.2.refs_1_.refs_8_.refs_15_), custom_call_target="tpu_custom_call" | custom-call | flops 1000 | bytes 1000 | tf_op jit(solution)/shard_map/moves/pallas_call | solution.py:214
  178.7 4.2 %collective-permute-done.12.refs_0_.refs_5_.refs_13_ = bf16[4,128,1536]{2,1,0:T(8,128)(2,1)} collective-permute-done((bf16[4,128,1536]{2,1,0:T(8,128)(2,1)}, bf16[4,128,1536]{2,1,0:T(8,128)(2,1)}, u32[]{:S(2)}, u32[]{:S(2)}) %collective-permute-start.12) | collective-permute-done | bytes 1572896 | tf_op jit(solution)/shard_map/ppermute | solution.py:89
  182.9 3.8 %moves.18 = (bf16[4,128,1536]{2,1,0:T(8,128)(2,1)}, bf16[4,128,1536]{2,1,0:T(8,128)(2,1)}, s32[8]{0:T(128)}) custom-call(s32[8]{0:T(128)} %get-tuple-element.66.flags, bf16[4,128,1536]{2,1,0:T(8,128)(2,1)} %collective-permute-done.12.refs_0_.refs_5_.refs_13_, bf16[4,128,1536]{2,1,0:T(8,128)(2,1)} %collective-permute-done.13.refs_1_, ...), custom_call_target="tpu_custom_call", output_to_operand_aliasing={{1}: (4, {})} | custom-call | flops 1000 | bytes 1000 | tf_op jit(solution)/shard_map/moves/pallas_call | solution.py:214
  187.2 11.8 %first_product.5 = (f32[1,4,128,1536]{3,2,1,0:T(8,128)}, s32[8]{0:T(128)}) custom-call(s32[8]{0:T(128)} %get-tuple-element.68.flags, bf16[384,3072]{1,0:T(8,128)(2,1)} %get-tuple-element.52.refs_0_, bf16[384,3072]{1,0:T(8,128)(2,1)} %collective-permute-done.6.refs_4_.refs_1_, bf16[384,3072]{1,0:T(8,128)(2,1)} %collective-permute-done.5.refs_3_.refs_2_, ...), custom_call_target="tpu_custom_call" | custom-call | flops 1000 | bytes 1000 | tf_op jit(solution)/shard_map/first_product/pallas_call | solution.py:373
  200.5 3.3 %moves.19 = (bf16[384,768]{1,0:T(8,128)(2,1)}, bf16[384,768]{1,0:T(8,128)(2,1)}, s32[8]{0:T(128)}) custom-call(s32[8]{0:T(128)} %get-tuple-element.69.flags, bf16[384,2304]{1,0:T(8,128)(2,1)} %collective-permute-done.15.refs_0_.refs_3_.refs_7_, bf16[384,2304]{1,0:T(8,128)(2,1)} %collective-permute-done.16.refs_1_.refs_4_.refs_6_), custom_call_target="tpu_custom_call" | custom-call | flops 1000 | bytes 1000 | tf_op jit(solution)/shard_map/moves/pallas_call | solution.py:214
  206.8 16.8 %stored_products.1 = (f32[4,4,128,128]{3,2,1,0:T(8,128)}, s32[8]{0:T(128)}) custom-call(s32[8]{0:T(128)} %get-tuple-element.72.flags, bf16[384,3072]{1,0:T(8,128)(2,1)} %get-tuple-element.52.refs_0_, bf16[384,3072]{1,0:T(8,128)(2,1)} %collective-permute-done.6.refs_4_.refs_1_, bf16[384,3072]{1,0:T(8,128)(2,1)} %collective-permute-done.5.refs_3_.refs_2_, ...), custom_call_target="tpu_custom_call" | custom-call | flops 1000 | bytes 1000 | tf_op jit(solution)/shard_map/stored_products/pallas_call | solution.py:483
  223.6 33.7 %both_products.1 = (f32[4,2,64,128]{3,2,1,0:T(8,128)}, f32[4,2,64,128]{3,2,1,0:T(8,128)}) custom-call(s32[8]{0:T(128)} %get-tuple-element.78.flags, bf16[384,3072]{1,0:T(8,128)(2,1)} %get-tuple-element.61.refs_0_, bf16[384,3072]{1,0:T(8,128)(2,1)} %collective-permute-done.11.refs_4_.refs_1_, bf16[384,3072]{1,0:T(8,128)(2,1)} %collective-permute-done.10.refs_3_.refs_2_, ...), custom_call_target="tpu_custom_call" | custom-call | flops 1000 | bytes 1000 | tf_op jit(solution)/shard_map/both_products/pallas_call | solution.py:615
  257.4 1.7 collective-permute-done.21
  260.2 3.8 %collective-permute-start.22 = (f32[2,2,64,128]{3,2,1,0:T(8,128)S(1)}, f32[2,2,64,128]{3,2,1,0:T(8,128)S(1)}, u32[]{:S(2)}, u32[]{:S(2)}) collective-permute-start(f32[2,2,64,128]{3,2,1,0:T(8,128)S(1)} %get-tuple-element.94), channel_id=1, source_target_pairs={{0,8},{1,9},{2,10},{3,11},{4,12},{5,13},{6,14},{7,15},{8,16},{9,17... | collective-permute-start | bytes 393224 | tf_op jit(solution)/shard_map/ppermute | solution.py:89
  264.0 2.7 collective-permute-start.24
  268.0 5.3 %collective-permute-done.23 = f32[2,2,64,128]{3,2,1,0:T(8,128)S(1)} collective-permute-done((f32[2,2,64,128]{3,2,1,0:T(8,128)S(1)}, f32[2,2,64,128]{3,2,1,0:T(8,128)S(1)}, u32[]{:S(2)}, u32[]{:S(2)}) %collective-permute-start.23) | collective-permute-done | bytes 131104 | tf_op jit(solution)/shard_map/ppermute | solution.py:89
  (55 shorter events, 23.8 us)
Async XLA Ops:
  4.6 17.2 %collective-permute-start = (bf16[384,3072]{1,0:T(8,128)(2,1)}, bf16[384,3072]{1,0:T(8,128)(2,1)}, u32[]{:S(2)}, u32[]{:S(2)}) collective-permute-start(bf16[384,3072]{1,0:T(8,128)(2,1)} %get-tuple-element.46), channel_id=1, source_target_pairs={{1,8},{3,10},{5,12},{7,14},{8,1},{10,3},{12,5},{14,7},{17,24},{19,... | collective-permute-start | bytes 7077896 | tf_op jit(solution)/shard_map/ppermute | solution.py:89
  12.5 9.3 %collective-permute-start.1 = (bf16[4,128,1536]{2,1,0:T(8,128)(2,1)}, bf16[4,128,1536]{2,1,0:T(8,128)(2,1)}, u32[]{:S(2)}, u32[]{:S(2)}) collective-permute-start(bf16[4,128,1536]{2,1,0:T(8,128)(2,1)} %get-tuple-element.47.refs_0_.refs_5_.refs_9_.refs_10_.refs_18_), channel_id=1, source_target_pairs={{0,1},{1,0},{2,3},{3,2},{4,5},{5,4},{6,7},{7,6},{8,9},{9,8},{10,11... | collective-permute-start | bytes 4718600 | tf_op jit(solution)/shard_map/ppermute | solution.py:89
  18.1 65.2 %collective-permute-start.2 = (bf16[8,128,1536]{2,1,0:T(8,128)(2,1)}, bf16[8,128,1536]{2,1,0:T(8,128)(2,1)}, u32[]{:S(2)}, u32[]{:S(2)}) collective-permute-start(bf16[8,128,1536]{2,1,0:T(8,128)(2,1)} %bitcast.27), channel_id=1, source_target_pairs={{8,16},{9,17},{10,18},{11,19},{12,20},{13,21},{14,22},{15,23},{16,... | collective-permute-start | bytes 9437192 | tf_op jit(solution)/shard_map/ppermute | solution.py:89
  25.7 72.4 %collective-permute-start.5 = (bf16[384,3072]{1,0:T(8,128)(2,1)}, bf16[384,3072]{1,0:T(8,128)(2,1)}, u32[]{:S(2)}, u32[]{:S(2)}) collective-permute-start(bf16[384,3072]{1,0:T(8,128)(2,1)} %get-tuple-element.52.refs_0_), channel_id=1, source_target_pairs={{0,4},{1,5},{2,6},{3,7},{4,0},{5,1},{6,2},{7,3},{8,12},{9,13},{10,... | collective-permute-start | bytes 7077896 | tf_op jit(solution)/shard_map/ppermute | solution.py:89
  27.3 70.8 %collective-permute-start.6 = (bf16[384,3072]{1,0:T(8,128)(2,1)}, bf16[384,3072]{1,0:T(8,128)(2,1)}, u32[]{:S(2)}, u32[]{:S(2)}) collective-permute-start(bf16[384,3072]{1,0:T(8,128)(2,1)} %get-tuple-element.52.refs_0_), channel_id=1, source_target_pairs={{0,2},{1,3},{2,0},{3,1},{4,6},{5,7},{6,4},{7,5},{8,10},{9,11},{10,... | collective-permute-start | bytes 7077896 | tf_op jit(solution)/shard_map/ppermute | solution.py:89
  28.7 54.5 %collective-permute-start.3 = (bf16[4,128,1536]{2,1,0:T(8,128)(2,1)}, bf16[4,128,1536]{2,1,0:T(8,128)(2,1)}, u32[]{:S(2)}, u32[]{:S(2)}) collective-permute-start(bf16[4,128,1536]{2,1,0:T(8,128)(2,1)} %get-tuple-element.44.refs_4_.refs_7_.refs_14_), channel_id=1, source_target_pairs={{0,8},{1,9},{2,10},{3,11},{4,12},{5,13},{6,14},{7,15},{8,0},{9,1},... | collective-permute-start | bytes 4718600 | tf_op jit(solution)/shard_map/ppermute | solution.py:89
  48.1 49.9 %collective-permute-start.4 = (bf16[384,1536]{1,0:T(8,128)(2,1)}, bf16[384,1536]{1,0:T(8,128)(2,1)}, u32[]{:S(2)}, u32[]{:S(2)}) collective-permute-start(bf16[384,1536]{1,0:T(8,128)(2,1)} %get-tuple-element.51), channel_id=1, source_target_pairs={{1,8},{3,10},{5,12},{7,14},{8,1},{10,3},{12,5},{14,7},{17,24},{19,... | collective-permute-start | bytes 3538952 | tf_op jit(solution)/shard_map/ppermute | solution.py:89
  87.6 43.7 %collective-permute-start.8 = (bf16[4,128,1536]{2,1,0:T(8,128)(2,1)}, bf16[4,128,1536]{2,1,0:T(8,128)(2,1)}, u32[]{:S(2)}, u32[]{:S(2)}) collective-permute-start(bf16[4,128,1536]{2,1,0:T(8,128)(2,1)} %get-tuple-element.57), channel_id=1, source_target_pairs={{0,8},{1,9},{2,10},{3,11},{4,12},{5,13},{6,14},{7,15},{8,0},{9,1},... | collective-permute-start | bytes 4718600 | tf_op jit(solution)/shard_map/ppermute | solution.py:89
  96.1 35.2 %collective-permute-start.9 = (bf16[4,128,1536]{2,1,0:T(8,128)(2,1)}, bf16[4,128,1536]{2,1,0:T(8,128)(2,1)}, u32[]{:S(2)}, u32[]{:S(2)}) collective-permute-start(bf16[4,128,1536]{2,1,0:T(8,128)(2,1)} %get-tuple-element.58), channel_id=1, source_target_pairs={{8,16},{9,17},{10,18},{11,19},{12,20},{13,21},{14,22},{15,23},{16,... | collective-permute-start | bytes 4718600 | tf_op jit(solution)/shard_map/ppermute | solution.py:89
  102.6 52.9 %collective-permute-start.10 = (bf16[384,3072]{1,0:T(8,128)(2,1)}, bf16[384,3072]{1,0:T(8,128)(2,1)}, u32[]{:S(2)}, u32[]{:S(2)}) collective-permute-start(bf16[384,3072]{1,0:T(8,128)(2,1)} %get-tuple-element.60), channel_id=1, source_target_pairs={{0,4},{1,5},{2,6},{3,7},{4,0},{5,1},{6,2},{7,3},{8,12},{9,13},{10,... | collective-permute-start | bytes 7077896 | tf_op jit(solution)/shard_map/ppermute | solution.py:89
  104.1 52.6 %collective-permute-start.11 = (bf16[384,3072]{1,0:T(8,128)(2,1)}, bf16[384,3072]{1,0:T(8,128)(2,1)}, u32[]{:S(2)}, u32[]{:S(2)}) collective-permute-start(bf16[384,3072]{1,0:T(8,128)(2,1)} %get-tuple-element.61.refs_0_), channel_id=1, source_target_pairs={{0,2},{1,3},{2,0},{3,1},{4,6},{5,7},{6,4},{7,5},{8,10},{9,11},{10,... | collective-permute-start | bytes 7077896 | tf_op jit(solution)/shard_map/ppermute | solution.py:89
  105.6 25.7 %collective-permute-start.7 = (bf16[384,1536]{1,0:T(8,128)(2,1)}, bf16[384,1536]{1,0:T(8,128)(2,1)}, u32[]{:S(2)}, u32[]{:S(2)}) collective-permute-start(bf16[384,1536]{1,0:T(8,128)(2,1)} %get-tuple-element.56), channel_id=1, source_target_pairs={{1,8},{3,10},{5,12},{7,14},{8,1},{10,3},{12,5},{14,7},{17,24},{19,... | collective-permute-start | bytes 3538952 | tf_op jit(solution)/shard_map/ppermute | solution.py:89
  131.3 47.4 %collective-permute-start.14 = (bf16[4,128,1536]{2,1,0:T(8,128)(2,1)}, bf16[4,128,1536]{2,1,0:T(8,128)(2,1)}, u32[]{:S(2)}, u32[]{:S(2)}) collective-permute-start(bf16[4,128,1536]{2,1,0:T(8,128)(2,1)} %collective-permute-done.3.refs_2_.refs_6_.refs_11_.refs_20_), channel_id=1, source_target_pairs={{0,1},{1,0},{2,3},{3,2},{4,5},{5,4},{6,7},{7,6},{8,9},{9,8},{10,11... | collective-permute-start | bytes 4718600 | tf_op jit(solution)/shard_map/ppermute | solution.py:89
  132.5 50.3 %collective-permute-start.12 = (bf16[4,128,1536]{2,1,0:T(8,128)(2,1)}, bf16[4,128,1536]{2,1,0:T(8,128)(2,1)}, u32[]{:S(2)}, u32[]{:S(2)}) collective-permute-start(bf16[4,128,1536]{2,1,0:T(8,128)(2,1)} %get-tuple-element.64.refs_6_.refs_16_), channel_id=1, source_target_pairs={{8,0},{9,1},{10,2},{11,3},{12,4},{13,5},{14,6},{15,7},{16,24},{17,... | collective-permute-start | bytes 4718600 | tf_op jit(solution)/shard_map/ppermute | solution.py:89
  133.8 49.0 %collective-permute-start.13 = (bf16[4,128,1536]{2,1,0:T(8,128)(2,1)}, bf16[4,128,1536]{2,1,0:T(8,128)(2,1)}, u32[]{:S(2)}, u32[]{:S(2)}) collective-permute-start(bf16[4,128,1536]{2,1,0:T(8,128)(2,1)} %get-tuple-element.63.refs_5_.refs_0_.refs_6_.refs_12_.refs_17_), channel_id=1, source_target_pairs={{8,16},{9,17},{10,18},{11,19},{12,20},{13,21},{14,22},{15,23},{16,... | collective-permute-start | bytes 4718600 | tf_op jit(solution)/shard_map/ppermute | solution.py:89
  160.9 39.2 %collective-permute-start.15 = (bf16[384,2304]{1,0:T(8,128)(2,1)}, bf16[384,2304]{1,0:T(8,128)(2,1)}, u32[]{:S(2)}, u32[]{:S(2)}) collective-permute-start(bf16[384,2304]{1,0:T(8,128)(2,1)} %get-tuple-element.70), channel_id=1, source_target_pairs={{0,4},{1,5},{2,6},{3,7},{4,0},{5,1},{6,2},{7,3},{8,12},{9,13},{10,... | collective-permute-start | bytes 5308424 | tf_op jit(solution)/shard_map/ppermute | solution.py:89
  161.5 39.0 %collective-permute-start.16 = (bf16[384,2304]{1,0:T(8,128)(2,1)}, bf16[384,2304]{1,0:T(8,128)(2,1)}, u32[]{:S(2)}, u32[]{:S(2)}) collective-permute-start(bf16[384,2304]{1,0:T(8,128)(2,1)} %get-tuple-element.71.refs_5_), channel_id=1, source_target_pairs={{0,2},{1,3},{2,0},{3,1},{4,6},{5,7},{6,4},{7,5},{8,10},{9,11},{10,... | collective-permute-start | bytes 5308424 | tf_op jit(solution)/shard_map/ppermute | solution.py:89
  186.6 20.2 %collective-permute-start.17 = (bf16[4,128,1536]{2,1,0:T(8,128)(2,1)}, bf16[4,128,1536]{2,1,0:T(8,128)(2,1)}, u32[]{:S(2)}, u32[]{:S(2)}) collective-permute-start(bf16[4,128,1536]{2,1,0:T(8,128)(2,1)} %get-tuple-element.73.refs_13_.refs_22_), channel_id=1, source_target_pairs={{0,1},{1,0},{2,3},{3,2},{4,5},{5,4},{6,7},{7,6},{8,9},{9,8},{10,11... | collective-permute-start | bytes 4718600 | tf_op jit(solution)/shard_map/ppermute | solution.py:89
  186.9 20.0 %collective-permute-start.18 = (bf16[4,128,1536]{2,1,0:T(8,128)(2,1)}, bf16[4,128,1536]{2,1,0:T(8,128)(2,1)}, u32[]{:S(2)}, u32[]{:S(2)}) collective-permute-start(bf16[4,128,1536]{2,1,0:T(8,128)(2,1)} %get-tuple-element.74.refs_15_.refs_24_), channel_id=1, source_target_pairs={{0,1},{1,0},{2,3},{3,2},{4,5},{5,4},{6,7},{7,6},{8,9},{9,8},{10,11... | collective-permute-start | bytes 4718600 | tf_op jit(solution)/shard_map/ppermute | solution.py:89
  203.8 19.8 %collective-permute-start.19 = (bf16[384,768]{1,0:T(8,128)(2,1)}, bf16[384,768]{1,0:T(8,128)(2,1)}, u32[]{:S(2)}, u32[]{:S(2)}) collective-permute-start(bf16[384,768]{1,0:T(8,128)(2,1)} %get-tuple-element.79), channel_id=1, source_target_pairs={{0,4},{1,5},{2,6},{3,7},{4,0},{5,1},{6,2},{7,3},{8,12},{9,13},{10,... | collective-permute-start | bytes 1769480 | tf_op jit(solution)/shard_map/ppermute | solution.py:89
  205.3 18.3 %collective-permute-start.20 = (bf16[384,768]{1,0:T(8,128)(2,1)}, bf16[384,768]{1,0:T(8,128)(2,1)}, u32[]{:S(2)}, u32[]{:S(2)}) collective-permute-start(bf16[384,768]{1,0:T(8,128)(2,1)} %get-tuple-element.80), channel_id=1, source_target_pairs={{0,2},{1,3},{2,0},{3,1},{4,6},{5,7},{6,4},{7,5},{8,10},{9,11},{10,... | collective-permute-start | bytes 1769480 | tf_op jit(solution)/shard_map/ppermute | solution.py:89
  257.3 1.8 collective-permute-start.21
  259.1 15.6 %copy-start = (s32[64]{0:T(128)S(1)}, s32[64]{0:T(128)}, u32[]{:S(2)}) copy-start(s32[64]{0:T(128)} %param.7) | copy-start | bytes 772
  260.2 7.8 %collective-permute-start.22 = (f32[2,2,64,128]{3,2,1,0:T(8,128)S(1)}, f32[2,2,64,128]{3,2,1,0:T(8,128)S(1)}, u32[]{:S(2)}, u32[]{:S(2)}) collective-permute-start(f32[2,2,64,128]{3,2,1,0:T(8,128)S(1)} %get-tuple-element.94), channel_id=1, source_target_pairs={{0,8},{1,9},{2,10},{3,11},{4,12},{5,13},{6,14},{7,15},{8,16},{9,17... | collective-permute-start | bytes 393224 | tf_op jit(solution)/shard_map/ppermute | solution.py:89
  264.0 9.3 %collective-permute-start.23 = (f32[2,2,64,128]{3,2,1,0:T(8,128)S(1)}, f32[2,2,64,128]{3,2,1,0:T(8,128)S(1)}, u32[]{:S(2)}, u32[]{:S(2)}) collective-permute-start(f32[2,2,64,128]{3,2,1,0:T(8,128)S(1)} %get-tuple-element.95), channel_id=1, source_target_pairs={{0,16},{1,17},{2,18},{3,19},{4,20},{5,21},{6,22},{7,23},{8,24},{9,... | collective-permute-start | bytes 393224 | tf_op jit(solution)/shard_map/ppermute | solution.py:89
  264.0 9.3 %collective-permute-start.24 = (f32[2,2,64,128]{3,2,1,0:T(8,128)S(1)}, f32[2,2,64,128]{3,2,1,0:T(8,128)S(1)}, u32[]{:S(2)}, u32[]{:S(2)}) collective-permute-start(f32[2,2,64,128]{3,2,1,0:T(8,128)S(1)} %get-tuple-element.96), channel_id=1, source_target_pairs={{0,24},{1,25},{2,26},{3,27},{4,28},{5,29},{6,30},{7,31},{8,0},{9,1... | collective-permute-start | bytes 393224 | tf_op jit(solution)/shard_map/ppermute | solution.py:89
  273.3 1.4 collective-permute-start.25
